TPU v7x, 32 devices: a whole 2x2x4 slice. The times are simulated.
32 devices in a mesh: gx: 4 (over x, core), gy: 4 (over z), gz: 2 (over y).
Axes of the slice: x: 2, y: 2, z: 4, core: 2. Of those that a mesh axis runs over, the one named last changes fastest.
Arguments:
- fine_blocks: float32 [8, 8, 8, 7, 4096], P('gx', 'gy', 'gz'), may hold values from -0.75 to 0.75
- prolong: float32 [8, 8, 8, 1024], P('gx', 'gy', 'gz'), may hold values from -1.5 to 1.5
- agg_map: int32 [8, 8, 8], replicated, may hold values from 0 to 7, as said below
- owner_map: int32 [4, 4, 16], P('gx', 'gy', 'gz'), may hold values from 0 to 1, as said below
Outputs:
- coarse_rows: float32 [4, 4, 16, 14336], P('gx', 'gy', 'gz')
Inputs may be any that keep to these rules, and one draw needn't show every extreme that they name: `agg_map`: every one of the 8 slots of each brick names at least one element of that brick. `owner_map`: owners are devices with the same gx and gy indices as the brick. Each brick gives exactly 4 of its slots to each owner. The elements of one brick whose rows go to one owner number at most 12, and exactly 12 for one owner of every brick.
All inputs are finite; a program needn't handle non-finite values.
Results may differ from a plain program's by a relative error of at most 0.0001.
Values sent between devices are 32-bit elements; how exact they have to be, the bound alone decides.
No kernel may reach another device: no remote copies, remote signals or barrier semaphores. Data moves between devices by JAX's collectives and lax.ppermute only.
A program may use at most 64 MiB of HBM per device.

v0:
```python
import jax
import jax.numpy as jnp
from jax import lax
from jax.sharding import PartitionSpec as P

DOF = 64
CDOF = 16
AGGS = 8


face_steps = ((0, 0, 0), (-1, 0, 0), (1, 0, 0), (0, -1, 0), (0, 1, 0), (0, 0, -1), (0, 0, 1))


def extended(block, sides, width):
    for axis, dim in sides:
        count = lax.axis_size(axis)
        forward = [(i, i + 1) for i in range(count - 1)]
        backward = [(target, source) for source, target in forward]
        low = lax.ppermute(
            lax.slice_in_dim(block, block.shape[dim] - width, None, axis=dim), axis, forward
        )
        high = lax.ppermute(lax.slice_in_dim(block, 0, width, axis=dim), axis, backward)
        block = jnp.concatenate([low, block, high], axis=dim)
    return block


def shards(fine_blocks, prolong, agg_map, owner_map):
    size_x = fine_blocks.shape[0]
    size_y = fine_blocks.shape[1]
    size_z = fine_blocks.shape[2]
    elements = size_x * size_y * size_z
    group_size = lax.axis_size("gz")
    rows_each = AGGS // group_size
    capacity = min(2 * elements // group_size, elements - (group_size - 1) * rows_each)
    padded = extended(prolong, (("gx", 0), ("gy", 1), ("gz", 2)), 1)
    window = padded.reshape(size_x + 2, size_y + 2, size_z + 2, DOF, CDOF)
    beside = jnp.stack(
        [
            window[1 + sx : 1 + sx + size_x, 1 + sy : 1 + sy + size_y, 1 + sz : 1 + sz + size_z]
            for sx, sy, sz in face_steps
        ],
        axis=3,
    )
    blocks = fine_blocks.reshape(size_x, size_y, size_z, 7, DOF, DOF)
    products = jnp.einsum("xyzkij,xyzkjc->xyzkic", blocks, beside, precision=lax.Precision.HIGHEST)
    own_base = window[1:-1, 1:-1, 1:-1]
    anchor_x = lax.axis_index("gx") * size_x
    anchor_y = lax.axis_index("gy") * size_y
    anchor_z = lax.axis_index("gz") * size_z
    padded_agg = jnp.pad(agg_map, 1)
    agg_window = lax.dynamic_slice(
        padded_agg, (anchor_x, anchor_y, anchor_z), (size_x + 2, size_y + 2, size_z + 2)
    )
    local_x = jnp.arange(size_x, dtype=jnp.int32)[:, None, None]
    local_y = jnp.arange(size_y, dtype=jnp.int32)[None, :, None]
    local_z = jnp.arange(size_z, dtype=jnp.int32)[None, None, :]
    columns = []
    for face, (sx, sy, sz) in enumerate(face_steps):
        neighbour = agg_window[
            1 + sx : 1 + sx + size_x, 1 + sy : 1 + sy + size_y, 1 + sz : 1 + sz + size_z
        ]
        inside = (
            (local_x + sx >= 0)
            & (local_x + sx < size_x)
            & (local_y + sy >= 0)
            & (local_y + sy < size_y)
            & (local_z + sz >= 0)
            & (local_z + sz < size_z)
        )
        relation = jnp.where(inside, 0, face).astype(jnp.int32)
        columns.append(relation * AGGS + neighbour)
    column_slot = jnp.stack(columns, axis=3).reshape(elements, 7)
    own_agg = agg_window[1:-1, 1:-1, 1:-1].reshape(elements)
    owners = owner_map.reshape(AGGS)
    slot_ids = jnp.arange(AGGS, dtype=jnp.int32)
    earlier = (owners[None, :] == owners[:, None]) & (slot_ids[None, :] < slot_ids[:, None])
    rank_in_owner = jnp.sum(earlier.astype(jnp.int32), axis=1)
    member = (own_agg[:, None] == slot_ids[None, :]).astype(jnp.int32)
    element_owner = jnp.sum(member * owners[None, :], axis=1)
    element_rank = jnp.sum(member * rank_in_owner[None, :], axis=1)
    element_ids = jnp.arange(elements, dtype=jnp.int32)
    before = (element_owner[None, :] == element_owner[:, None]) & (
        element_ids[None, :] < element_ids[:, None]
    )
    position = jnp.sum(before.astype(jnp.int32), axis=1)
    owner_ids = jnp.arange(group_size, dtype=jnp.int32)
    place_ids = jnp.arange(capacity, dtype=jnp.int32)
    select = (
        (element_owner[None, None, :] == owner_ids[:, None, None])
        & (position[None, None, :] == place_ids[None, :, None])
    ).astype(jnp.float32)
    labels = jnp.concatenate([element_rank[:, None], column_slot], axis=1).astype(jnp.float32)

    def bucket(values):
        return jnp.einsum("oce,ef->ocf", select, values, precision=lax.Precision.HIGHEST)

    coarse = jnp.einsum("xyzic,xyzkid->xyzkcd", own_base, products, precision=lax.Precision.HIGHEST)
    received, received_labels = (
        lax.all_to_all(
            bucket(coarse.reshape(elements, 7 * CDOF * CDOF)),
            "gz",
            split_axis=0,
            concat_axis=0,
            tiled=True,
        ),
        lax.all_to_all(bucket(labels), "gz", split_axis=0, concat_axis=0, tiled=True),
    )
    sender_ids = jnp.arange(group_size, dtype=jnp.float32)[:, None]
    row_target = sender_ids * rows_each + received_labels[:, :, 0]
    target = row_target[:, :, None] * (7 * AGGS) + received_labels[:, :, 1:]
    target_ids = jnp.arange(AGGS * 7 * AGGS, dtype=jnp.float32)
    spread = (target.reshape(group_size * capacity * 7)[:, None] == target_ids[None, :]).astype(
        jnp.float32
    )
    flat_terms = received.reshape(group_size * capacity * 7, CDOF * CDOF)
    summed = jnp.einsum("rm,rf->mf", spread, flat_terms, precision=lax.Precision.HIGHEST)
    return summed.reshape(1, 1, AGGS, 7 * AGGS * CDOF * CDOF)


def solution(mesh):
    placed = (P("gx", "gy", "gz", None, None), P("gx", "gy", "gz", None), P(), P("gx", "gy", "gz"))
    return jax.shard_map(
        shards, mesh=mesh, in_specs=placed, out_specs=P("gx", "gy", "gz", None), check_vma=False
    )
```

profile of v0, /device:TPU:10, one launch (start us, length us, event | category | flops | bytes accessed | tf_op | source)
XLA Modules:
  0.0 84.5 jit_solution(9501813821584143161)
XLA Ops:
  0.0 0.8 fusion.46
  0.8 1.9 %collective-permute-start = (f32[1,2,4,1024]{3,2,1,0:T(4,128)S(1)}, f32[1,2,4,1024]{3,2,1,0:T(4,128)S(1)}, u32[]{:S(2)}, u32[]{:S(2)}) collective-permute-start(f32[1,2,4,1024]{3,2,1,0:T(4,128)S(1)} %get-tuple-element.19), channel_id=1, source_target_pairs={{0,8},{8,16},{16,24},{1,9},{9,17},{17,25},{2,10},{10,18},{18,26},{... | collective-permute-start | bytes 98312 | tf_op jit(solution)/shard_map/ppermute | solution.py:19
  2.8 3.6 %collective-permute-start.1 = (f32[1,2,4,1024]{3,2,1,0:T(4,128)S(1)}, f32[1,2,4,1024]{3,2,1,0:T(4,128)S(1)}, u32[]{:S(2)}, u32[]{:S(2)}) collective-permute-start(f32[1,2,4,1024]{3,2,1,0:T(4,128)S(1)} %get-tuple-element.18), channel_id=1, source_target_pairs={{8,0},{16,8},{24,16},{9,1},{17,9},{25,17},{10,2},{18,10},{26,18},{... | collective-permute-start | bytes 98312 | tf_op jit(solution)/shard_map/ppermute | solution.py:22
  6.5 0.1 broadcast_and_fusion
  6.6 0.9 %fusion.23 = (s32[2,2,4]{2,1,0:T(2,128)S(1)}, s32[2,2,4]{2,1,0:T(2,128)S(1)}, s32[2,2,4]{2,1,0:T(2,128)S(1)}) fusion(s32[]{:T(128)S(6)} %add.133, s32[]{:T(128)S(6)} %add.134, s32[]{:T(128)S(6)} %add.150, s32[8,8,8]{2,1,0:T(8,128)} %param.6, pred[4]{0:T(512)(128)(4,1)S(1)} %get-tuple-element.38, pred[4]{0:T(512)(128)(4,1)S(1)} %get-tuple-element.39, ...), kind=kLoop, calls=%fused_computation.59 | loop fusion | flops 160 | bytes 2280 | tf_op jit(solution)/shard_map/add | solution.py:71
  7.5 0.1 eq.92
  7.6 0.9 %convert_reduce_fusion.1 = s32[8]{0:T(128)S(1)} fusion(s32[8]{0:T(128)} %bitcast.40), kind=kLoop, calls=%fused_computation.45 | loop fusion | flops 312 | bytes 64 | tf_op jit(solution)/shard_map/reduce_sum | solution.py:77
  8.5 0.7 select_reduce_fusion
  9.2 0.2 convert_reduce_fusion
  9.4 0.1 stack.46
  9.5 1.0 %fusion.27 = (s32[2,2,4]{2,1,0:T(2,128)S(1)}, s32[2,2,4]{2,1,0:T(2,128)S(1)}, s32[2,2,4]{2,1,0:T(2,128)S(1)}, s32[2,2,4]{2,1,0:T(2,128)S(1)}) fusion(s32[]{:T(128)S(6)} %add.133, s32[]{:T(128)S(6)} %add.144, s32[]{:T(128)S(6)} %add.135, s32[8,8,8]{2,1,0:T(8,128)} %param.6, pred[2,2]{1,0:T(4,128)(4,1)S(1)} %get-tuple-element.28, ...), kind=kLoop, calls=%fused_computation.63 | loop fusion | flops 256 | bytes 2352 | tf_op jit(solution)/shard_map/add | solution.py:71
  10.5 0.1 stack.47
  10.6 0.1 stack.48
  10.6 0.1 stack.49
  10.7 0.1 stack.50
  10.8 0.1 stack.51
  10.9 0.1 stack.52
  11.0 0.8 fusion.10
  11.8 3.2 %all-to-all-start = ((f32[2,12,8]{1,2,0:T(8,128)}), f32[2,12,8]{1,2,0:T(8,128)S(1)}, u32[]{:S(2)}, u32[]{:S(2)}) async-start(f32[2,12,8]{1,2,0:T(8,128)} %fusion.10), calls=%async_computation | async-start | bytes 16384 | tf_op jit(solution)/shard_map/all_to_all | solution.py:106
  15.0 4.4 %reshape.371 = f32[2,2,4,7,64,64]{5,4,2,3,1,0:T(8,128)} reshape(f32[2,2,4,7,4096]{4,2,3,1,0:T(4,128)} %param.4) | data formatting | bytes 3670016 | tf_op jit(solution)/shard_map/reshape | solution.py:44
  19.4 0.0 copy-done.1
  19.4 0.0 collective-permute-done
  19.4 0.0 copy-done
  19.4 0.0 collective-permute-done.1
  19.5 3.5 %collective-permute-start.2 = (f32[4,1,4,1024]{3,2,1,0:T(4,128)S(1)}, f32[4,1,4,1024]{3,2,1,0:T(4,128)S(1)}, u32[]{:S(2)}, u32[]{:S(2)}) collective-permute-start(f32[4,1,4,1024]{3,2,1,0:T(4,128)S(1)} %get-tuple-element.16), channel_id=1, source_target_pairs={{0,2},{2,4},{4,6},{1,3},{3,5},{5,7},{8,10},{10,12},{12,14},{9,11},... | collective-permute-start | bytes 196616 | tf_op jit(solution)/shard_map/ppermute | solution.py:19
  23.0 2.4 %collective-permute-start.3 = (f32[4,1,4,1024]{3,2,1,0:T(4,128)S(1)}, f32[4,1,4,1024]{3,2,1,0:T(4,128)S(1)}, u32[]{:S(2)}, u32[]{:S(2)}) collective-permute-start(f32[4,1,4,1024]{3,2,1,0:T(4,128)S(1)} %get-tuple-element.17), channel_id=1, source_target_pairs={{2,0},{4,2},{6,4},{3,1},{5,3},{7,5},{10,8},{12,10},{14,12},{11,9},... | collective-permute-start | bytes 196616 | tf_op jit(solution)/shard_map/ppermute | solution.py:22
  25.4 0.3 collective-permute-done.2
  25.6 3.5 %collective-permute-done.3 = f32[4,1,4,1024]{3,2,1,0:T(4,128)S(1)} collective-permute-done((f32[4,1,4,1024]{3,2,1,0:T(4,128)S(1)}, f32[4,1,4,1024]{3,2,1,0:T(4,128)S(1)}, u32[]{:S(2)}, u32[]{:S(2)}) %collective-permute-start.3) | collective-permute-done | bytes 65568 | tf_op jit(solution)/shard_map/ppermute | solution.py:22
  29.1 0.1 pad_maximum_fusion.3
  29.2 3.9 %collective-permute-start.4 = (f32[4,4,1,1024]{3,2,1,0:T(1,128)S(1)}, f32[4,4,1,1024]{3,2,1,0:T(1,128)S(1)}, u32[]{:S(2)}, u32[]{:S(2)}) collective-permute-start(f32[4,4,1,1024]{3,2,1,0:T(1,128)S(1)} %get-tuple-element.14), channel_id=1, source_target_pairs={{0,1},{2,3},{4,5},{6,7},{8,9},{10,11},{12,13},{14,15},{16,17},{18,... | collective-permute-start | bytes 196616 | tf_op jit(solution)/shard_map/ppermute | solution.py:19
  33.2 1.3 %collective-permute-start.5 = (f32[4,4,1,1024]{3,2,1,0:T(1,128)S(1)}, f32[4,4,1,1024]{3,2,1,0:T(1,128)S(1)}, u32[]{:S(2)}, u32[]{:S(2)}) collective-permute-start(f32[4,4,1,1024]{3,2,1,0:T(1,128)S(1)} %get-tuple-element.15), channel_id=1, source_target_pairs={{1,0},{3,2},{5,4},{7,6},{9,8},{11,10},{13,12},{15,14},{17,16},{19,... | collective-permute-start | bytes 196616 | tf_op jit(solution)/shard_map/ppermute | solution.py:22
  34.5 0.0 all-to-all-done
  34.5 0.1 fusion.32
  34.5 0.5 collective-permute-done.4
  35.0 4.3 %collective-permute-done.5 = f32[4,4,1,1024]{3,2,1,0:T(1,128)S(1)} collective-permute-done((f32[4,4,1,1024]{3,2,1,0:T(1,128)S(1)}, f32[4,4,1,1024]{3,2,1,0:T(1,128)S(1)}, u32[]{:S(2)}, u32[]{:S(2)}) %collective-permute-start.5) | collective-permute-done | bytes 65568 | tf_op jit(solution)/shard_map/ppermute | solution.py:22
  39.3 1.0 %pad_maximum_fusion = f32[4,4,6,1024]{3,2,1,0:T(8,128)} fusion(f32[4,4,1,1024]{3,2,1,0:T(1,128)S(1)} %collective-permute-done.5, f32[4,1,4,1024]{3,2,1,0:T(4,128)S(1)} %collective-permute-done.3, f32[4,2,4,1024]{3,2,1,0:T(4,128)S(1)} %constant_dynamic-update-slice_fusion, f32[4,1,4,1024]{3,2,1,0:T(4,128)S(1)} %collective-permute-done.2, ...), kind=kLoop, calls=%fused_computation.4 | loop fusion | flops 393216 | bytes 786432 | tf_op jit(solution)/shard_map/concatenate | solution.py:23
  40.3 2.1 %reshape.379 = f32[4,4,6,64,16]{4,3,2,1,0:T(8,128)S(1)} reshape(f32[4,4,6,1024]{3,2,1,0:T(8,128)} %pad_maximum_fusion) | data formatting | bytes 786432 | tf_op jit(solution)/shard_map/reshape | solution.py:36
  42.4 1.9 %fusion.44 = (f32[2,2,4,64,16]{4,3,2,1,0:T(8,128)}, f32[2,2,4,64,16]{4,3,2,1,0:T(8,128)}, f32[2,2,4,64,16]{4,3,2,1,0:T(8,128)}, f32[2,2,4,64,16]{4,3,2,1,0:T(8,1...) fusion(f32[4,4,6,64,16]{4,3,2,1,0:T(8,128)S(1)} %reshape.379), kind=kLoop, calls=%fused_computation.94 | loop fusion | bytes 917504 | tf_op jit(solution)/shard_map/slice | solution.py:39
  44.3 1.2 %copy.29 = f32[2,2,4,64,16]{3,4,2,1,0:T(8,128)S(1)} copy(f32[2,2,4,64,16]{4,3,2,1,0:T(8,128)} %get-tuple-element.13) | data formatting | bytes 131072
  45.5 0.7 bitcast_dynamic-update-slice_fusion.6
  46.2 1.9 %copy.30 = f32[2,2,4,64,16]{3,4,2,1,0:T(8,128)} copy(f32[2,2,4,64,16]{4,3,2,1,0:T(8,128)} %get-tuple-element.12) | data formatting | bytes 131072
  48.1 1.9 %copy.31 = f32[2,2,4,64,16]{3,4,2,1,0:T(8,128)} copy(f32[2,2,4,64,16]{4,3,2,1,0:T(8,128)} %get-tuple-element.11) | data formatting | bytes 131072
  49.9 1.9 %copy.32 = f32[2,2,4,64,16]{3,4,2,1,0:T(8,128)} copy(f32[2,2,4,64,16]{4,3,2,1,0:T(8,128)} %get-tuple-element.10) | data formatting | bytes 131072
  51.8 1.2 %copy.33 = f32[2,2,4,64,16]{3,4,2,1,0:T(8,128)S(1)} copy(f32[2,2,4,64,16]{4,3,2,1,0:T(8,128)} %get-tuple-element.9) | data formatting | bytes 131072
  53.0 1.2 %copy.34 = f32[2,2,4,64,16]{3,4,2,1,0:T(8,128)S(1)} copy(f32[2,2,4,64,16]{4,3,2,1,0:T(8,128)} %get-tuple-element.8) | data formatting | bytes 131072
  54.3 1.2 %copy.35 = f32[2,2,4,64,16]{3,4,2,1,0:T(8,128)S(1)} copy(f32[2,2,4,64,16]{4,3,2,1,0:T(8,128)} %get-tuple-element.7) | data formatting | bytes 131072
  55.5 1.6 %bitcast_dynamic-update-slice_fusion.5 = f32[2,2,4,7,64,16]{4,5,3,2,1,0:T(8,128)} fusion(f32[2,2,4,7,64,16]{4,5,3,2,1,0:T(8,128)} %bitcast_dynamic-update-slice_fusion.6, f32[2,2,4,64,16]{3,4,2,1,0:T(8,128)} %copy.30), kind=kLoop, calls=%fused_computation.21 | loop fusion | bytes 262144
  57.1 1.6 %bitcast_dynamic-update-slice_fusion.4 = f32[2,2,4,7,64,16]{4,5,3,2,1,0:T(8,128)} fusion(f32[2,2,4,7,64,16]{4,5,3,2,1,0:T(8,128)} %bitcast_dynamic-update-slice_fusion.5, f32[2,2,4,64,16]{3,4,2,1,0:T(8,128)} %copy.31), kind=kLoop, calls=%fused_computation.20 | loop fusion | bytes 262144
  58.6 1.6 %bitcast_dynamic-update-slice_fusion.3 = f32[2,2,4,7,64,16]{4,5,3,2,1,0:T(8,128)} fusion(f32[2,2,4,7,64,16]{4,5,3,2,1,0:T(8,128)} %bitcast_dynamic-update-slice_fusion.4, f32[2,2,4,64,16]{3,4,2,1,0:T(8,128)} %copy.32), kind=kLoop, calls=%fused_computation.19 | loop fusion | bytes 262144
  60.2 0.7 bitcast_dynamic-update-slice_fusion.2
  60.9 0.7 bitcast_dynamic-update-slice_fusion.1
  61.5 0.7 bitcast_dynamic-update-slice_fusion
  62.2 7.6 %fusion.2 = f32[2,2,4,7,64,16]{4,5,3,2,1,0:T(8,128)S(1)} fusion(f32[2,2,4,7,64,16]{4,5,3,2,1,0:T(8,128)} %bitcast_dynamic-update-slice_fusion, f32[2,2,4,7,64,64]{5,4,2,3,1,0:T(8,128)} %reshape.371), kind=kOutput, calls=%fused_computation.2 | convolution fusion | flops 88080384 | bytes 2752512 | tf_op jit(solution)/shard_map/xyzkij,xyzkjc->xyzkic/dot_general | solution.py:45
  69.8 0.0 copy-start.2
  69.8 1.9 %convolution_bitcast_fusion = f32[2,2,4,7,16,16]{4,5,3,2,1,0:T(8,128)} fusion(f32[2,2,4,7,64,16]{4,5,3,2,1,0:T(8,128)S(1)} %fusion.2, f32[4,4,6,64,16]{4,3,2,1,0:T(8,128)S(1)} %reshape.379), kind=kOutput, calls=%fused_computation.3 | convolution fusion | flops 22020096 | bytes 1556480 | tf_op jit(solution)/shard_map/xyzic,xyzkid->xyzkcd/dot_general | solution.py:97
  71.7 1.5 %copy.25 = f32[2,2,4,7,16,16]{5,4,3,2,1,0:T(8,128)S(1)} copy(f32[2,2,4,7,16,16]{4,5,3,2,1,0:T(8,128)} %convolution_bitcast_fusion) | data formatting | bytes 229376 | tf_op jit(solution)/shard_map/xyzic,xyzkid->xyzkcd/transpose | solution.py:97
  73.2 0.4 reshape.377
  73.6 0.9 %fusion.8 = f32[2,12,1792]{2,1,0:T(8,128)} fusion(f32[16,1792,1]{1,0,2:T(8,128)S(1)} %reshape.377, pred[12,16]{1,0:T(8,128)(4,1)S(1)} %iota_compare_fusion.2, pred[2,16]{1,0:T(4,128)(4,1)S(1)} %copy-done.2), kind=kOutput, calls=%fused_computation.29 | convolution fusion | flops 8257920 | bytes 286944 | tf_op jit(solution)/shard_map/oce,ef->ocf/dot_general | solution.py:95
  74.5 3.4 %all-to-all-start.1 = ((f32[2,12,1792]{2,1,0:T(8,128)}), f32[2,12,1792]{2,1,0:T(8,128)S(1)}, u32[]{:S(2)}, u32[]{:S(2)}) async-start(f32[2,12,1792]{2,1,0:T(8,128)} %fusion.8), calls=%async_computation.1 | async-start | bytes 458752 | tf_op jit(solution)/shard_map/all_to_all | solution.py:99
  77.9 0.1 copy.15
  78.0 0.1 eq.108
  78.1 4.8 %all-to-all-done.1 = f32[2,12,1792]{2,1,0:T(8,128)S(1)} async-done(((f32[2,12,1792]{2,1,0:T(8,128)}), f32[2,12,1792]{2,1,0:T(8,128)S(1)}, u32[]{:S(2)}, u32[]{:S(2)}) %all-to-all-start.1) | async-done | bytes 172064 | tf_op jit(solution)/shard_map/all_to_all | solution.py:99
  83.0 0.7 fusion.6
  83.6 0.8 reshape.374
  (20 shorter events, 0.2 us)
Async XLA Ops:
  0.0 19.4 %copy-start = (f32[2,2,4,1024]{3,2,1,0:T(4,128)S(1)}, f32[2,2,4,1024]{3,2,1,0:T(4,128)}, u32[]{:S(2)}) copy-start(f32[2,2,4,1024]{3,2,1,0:T(4,128)} %param.5) | copy-start | bytes 196612
  0.8 18.6 %collective-permute-start = (f32[1,2,4,1024]{3,2,1,0:T(4,128)S(1)}, f32[1,2,4,1024]{3,2,1,0:T(4,128)S(1)}, u32[]{:S(2)}, u32[]{:S(2)}) collective-permute-start(f32[1,2,4,1024]{3,2,1,0:T(4,128)S(1)} %get-tuple-element.19), channel_id=1, source_target_pairs={{0,8},{8,16},{16,24},{1,9},{9,17},{17,25},{2,10},{10,18},{18,26},{... | collective-permute-start | bytes 98312 | tf_op jit(solution)/shard_map/ppermute | solution.py:19
  2.8 16.7 %collective-permute-start.1 = (f32[1,2,4,1024]{3,2,1,0:T(4,128)S(1)}, f32[1,2,4,1024]{3,2,1,0:T(4,128)S(1)}, u32[]{:S(2)}, u32[]{:S(2)}) collective-permute-start(f32[1,2,4,1024]{3,2,1,0:T(4,128)S(1)} %get-tuple-element.18), channel_id=1, source_target_pairs={{8,0},{16,8},{24,16},{9,1},{17,9},{25,17},{10,2},{18,10},{26,18},{... | collective-permute-start | bytes 98312 | tf_op jit(solution)/shard_map/ppermute | solution.py:22
  9.4 10.0 %copy-start.1 = (pred[2,16]{1,0:T(4,128)(4,1)}, pred[2,16]{1,0:T(4,128)(4,1)S(1)}, u32[]{:S(2)}) copy-start(pred[2,16]{1,0:T(4,128)(4,1)S(1)} %iota_compare_fusion.6) | copy-start | bytes 100
  11.8 22.7 %all-to-all-start = ((f32[2,12,8]{1,2,0:T(8,128)}), f32[2,12,8]{1,2,0:T(8,128)S(1)}, u32[]{:S(2)}, u32[]{:S(2)}) async-start(f32[2,12,8]{1,2,0:T(8,128)} %fusion.10), calls=%async_computation | async-start | bytes 16384 | tf_op jit(solution)/shard_map/all_to_all | solution.py:106
  19.5 6.2 %collective-permute-start.2 = (f32[4,1,4,1024]{3,2,1,0:T(4,128)S(1)}, f32[4,1,4,1024]{3,2,1,0:T(4,128)S(1)}, u32[]{:S(2)}, u32[]{:S(2)}) collective-permute-start(f32[4,1,4,1024]{3,2,1,0:T(4,128)S(1)} %get-tuple-element.16), channel_id=1, source_target_pairs={{0,2},{2,4},{4,6},{1,3},{3,5},{5,7},{8,10},{10,12},{12,14},{9,11},... | collective-permute-start | bytes 196616 | tf_op jit(solution)/shard_map/ppermute | solution.py:19
  23.0 6.2 %collective-permute-start.3 = (f32[4,1,4,1024]{3,2,1,0:T(4,128)S(1)}, f32[4,1,4,1024]{3,2,1,0:T(4,128)S(1)}, u32[]{:S(2)}, u32[]{:S(2)}) collective-permute-start(f32[4,1,4,1024]{3,2,1,0:T(4,128)S(1)} %get-tuple-element.17), channel_id=1, source_target_pairs={{2,0},{4,2},{6,4},{3,1},{5,3},{7,5},{10,8},{12,10},{14,12},{11,9},... | collective-permute-start | bytes 196616 | tf_op jit(solution)/shard_map/ppermute | solution.py:22
  29.2 5.8 %collective-permute-start.4 = (f32[4,4,1,1024]{3,2,1,0:T(1,128)S(1)}, f32[4,4,1,1024]{3,2,1,0:T(1,128)S(1)}, u32[]{:S(2)}, u32[]{:S(2)}) collective-permute-start(f32[4,4,1,1024]{3,2,1,0:T(1,128)S(1)} %get-tuple-element.14), channel_id=1, source_target_pairs={{0,1},{2,3},{4,5},{6,7},{8,9},{10,11},{12,13},{14,15},{16,17},{18,... | collective-permute-start | bytes 196616 | tf_op jit(solution)/shard_map/ppermute | solution.py:19
  33.2 6.2 %collective-permute-start.5 = (f32[4,4,1,1024]{3,2,1,0:T(1,128)S(1)}, f32[4,4,1,1024]{3,2,1,0:T(1,128)S(1)}, u32[]{:S(2)}, u32[]{:S(2)}) collective-permute-start(f32[4,4,1,1024]{3,2,1,0:T(1,128)S(1)} %get-tuple-element.15), channel_id=1, source_target_pairs={{1,0},{3,2},{5,4},{7,6},{9,8},{11,10},{13,12},{15,14},{17,16},{19,... | collective-permute-start | bytes 196616 | tf_op jit(solution)/shard_map/ppermute | solution.py:22
  69.8 3.7 %copy-start.2 = (pred[2,16]{1,0:T(4,128)(4,1)S(1)}, pred[2,16]{1,0:T(4,128)(4,1)}, u32[]{:S(2)}) copy-start(pred[2,16]{1,0:T(4,128)(4,1)} %copy-done.1) | copy-start | bytes 100
  74.5 8.4 %all-to-all-start.1 = ((f32[2,12,1792]{2,1,0:T(8,128)}), f32[2,12,1792]{2,1,0:T(8,128)S(1)}, u32[]{:S(2)}, u32[]{:S(2)}) async-start(f32[2,12,1792]{2,1,0:T(8,128)} %fusion.8), calls=%async_computation.1 | async-start | bytes 458752 | tf_op jit(solution)/shard_map/all_to_all | solution.py:99
where the time goes:
time: 85.5 us; the launch traced here: 84.5 us
  local copies, waits for them, and re-layouts  30.8 us (36%)
  starting transfers between devices  23.3 us (27%)
  waiting for transfers between devices  13.3 us (16%)
  matrix products  11.8 us (14%)
  other arithmetic  4.99 us (6%)
    unnamed x21, local copies, waits for them, and re-layouts  17.3 us
    ppermute x3, starting transfers between devices, extended(): lax.ppermute(lax.slice_in_dim(block, block.shape[dim] - width, None, axis...  9.3 us
    ppermute x3, waiting for transfers between devices, extended(): lax.ppermute(lax.slice_in_dim(block, 0, width, axis=dim), axis, backward)  7.77 us
    dot_general x1, matrix products, shards(): jnp.einsum('xyzkij,xyzkjc->xyzkic', blocks, beside, precision=lax.Precisi...  7.55 us
    ppermute x3, starting transfers between devices, extended(): lax.ppermute(lax.slice_in_dim(block, 0, width, axis=dim), axis, backward)  7.29 us
    all_to_all x1, waiting for transfers between devices, shards(): lax.all_to_all(bucket(coarse.reshape(elements, 7 * CDOF * CDOF)), 'gz', s...  4.77 us
    reshape x1, local copies, waits for them, and re-layouts, shards(): blocks = fine_blocks.reshape(size_x, size_y, size_z, 7, DOF, DOF)  4.36 us
    all_to_all x1, starting transfers between devices, shards(): lax.all_to_all(bucket(coarse.reshape(elements, 7 * CDOF * CDOF)), 'gz', s...  3.44 us
  transfers between devices with their start and end apart: 8, of which 5 were waited for; matrix products, arithmetic and copies ran while one was open for 12% of the time, Pallas kernels for 0%

commit v1 on v0

v1 whole, which is shorter than its diff:
```python
import functools

import jax
import jax.numpy as jnp
from jax import lax
from jax.experimental import pallas as pl
from jax.experimental.pallas import tpu as pltpu
from jax.sharding import PartitionSpec as P

DOF = 64
CDOF = 16
AGGS = 8
LANES = 128
F32 = jnp.float32
BF16 = jnp.bfloat16
VMEM = pl.BlockSpec(memory_space=pltpu.VMEM)
SMEM = pl.BlockSpec(memory_space=pltpu.SMEM)


def iota(shape, dim):
    return lax.broadcasted_iota(jnp.int32, shape, dim)


def dot(a, b):
    return lax.dot_general(a, b, (((1,), (0,)), ((), ())), preferred_element_type=F32)


def split(x):
    high = x.astype(BF16)
    return high, (x - high.astype(F32)).astype(BF16)


def ones_where(mask):
    return jnp.where(mask, 1.0, 0.0).astype(BF16)


def collapse_matrix():
    same = iota((LANES, LANES), 0) % CDOF == iota((LANES, LANES), 1) % CDOF
    one = ones_where(same)
    return jnp.concatenate([one, one], axis=0)


def prolong_weights(pieces, collapse):
    diag = iota((DOF, LANES), 0) % 8 == iota((DOF, LANES), 1) // CDOF
    rows = []
    for piece in pieces:
        high, low = split(piece)
        parts = []
        for part in (high.astype(F32), low.astype(F32)):
            wide = jnp.broadcast_to(part[:, None, :], (8, 8, LANES)).reshape(DOF, LANES)
            parts.append(jnp.where(diag, wide, 0.0).astype(BF16))
        rows.append(jnp.concatenate(parts, axis=1))
    spread = dot(jnp.concatenate(rows, axis=0), collapse)
    lane = iota((DOF, LANES), 1)
    slot = lane // CDOF % 4
    full = spread[:DOF]
    for i in range(1, 4):
        full = jnp.where(slot == i, spread[i * DOF : (i + 1) * DOF], full)
    high, low = split(full)
    left = lane < DOF
    high, low = high.astype(F32), low.astype(F32)
    both = jnp.where(left, high, low).astype(BF16)
    first = jnp.where(left, high, 0.0).astype(BF16)
    return jnp.concatenate([both, both, first, first], axis=0)


def blocks_of(rows, weights):
    out = dot(rows, weights)
    return out + pltpu.roll(out, DOF, 1)


def diagonal(product, shift):
    keep = iota((DOF, LANES), 0) // CDOF + shift == iota((DOF, LANES), 1) // CDOF % 4
    kept = jnp.where(keep, product, 0.0).reshape(4, CDOF, LANES)
    return (kept[0] + kept[1]) + (kept[2] + kept[3])


def scatter_tools():
    spread = ones_where(iota((LANES, 2 * LANES), 0) % CDOF == iota((LANES, 2 * LANES), 1) % CDOF)
    element = ones_where(iota((LANES, LANES), 0) // CDOF == iota((LANES, LANES), 1) // CDOF)
    row = ones_where(iota((LANES, 2 * LANES), 0) % CDOF == iota((LANES, 2 * LANES), 1) // CDOF)
    return spread, element, jnp.concatenate([row, row], axis=0)


def scatter(pack, labels, base, count, tools):
    spread, element, row = tools
    high, low = split(pack)
    wide = [jnp.concatenate([part] * 8, axis=0) * element for part in (high, low)]
    flat = dot(jnp.concatenate(wide, axis=0), spread).astype(BF16) * row
    choose = ones_where(iota((count, LANES), 0) + base == labels)
    return dot(jnp.concatenate([choose, choose], axis=1), flat)


def lane_row(values):
    group = iota((1, LANES), 1) // CDOF
    row = jnp.full((1, LANES), values[0], jnp.int32)
    for i in range(1, 8):
        row = jnp.where(group == i, values[i], row)
    return row


def local_kernel(shape, group_size, place_ref, agg_ref, owner_ref, prolong_ref, fine_ref,
                 outer_ref, inner_ref, label_ref, rows_scr):
    bx, by, bz = shape
    rows_each = AGGS // group_size
    gx, gy, gz = place_ref[0], place_ref[1], place_ref[2]
    nx, ny, nz = agg_ref.shape
    owners = [owner_ref[0, 0, a] for a in range(AGGS)]
    ranks = []
    for a in range(AGGS):
        rank = jnp.int32(0)
        for b in range(a):
            rank += (owners[b] == owners[a]).astype(jnp.int32)
        ranks.append(rank)

    def look(table, index):
        value = table[0]
        for a in range(1, AGGS):
            value = jnp.where(index == a, table[a], value)
        return value

    def agg_at(x, y, z):
        px, py, pz = gx * bx + x, gy * by + y, gz * bz + z
        inside = (px >= 0) & (px < nx) & (py >= 0) & (py < ny) & (pz >= 0) & (pz < nz)
        cx = jnp.clip(px, 0, nx - 1)
        cy = jnp.clip(py, 0, ny - 1)
        cz = jnp.clip(pz, 0, nz - 1)
        return agg_ref[cx, cy, cz], inside

    own, owner_of, rank_of = {}, {}, {}
    for x in range(bx):
        for y in range(by):
            for z in range(bz):
                own[x, y, z] = agg_at(x, y, z)[0]
                owner_of[x, y, z] = look(owners, own[x, y, z])
                rank_of[x, y, z] = look(ranks, own[x, y, z])

    def outer_label(e, f, slots, extra):
        column, inside = agg_at(*f)
        label = owner_of[e] * slots + extra + column * AGGS + gz * rows_each + rank_of[e]
        return jnp.where(inside, label, -1)

    rows = []
    for face in range(1, 5):
        step = -1 if face % 2 else 1
        edge = 0 if face % 2 else 1
        values = []
        for side in range(2):
            for z in range(bz):
                e = (edge, side, z) if face < 3 else (side, edge, z)
                f = (e[0] + step, e[1], z) if face < 3 else (e[0], e[1] + step, z)
                values.append(outer_label(e, f, 8 * AGGS, 0))
        rows.append(lane_row(values))
    values = []
    for face in range(2):
        for x in range(bx):
            for y in range(by):
                z = 0 if face == 0 else bz - 1
                step = -1 if face == 0 else 1
                values.append(outer_label((x, y, z), (x, y, z + step), 16 * AGGS, face * 8 * AGGS))
    rows.append(lane_row(values))
    rows.append(jnp.full((3, LANES), -1, jnp.int32))
    label_ref[...] = jnp.concatenate(rows, axis=0).astype(F32)

    lane = iota((32, LANES), 1)
    sub = iota((32, LANES), 0) % 4
    p0, p1 = iota((LANES, LANES), 0), iota((LANES, LANES), 1)
    permute = ones_where((p0 % 4 == p1 % 4) & (p0 // 32 == p1 // 4 % 4) & (p0 // 4 % 8 == p1 // 16))
    wide_lane = iota((4, CDOF, 2 * LANES), 2) % LANES
    for xy in range(bx * by):
        raw = prolong_ref[xy]
        rolled = [raw] + [pltpu.roll(raw, 32 * m, 1) for m in range(1, 4)]
        stacked = []
        for tau in range(4):
            part = jnp.zeros_like(raw)
            for z in range(4):
                part = jnp.where((sub == z) & (lane // 32 == z), rolled[(z - tau) % 4], part)
            stacked.append(part)
        turned = jnp.concatenate(stacked, axis=0).T
        high, low = split(turned)
        left = dot(jnp.concatenate([high, low], axis=0), permute).astype(BF16)
        high, low = left[:LANES], left[LANES:]
        left = jnp.concatenate(
            [jnp.concatenate([high, high], axis=1), jnp.concatenate([low, jnp.zeros_like(low)], axis=1)],
            axis=0,
        )
        for first in range(0, 7, 2):
            slabs = [fine_ref[xy * 7 + k] for k in range(first, min(first + 2, 7))]
            halves = [split(slab) for slab in slabs]
            right = jnp.concatenate(
                [jnp.concatenate([h[i] for h in halves], axis=1) for i in range(2)], axis=0
            )
            width = right.shape[1]
            out = dot(left, right).reshape(2, 4, 2, CDOF, width)
            out = out[0] + out[1]
            q = jnp.where(wide_lane[:, :, :width] < DOF, out[:, 0], out[:, 1]).reshape(DOF, width)
            high, low = split(q)
            for i in range(len(slabs)):
                cut = slice(i * LANES, (i + 1) * LANES)
                rows_scr[xy * 7 + first + i] = jnp.concatenate([high[:, cut], low[:, cut]], axis=1)

    for side in range(2):
        outer_ref[side] = rows_scr[side * 7 + 1]
        outer_ref[2 + side] = rows_scr[(2 + side) * 7 + 2]
        outer_ref[4 + side] = rows_scr[2 * side * 7 + 3]
        outer_ref[6 + side] = rows_scr[(2 * side + 1) * 7 + 4]
    for xy in range(4):
        outer_ref[8, xy * CDOF : (xy + 1) * CDOF] = rows_scr[xy * 7 + 5, :CDOF]
        outer_ref[9, xy * CDOF : (xy + 1) * CDOF] = rows_scr[xy * 7 + 6, DOF - CDOF :]

    collapse = collapse_matrix()
    tools = scatter_tools()
    pieces, values = [], []
    for x in range(bx):
        for y in range(by):
            xy = x * by + y
            weights = prolong_weights(
                [prolong_ref[xy, pl.ds(z, 8, stride=4), :] for z in range(4)], collapse
            )
            slabs = [
                (xy * 7, 0, (x, y, 0)),
                (((1 - x) * by + y) * 7 + (2 if x else 1), 0, (1 - x, y, 0)),
                ((x * by + 1 - y) * 7 + (4 if y else 3), 0, (x, 1 - y, 0)),
                (xy * 7 + 5, -1, (x, y, 1)),
                (xy * 7 + 6, 1, (x, y, -1)),
            ]
            for index, shift, (ex, ey, ez) in slabs:
                pieces.append(diagonal(blocks_of(rows_scr[index], weights), shift))
                for z in range(bz):
                    if 0 <= z + ez < bz:
                        e = (ex, ey, z + ez)
                        values.append(
                            (owner_of[e] * AGGS + own[x, y, z]) * rows_each + rank_of[e]
                        )
                    else:
                        values.append(jnp.int32(-1))
    half = iota((CDOF, LANES), 1) < DOF
    total = jnp.zeros((8 * AGGS, 2 * LANES), F32)
    for i in range(0, len(pieces), 2):
        pack = jnp.where(half, pieces[i], pieces[i + 1])
        labels = lane_row(values[4 * i : 4 * i + 8])
        total += scatter(pack, labels, 0, 8 * AGGS, tools)
    inner_ref[...] = total


def outer_kernel(group_size, links, place_ref, outer_ref, inner_ref, label_ref, *refs):
    halos, sends = refs[:links], refs[links:]
    low_x, high_x, low_y, high_y = halos[:4]
    low_z, high_z = halos[4], halos[-1]
    gz = place_ref[2]
    collapse = collapse_matrix()

    def column(ref, xy):
        return [ref[xy, pl.ds(z, 8, stride=4), :] for z in range(4)]

    def layer(ref, z):
        return [ref[xy, pl.ds(z, 8, stride=4), :] for xy in range(4)]

    sources = [column(low_x, 2), column(low_x, 3), column(high_x, 0), column(high_x, 1),
               column(low_y, 1), column(low_y, 3), column(high_y, 0), column(high_y, 2),
               layer(low_z, 3), layer(high_z, 0)]
    half = iota((CDOF, LANES), 1) < DOF
    packs = []
    for i in range(0, 10, 2):
        pair = [
            diagonal(blocks_of(outer_ref[j], prolong_weights(sources[j], collapse)), 0)
            for j in (i, i + 1)
        ]
        packs.append(jnp.where(half, *pair))
    tail = jnp.concatenate(packs + [label_ref[...]], axis=0)
    count = 8 * AGGS // group_size
    for shift, send in enumerate(sends, 1):
        target = lax.rem(gz + shift, group_size)
        block = inner_ref[pl.ds(pl.multiple_of(target * count, count), count)]
        send[:count] = block[:, :LANES]
        send[count : 2 * count] = block[:, LANES:]
        send[2 * count :] = tail


def place_terms(out_ref, tail, gz, tools, add):
    labels = tail[5 * CDOF :].astype(jnp.int32)
    for k in range(5):
        rows = (16 if k == 4 else 8) * AGGS
        sums = scatter(tail[k * CDOF : (k + 1) * CDOF], labels[k : k + 1], gz * rows, rows, tools)
        for c in range(rows // 8):
            at = slice(((k + 1) * 8 + c) * 2 * LANES, ((k + 1) * 8 + c + 1) * 2 * LANES)
            value = sums[c * 8 : (c + 1) * 8]
            out_ref[:, at] = add[:, at] + value if add is not None else value


def own_kernel(group_size, place_ref, inner_ref, send_ref, out_ref):
    gz = place_ref[2]
    rows_each = AGGS // group_size
    count = 8 * AGGS // group_size
    place_terms(out_ref, send_ref[2 * count :], gz, scatter_tools(), None)
    mine = iota((AGGS, 2 * LANES), 0) // rows_each == gz
    block = inner_ref[pl.ds(pl.multiple_of(gz * count, count), count)]
    for c in range(AGGS):
        part = block[c * rows_each : (c + 1) * rows_each]
        part = jnp.concatenate([part] * group_size, axis=0)
        out_ref[:, c * 2 * LANES : (c + 1) * 2 * LANES] = jnp.where(mine, part, 0.0)


def final_kernel(group_size, place_ref, own_ref, *refs):
    received, out_ref = refs[:-1], refs[-1]
    gz = place_ref[2]
    rows_each = AGGS // group_size
    count = 8 * AGGS // group_size
    tools = scatter_tools()
    total = own_ref
    for shift, ref in enumerate(received, 1):
        brick = lax.rem(gz - shift + group_size, group_size)
        place_terms(out_ref, ref[2 * count :], gz, tools, total)
        theirs = iota((AGGS, LANES), 0) // rows_each == brick
        for c in range(AGGS):
            for h in range(2):
                part = ref[h * count + c * rows_each : h * count + (c + 1) * rows_each]
                part = jnp.concatenate([part] * group_size, axis=0)
                at = slice((2 * c + h) * LANES, (2 * c + h + 1) * LANES)
                out_ref[:, at] = jnp.where(theirs, part, total[:, at])
        total = out_ref


def rotation(count, step):
    return [(i, (i + step) % count) for i in range(count)]


def shards(fine_blocks, prolong, agg_map, owner_map):
    bx, by, bz = fine_blocks.shape[:3]
    group_size = lax.axis_size("gz")
    fine = fine_blocks.transpose(0, 1, 3, 2, 4).reshape(bx * by * 7, bz, 32, LANES)
    fine = fine.transpose(0, 2, 1, 3).reshape(bx * by * 7, 32 * bz, LANES)
    base = prolong.reshape(bx * by, bz, 8, LANES).transpose(0, 2, 1, 3).reshape(bx * by, 8 * bz, LANES)
    place = jnp.stack([lax.axis_index(axis) for axis in ("gx", "gy", "gz")]).astype(jnp.int32)
    halos = []
    for axis in ("gx", "gy", "gz"):
        count = lax.axis_size(axis)
        halos.append(lax.ppermute(base, axis, rotation(count, 1)))
        if axis != "gz" or count > 2:
            halos.append(lax.ppermute(base, axis, rotation(count, -1)))
    params = pltpu.CompilerParams(vmem_limit_bytes=32 * 1024 * 1024)
    shape = jax.ShapeDtypeStruct
    outer, inner, labels = pl.pallas_call(
        functools.partial(local_kernel, (bx, by, bz), group_size),
        out_shape=[shape((10, DOF, 2 * LANES), BF16), shape((8 * AGGS, 2 * LANES), F32), shape((8, LANES), F32)],
        in_specs=[SMEM, SMEM, SMEM, VMEM, VMEM],
        out_specs=[VMEM] * 3,
        scratch_shapes=[pltpu.VMEM((bx * by * 7, DOF, 2 * LANES), BF16)],
        compiler_params=params,
        cost_estimate=pl.CostEstimate(flops=int(2e9), bytes_accessed=int(4e6), transcendentals=0),
    )(place, agg_map, owner_map, base, fine)
    count = 8 * AGGS // group_size
    size = 2 * count + 5 * CDOF + 8
    sends = pl.pallas_call(
        functools.partial(outer_kernel, group_size, len(halos)),
        out_shape=[shape((size, LANES), F32)] * (group_size - 1),
        in_specs=[SMEM] + [VMEM] * (3 + len(halos)),
        out_specs=[VMEM] * (group_size - 1),
        compiler_params=params,
    )(place, outer, inner, labels, *halos)
    received = [
        lax.ppermute(send, "gz", rotation(group_size, shift)) for shift, send in enumerate(sends, 1)
    ]
    full = shape((AGGS, 7 * AGGS * CDOF * CDOF), F32)
    own = pl.pallas_call(
        functools.partial(own_kernel, group_size),
        out_shape=full,
        in_specs=[SMEM, VMEM, VMEM],
        out_specs=VMEM,
        compiler_params=params,
        cost_estimate=pl.CostEstimate(flops=int(1e9), bytes_accessed=int(2e6), transcendentals=0),
    )(place, inner, sends[0])
    out = pl.pallas_call(
        functools.partial(final_kernel, group_size),
        out_shape=full,
        in_specs=[SMEM, VMEM] + [VMEM] * (group_size - 1),
        out_specs=VMEM,
        compiler_params=params,
    )(place, own, *received)
    return out[None, None]


def solution(mesh):
    placed = (P("gx", "gy", "gz", None, None), P("gx", "gy", "gz", None), P(), P("gx", "gy", "gz"))
    return jax.shard_map(
        shards, mesh=mesh, in_specs=placed, out_specs=P("gx", "gy", "gz", None), check_vma=False
    )
```

time: 85.5 us -> 26.5 us (0.31)
  the two profiles are of different devices: /device:TPU:10 before, /device:TPU:0 now
where the time goes in v1:
time: 26.5 us; the launch traced here: 26.3 us
  Pallas kernels  11.8 us (45%)
  starting transfers between devices  7.65 us (29%)
  local copies, waits for them, and re-layouts  3.75 us (14%)
  waiting for transfers between devices  2.9 us (11%)
    pallas_call x1, Pallas kernels, shards(): pl.pallas_call(functools.partial(local_kernel, (bx, by, bz), group_size),...  4.76 us
    ppermute x2, starting transfers between devices, shards(): halos.append(lax.ppermute(base, axis, rotation(count, -1)))  3.97 us
    unnamed x8, local copies, waits for them, and re-layouts  3.75 us
    ppermute x3, starting transfers between devices, shards(): halos.append(lax.ppermute(base, axis, rotation(count, 1)))  3.11 us
    pallas_call x1, Pallas kernels, shards(): pl.pallas_call(functools.partial(outer_kernel, group_size, len(halos)), o...  2.89 us
    ppermute x1, waiting for transfers between devices, shards(): lax.ppermute(send, 'gz', rotation(group_size, shift))  2.88 us
    pallas_call x1, Pallas kernels, shards(): pl.pallas_call(functools.partial(final_kernel, group_size), out_shape=ful...  2.48 us
    pallas_call x1, Pallas kernels, shards(): pl.pallas_call(functools.partial(own_kernel, group_size), out_shape=full,...  1.7 us
  transfers between devices with their start and end apart: 6, of which 1 were waited for; matrix products, arithmetic and copies ran while one was open for 0% of the time, Pallas kernels for 25%

profile of v1, /device:TPU:0, one launch (start us, length us, event | category | flops | bytes accessed | tf_op | source)
XLA Modules:
  0.0 26.3 jit_solution(10834959006208114578)
XLA Ops:
  0.0 3.0 %collective-permute-start.4 = (f32[4,32,128]{2,1,0:T(8,128)}, f32[4,32,128]{2,1,0:T(8,128)S(1)}, u32[]{:S(2)}, u32[]{:S(2)}) collective-permute-start(f32[4,32,128]{2,1,0:T(8,128)} %bitcast.17), channel_id=1, source_target_pairs={{0,1},{1,0},{2,3},{3,2},{4,5},{5,4},{6,7},{7,6},{8,9},{9,8},{10,11... | collective-permute-start | bytes 196616 | tf_op jit(solution)/shard_map/ppermute | solution.py:338
  3.0 3.6 %collective-permute-start.3 = (f32[4,32,128]{2,1,0:T(8,128)}, f32[4,32,128]{2,1,0:T(8,128)S(1)}, u32[]{:S(2)}, u32[]{:S(2)}) collective-permute-start(f32[4,32,128]{2,1,0:T(8,128)} %bitcast.18), channel_id=1, source_target_pairs={{0,6},{2,0},{4,2},{6,4},{1,7},{3,1},{5,3},{7,5},{8,14},{10,8},{12,... | collective-permute-start | bytes 196616 | tf_op jit(solution)/shard_map/ppermute | solution.py:340
  6.6 0.0 collective-permute-start.2
  6.6 0.4 %collective-permute-start.1 = (f32[4,32,128]{2,1,0:T(8,128)}, f32[4,32,128]{2,1,0:T(8,128)S(1)}, u32[]{:S(2)}, u32[]{:S(2)}) collective-permute-start(f32[4,32,128]{2,1,0:T(8,128)} %bitcast.20), channel_id=1, source_target_pairs={{0,24},{8,0},{16,8},{24,16},{1,25},{9,1},{17,9},{25,17},{2,26},{10... | collective-permute-start | bytes 196616 | tf_op jit(solution)/shard_map/ppermute | solution.py:340
  6.9 0.1 collective-permute-start
  7.1 0.1 pad_add_fusion.place_ref
  7.2 0.0 copy-start
  7.2 1.5 %copy-done = f32[2,2,4,7,4096]{4,2,3,1,0:T(4,128)S(1)} copy-done((f32[2,2,4,7,4096]{4,2,3,1,0:T(4,128)S(1)}, f32[2,2,4,7,4096]{4,2,3,1,0:T(4,128)}, u32[]{:S(2)}) %copy-start) | copy-done | bytes 1835032
  8.7 0.0 copy-start.1
  8.7 0.8 %copy-done.1 = f32[2,2,4,1024]{3,2,1,0:T(4,128)S(1)} copy-done((f32[2,2,4,1024]{3,2,1,0:T(4,128)S(1)}, f32[2,2,4,1024]{3,2,1,0:T(4,128)}, u32[]{:S(2)}) %copy-start.1) | copy-done | bytes 65560
  9.5 0.0 copy-start.2
  9.5 0.8 %copy-done.2 = s32[8,8,8]{2,1,0:T(8,128)S(1)} copy-done((s32[8,8,8]{2,1,0:T(8,128)S(1)}, s32[8,8,8]{2,1,0:T(8,128)}, u32[]{:S(2)}) %copy-start.2) | copy-done | bytes 2072
  10.3 0.0 copy-start.3
  10.3 0.7 %copy-done.3 = s32[1,1,8]{2,1,0:T(1,128)S(1)} copy-done((s32[1,1,8]{2,1,0:T(1,128)S(1)}, s32[1,1,8]{2,1,0:T(1,128)}, u32[]{:S(2)}) %copy-start.3) | copy-done | bytes 56
  10.9 4.8 %shard_map.46 = (bf16[10,64,256]{2,1,0:T(8,128)(2,1)S(1)}, f32[64,256]{1,0:T(8,128)S(1)}, f32[8,128]{1,0:T(8,128)S(1)}) custom-call(s32[3]{0:T(128)S(1)} %pad_add_fusion.place_ref, s32[8,8,8]{2,1,0:T(8,128)S(1)} %copy-done.2, s32[1,1,8]{2,1,0:T(1,128)S(1)} %copy-done.3, f32[4,32,128]{2,1,0:T(8,128)S(1)} %bitcast.22, f32[28,128,128]{2,1,0:T(8,128)S(1)} %bitcast.16), custom_call_target="tpu_custom_call" | custom-call | flops 2000000000 | bytes 4000000 | tf_op jit(solution)/shard_map/pallas_call | solution.py:343
  15.7 0.0 collective-permute-done.4.refs_4_
  15.7 0.0 collective-permute-done.3.refs_3_
  15.7 0.0 collective-permute-done.2.refs_2_
  15.7 0.0 collective-permute-done.1.refs_1_
  15.7 0.0 collective-permute-done.refs_0_
  15.7 2.9 %shard_map.47.send_ref = f32[152,128]{1,0:T(8,128)S(1)} custom-call(s32[3]{0:T(128)S(1)} %pad_add_fusion.place_ref, bf16[10,64,256]{2,1,0:T(8,128)(2,1)S(1)} %get-tuple-element.9.outer_ref, f32[64,256]{1,0:T(8,128)S(1)} %get-tuple-element.8.inner_ref, f32[8,128]{1,0:T(8,128)S(1)} %get-tuple-element.10.label_ref, ...), custom_call_target="tpu_custom_call" | custom-call | tf_op jit(solution)/shard_map/pallas_call | solution.py:354
  18.6 0.6 %collective-permute-start.5 = (f32[152,128]{1,0:T(8,128)S(1)}, f32[152,128]{1,0:T(8,128)S(1)}, u32[]{:S(2)}, u32[]{:S(2)}) collective-permute-start(f32[152,128]{1,0:T(8,128)S(1)} %shard_map.47.send_ref), channel_id=1, source_target_pairs={{0,1},{1,0},{2,3},{3,2},{4,5},{5,4},{6,7},{7,6},{8,9},{9,8},{10,11... | collective-permute-start | bytes 233480 | tf_op jit(solution)/shard_map/ppermute | solution.py:362
  19.2 1.7 %shard_map.48.own_ref = f32[8,14336]{1,0:T(8,128)S(1)} custom-call(s32[3]{0:T(128)S(1)} %pad_add_fusion.place_ref, f32[64,256]{1,0:T(8,128)S(1)} %get-tuple-element.8.inner_ref, f32[152,128]{1,0:T(8,128)S(1)} %shard_map.47.send_ref), custom_call_target="tpu_custom_call" | custom-call | flops 1000000000 | bytes 2000000 | tf_op jit(solution)/shard_map/pallas_call | solution.py:365
  20.9 2.9 %collective-permute-done.5.refs_0_ = f32[152,128]{1,0:T(8,128)S(1)} collective-permute-done((f32[152,128]{1,0:T(8,128)S(1)}, f32[152,128]{1,0:T(8,128)S(1)}, u32[]{:S(2)}, u32[]{:S(2)}) %collective-permute-start.5) | collective-permute-done | bytes 77856 | tf_op jit(solution)/shard_map/ppermute | solution.py:362
  23.8 2.5 %shard_map.49 = f32[8,14336]{1,0:T(8,128)} custom-call(s32[3]{0:T(128)S(1)} %pad_add_fusion.place_ref, f32[8,14336]{1,0:T(8,128)S(1)} %shard_map.48.own_ref, f32[152,128]{1,0:T(8,128)S(1)} %collective-permute-done.5.refs_0_), custom_call_target="tpu_custom_call" | custom-call | tf_op jit(solution)/shard_map/pallas_call | solution.py:373
Async XLA Ops:
  0.0 15.7 %collective-permute-start.4 = (f32[4,32,128]{2,1,0:T(8,128)}, f32[4,32,128]{2,1,0:T(8,128)S(1)}, u32[]{:S(2)}, u32[]{:S(2)}) collective-permute-start(f32[4,32,128]{2,1,0:T(8,128)} %bitcast.17), channel_id=1, source_target_pairs={{0,1},{1,0},{2,3},{3,2},{4,5},{5,4},{6,7},{7,6},{8,9},{9,8},{10,11... | collective-permute-start | bytes 196616 | tf_op jit(solution)/shard_map/ppermute | solution.py:338
  3.0 12.7 %collective-permute-start.3 = (f32[4,32,128]{2,1,0:T(8,128)}, f32[4,32,128]{2,1,0:T(8,128)S(1)}, u32[]{:S(2)}, u32[]{:S(2)}) collective-permute-start(f32[4,32,128]{2,1,0:T(8,128)} %bitcast.18), channel_id=1, source_target_pairs={{0,6},{2,0},{4,2},{6,4},{1,7},{3,1},{5,3},{7,5},{8,14},{10,8},{12,... | collective-permute-start | bytes 196616 | tf_op jit(solution)/shard_map/ppermute | solution.py:340
  6.6 9.1 %collective-permute-start.2 = (f32[4,32,128]{2,1,0:T(8,128)}, f32[4,32,128]{2,1,0:T(8,128)S(1)}, u32[]{:S(2)}, u32[]{:S(2)}) collective-permute-start(f32[4,32,128]{2,1,0:T(8,128)} %bitcast.19), channel_id=1, source_target_pairs={{0,2},{2,4},{4,6},{6,0},{1,3},{3,5},{5,7},{7,1},{8,10},{10,12},{12... | collective-permute-start | bytes 196616 | tf_op jit(solution)/shard_map/ppermute | solution.py:338
  6.6 9.1 %collective-permute-start.1 = (f32[4,32,128]{2,1,0:T(8,128)}, f32[4,32,128]{2,1,0:T(8,128)S(1)}, u32[]{:S(2)}, u32[]{:S(2)}) collective-permute-start(f32[4,32,128]{2,1,0:T(8,128)} %bitcast.20), channel_id=1, source_target_pairs={{0,24},{8,0},{16,8},{24,16},{1,25},{9,1},{17,9},{25,17},{2,26},{10... | collective-permute-start | bytes 196616 | tf_op jit(solution)/shard_map/ppermute | solution.py:340
  6.9 8.8 %collective-permute-start = (f32[4,32,128]{2,1,0:T(8,128)}, f32[4,32,128]{2,1,0:T(8,128)S(1)}, u32[]{:S(2)}, u32[]{:S(2)}) collective-permute-start(f32[4,32,128]{2,1,0:T(8,128)} %bitcast.21), channel_id=1, source_target_pairs={{0,8},{8,16},{16,24},{24,0},{1,9},{9,17},{17,25},{25,1},{2,10},{10... | collective-permute-start | bytes 196616 | tf_op jit(solution)/shard_map/ppermute | solution.py:338
  7.2 1.5 %copy-start = (f32[2,2,4,7,4096]{4,2,3,1,0:T(4,128)S(1)}, f32[2,2,4,7,4096]{4,2,3,1,0:T(4,128)}, u32[]{:S(2)}) copy-start(f32[2,2,4,7,4096]{4,2,3,1,0:T(4,128)} %param.4) | copy-start | bytes 5505028
  8.7 0.8 %copy-start.1 = (f32[2,2,4,1024]{3,2,1,0:T(4,128)S(1)}, f32[2,2,4,1024]{3,2,1,0:T(4,128)}, u32[]{:S(2)}) copy-start(f32[2,2,4,1024]{3,2,1,0:T(4,128)} %param.5) | copy-start | bytes 196612
  9.5 0.8 %copy-start.2 = (s32[8,8,8]{2,1,0:T(8,128)S(1)}, s32[8,8,8]{2,1,0:T(8,128)}, u32[]{:S(2)}) copy-start(s32[8,8,8]{2,1,0:T(8,128)} %agg_ref.1) | copy-start | bytes 6148
  10.3 0.7 %copy-start.3 = (s32[1,1,8]{2,1,0:T(1,128)S(1)}, s32[1,1,8]{2,1,0:T(1,128)}, u32[]{:S(2)}) copy-start(s32[1,1,8]{2,1,0:T(1,128)} %owner_ref.1) | copy-start | bytes 100
  18.6 5.2 %collective-permute-start.5 = (f32[152,128]{1,0:T(8,128)S(1)}, f32[152,128]{1,0:T(8,128)S(1)}, u32[]{:S(2)}, u32[]{:S(2)}) collective-permute-start(f32[152,128]{1,0:T(8,128)S(1)} %shard_map.47.send_ref), channel_id=1, source_target_pairs={{0,1},{1,0},{2,3},{3,2},{4,5},{5,4},{6,7},{7,6},{8,9},{9,8},{10,11... | collective-permute-start | bytes 233480 | tf_op jit(solution)/shard_map/ppermute | solution.py:362

commit v2 on v0

v2 whole, which is shorter than its diff:
```python
import functools

import jax
import jax.numpy as jnp
from jax import lax
from jax.experimental import pallas as pl
from jax.experimental.pallas import tpu as pltpu
from jax.sharding import PartitionSpec as P

DOF = 64
CDOF = 16
AGGS = 8
FACES = 7
LANES = 128
WIDE = 2 * LANES
F32 = jnp.float32
BF16 = jnp.bfloat16
VMEM = pl.BlockSpec(memory_space=pltpu.VMEM)
HBM = pl.BlockSpec(memory_space=pltpu.HBM)


def iota(shape, dim):
    return lax.broadcasted_iota(jnp.int32, shape, dim)


def dot(a, b):
    return lax.dot_general(a, b, (((1,), (0,)), ((), ())), preferred_element_type=F32)


def split(x):
    high = x.astype(BF16)
    return high, (x - high.astype(F32)).astype(BF16)


def ones_where(mask):
    return jnp.where(mask, 1.0, 0.0).astype(BF16)


def rows_of(parts):
    return jnp.concatenate(parts, axis=0)


def lanes_of(parts):
    return jnp.concatenate(parts, axis=1)


def column_picker():
    r, q = iota((WIDE, 32), 0), iota((WIDE, 32), 1)
    return ones_where(q == r // 8 % 8 * 4 + r // DOF)


def layer_picker(z):
    r, q = iota((WIDE, LANES), 0), iota((WIDE, LANES), 1)
    return ones_where(q == r // DOF * 32 + r // 8 % 8 * 4 + z)


def prolong_weights(picked):
    count = len(picked)
    keep = iota((WIDE, WIDE), 0) % 8 == iota((WIDE, WIDE), 1) // CDOF % 8
    kept = [jnp.where(keep, p, 0.0).astype(BF16) for p in picked]
    collapse = ones_where(iota((WIDE, LANES), 0) % CDOF == iota((WIDE, LANES), 1) % CDOF)
    spread = dot(rows_of(kept), collapse).reshape(count, 4, DOF, LANES)
    lane = iota((DOF, LANES), 1)
    slot = lane // CDOF % 4
    left = lane < DOF
    factors = []
    for c in range(count):
        full = spread[c, 0]
        for i in range(1, 4):
            full = jnp.where(slot == i, spread[c, i], full)
        high = full.astype(BF16).astype(F32)
        both = jnp.where(left, high, full - high).astype(BF16)
        first = jnp.where(left, high, 0.0).astype(BF16)
        factors.append(rows_of([both, both, first, first]))
    return factors


def blocks_of(rows, factor):
    out = dot(rows, factor)
    return out + pltpu.roll(out, DOF, 1)


def diagonal(product, shift):
    keep = iota((DOF, LANES), 0) // CDOF + shift == iota((DOF, LANES), 1) // CDOF % 4
    kept = jnp.where(keep, product, 0.0).reshape(4, CDOF, LANES)
    return (kept[0] + kept[1]) + (kept[2] + kept[3])


def flatten(packs):
    spread = ones_where(iota((LANES, WIDE), 0) % CDOF == iota((LANES, WIDE), 1) % CDOF)
    element = ones_where(iota((LANES, LANES), 0) // CDOF == iota((LANES, LANES), 1) // CDOF)
    row = ones_where(iota((WIDE, WIDE), 0) % CDOF == iota((WIDE, WIDE), 1) // CDOF)
    wide = [rows_of([part] * 8) * element for pack in packs for part in split(pack)]
    flat = dot(rows_of(wide), spread).astype(BF16)
    return [flat[i * WIDE : (i + 1) * WIDE] * row for i in range(len(packs))]


def choose(labels, base, count):
    return ones_where(iota((count, LANES), 0) + base == labels)


def local_kernel(shape, group_size, agg_hbm, owner_hbm, prolong_hbm, fine_hbm, outer_ref, inner_ref, label_ref,
                 agg_ref, owner_ref, prolong_ref, fine_ref, rows_scr, sems):
    bx, by, bz = shape
    columns = bx * by
    rows_each = AGGS // group_size
    copies = [
        pltpu.make_async_copy(prolong_hbm, prolong_ref, sems.at[0]),
        pltpu.make_async_copy(agg_hbm, agg_ref, sems.at[1]),
        pltpu.make_async_copy(owner_hbm, owner_ref, sems.at[2]),
    ]
    for i in range(columns):
        part = pl.ds(i * FACES, FACES)
        copies.append(pltpu.make_async_copy(fine_hbm.at[part], fine_ref.at[part], sems.at[3 + i]))
    for copy in copies:
        copy.start()
    gx, gy, gz = lax.axis_index("gx"), lax.axis_index("gy"), lax.axis_index("gz")
    nx, ny, nz = agg_ref.shape

    copies[0].wait()
    lane = iota((32, LANES), 1)
    sub = iota((32, LANES), 0) % 4
    p0, p1 = iota((LANES, LANES), 0), iota((LANES, LANES), 1)
    permute = ones_where((p0 % 4 == p1 % 4) & (p0 // 32 == p1 // 4 % 4) & (p0 // 4 % 8 == p1 // 16))
    turned = []
    for xy in range(columns):
        raw = prolong_ref[xy]
        rolled = [raw] + [pltpu.roll(raw, 32 * m, 1) for m in range(1, 4)]
        stacked = []
        for tau in range(4):
            part = jnp.zeros_like(raw)
            for z in range(4):
                part = jnp.where((sub == z) & (lane // 32 == z), rolled[(z - tau) % 4], part)
            stacked.append(part)
        turned += split(rows_of(stacked).T)
    lefts = dot(rows_of(turned), permute).astype(BF16)
    picked = dot(column_picker(), lanes_of([h for xy in range(columns) for h in split(prolong_ref[xy])]))
    factors = prolong_weights([picked[:, xy * WIDE : (xy + 1) * WIDE] for xy in range(columns)])

    wide_lane = iota((4, CDOF, WIDE), 2) % LANES
    for xy in range(columns):
        copies[3 + xy].wait()
        high = lefts[xy * WIDE : xy * WIDE + LANES]
        low = lefts[xy * WIDE + LANES : (xy + 1) * WIDE]
        left = rows_of([lanes_of([high, high]), lanes_of([low, jnp.zeros_like(low)])])
        for first in range(0, FACES, 2):
            count = min(2, FACES - first)
            width = count * LANES
            halves = [split(fine_ref[xy * FACES + first + i]) for i in range(count)]
            right = rows_of([lanes_of([h[i] for h in halves]) for i in range(2)])
            out = dot(left, right).reshape(2, 4, 2, CDOF, width)
            out = out[0] + out[1]
            q = jnp.where(wide_lane[:, :, :width] < DOF, out[:, 0], out[:, 1]).reshape(DOF, width)
            high_q, low_q = split(q)
            for i in range(count):
                cut = slice(i * LANES, (i + 1) * LANES)
                rows_scr[xy * FACES + first + i] = lanes_of([high_q[:, cut], low_q[:, cut]])

    for side in range(2):
        outer_ref[side] = rows_scr[side * FACES + 1]
        outer_ref[2 + side] = rows_scr[(2 + side) * FACES + 2]
        outer_ref[4 + side] = rows_scr[2 * side * FACES + 3]
        outer_ref[6 + side] = rows_scr[(2 * side + 1) * FACES + 4]
    for xy in range(columns):
        at = slice(xy * CDOF, (xy + 1) * CDOF)
        outer_ref[8, at] = rows_scr[xy * FACES + 5, :CDOF]
        outer_ref[9, at] = rows_scr[xy * FACES + 6, DOF - CDOF :]

    copies[1].wait()
    copies[2].wait()
    aggs = (agg_ref[...] + 1).reshape(nx * ny, nz).astype(F32).astype(BF16)
    width = 5 * LANES
    z_row, z_lane = iota((nz, width), 0), iota((nz, width), 1)
    kind, place = z_lane // LANES, z_lane % LANES
    slot, face = place // CDOF % 4, place // DOF
    z_off = jnp.where(kind == 0, slot, jnp.where(kind == 1, slot + 1, slot - 1))
    z_off = jnp.where(kind == 3, face * (bz - 1), jnp.where(kind == 4, face * (bz + 1) - 1, z_off))
    by_lane = dot(aggs, ones_where(z_row == gz * bz + z_off)).astype(BF16)
    count = 24
    r = iota((count, nx * ny), 0)
    own_x, own_y = r // 2 % 2, r % 2
    group = r // 4
    dx = jnp.where(group == 1, 1 - own_x, own_x)
    dy = jnp.where(group == 2, 1 - own_y, own_y)
    dx = jnp.where(group == 4, own_x * (bx + 1) - 1, jnp.where(group == 5, own_y, dx))
    dy = jnp.where(group == 4, own_y, jnp.where(group == 5, own_x * (by + 1) - 1, dy))
    px, py = gx * bx + dx, gy * by + dy
    inside = (px >= 0) & (px < nx) & (py >= 0) & (py < ny) & (group != 3)
    at = jnp.where(inside, px * ny + py, -1)
    table = dot(ones_where(iota((count, nx * ny), 1) == at), by_lane).astype(jnp.int32)
    owners = owner_ref[0]
    slots = iota((1, AGGS), 1)
    rank = jnp.zeros((1, AGGS), jnp.int32)
    for a in range(AGGS - 1):
        rank += jnp.where((slots > a) & (owners == owners[:, a : a + 1]), 1, 0)
    own = table[:16]
    owner = jnp.zeros_like(own)
    ranks = jnp.zeros_like(own)
    for a in range(AGGS):
        owner = jnp.where(own == a + 1, owners[:, a : a + 1], owner)
        ranks = jnp.where(own == a + 1, rank[:, a : a + 1], ranks)
    inner_base = owner * (AGGS * rows_each) + ranks
    outer_base = owner * (AGGS * AGGS) + gz * rows_each + ranks

    def cut(array, row, part):
        return array[row : row + 1, part * LANES : (part + 1) * LANES]

    first_half = iota((1, LANES), 1) < DOF
    level = iota((1, LANES), 1) // CDOF % 4

    def pair(array, one, two, part=0):
        return jnp.where(first_half, cut(array, one, part), cut(array, two, part))

    labels = []
    for row, part, valid in ((0, 0, None), (4, 0, None), (8, 0, None), (0, 1, level < bz - 1), (0, 2, level > 0)):
        for x in range(bx):
            label = pair(inner_base, row + 2 * x, row + 2 * x + 1, part)
            label += (pair(table, 2 * x, 2 * x + 1) - 1) * rows_each
            labels.append(label if valid is None else jnp.where(valid, label, -1))
    outer_labels = []
    for k, pick in enumerate(((0, 1), (2, 3), (0, 2), (1, 3))):
        other = pair(table, 16 + 2 * k, 17 + 2 * k)
        label = pair(outer_base, *pick) + (other - 1) * AGGS
        outer_labels.append(jnp.where(other > 0, label, -1))

    def by_column(array, part):
        value = cut(array, 0, part)
        for xy in range(1, columns):
            value = jnp.where(level == xy, cut(array, xy, part), value)
        return value

    other = by_column(table, 4)
    label = by_column(outer_base + owner * (AGGS * AGGS), 3) + (other - 1) * AGGS
    label += jnp.where(first_half, 0, AGGS * AGGS)
    outer_labels.append(jnp.where(other > 0, label, -1))
    label_ref[...] = rows_of(outer_labels + [jnp.full((3, LANES), -1, jnp.int32)]).astype(F32)

    pieces = [[] for _ in range(5)]
    for x in range(bx):
        for y in range(by):
            xy = x * by + y
            sources = (
                (xy * FACES, 0),
                (((1 - x) * by + y) * FACES + (2 if x else 1), 0),
                ((x * by + 1 - y) * FACES + (4 if y else 3), 0),
                (xy * FACES + 5, -1),
                (xy * FACES + 6, 1),
            )
            product = blocks_of(rows_of([rows_scr[index] for index, _ in sources]), factors[xy])
            for i, (_, shift) in enumerate(sources):
                pieces[i].append(diagonal(product[i * DOF : (i + 1) * DOF], shift))
    half = iota((CDOF, LANES), 1) < DOF
    packs = [jnp.where(half, p[2 * x], p[2 * x + 1]) for p in pieces for x in range(bx)]
    flat = flatten(packs)
    chosen = [choose(label, 0, AGGS * AGGS) for label in labels]
    inner_ref[...] = dot(lanes_of([c for c in chosen for _ in range(2)]), rows_of(flat))


def outer_kernel(group_size, links, outer_ref, inner_ref, label_ref, *refs):
    halos, sends = refs[:links], refs[links:]
    low_x, high_x, low_y, high_y = halos[:4]
    low_z, high_z = halos[4], halos[-1]
    gz = lax.axis_index("gz")
    sources = ((low_x, 2), (low_x, 3), (high_x, 0), (high_x, 1), (low_y, 1), (low_y, 3), (high_y, 0), (high_y, 2))
    picked = dot(column_picker(), lanes_of([h for ref, xy in sources for h in split(ref[xy])]))
    picked = [picked[:, i * WIDE : (i + 1) * WIDE] for i in range(len(sources))]
    for ref, z in ((low_z, 3), (high_z, 0)):
        picked.append(dot(layer_picker(z), lanes_of(split(ref[...].reshape(LANES, LANES)))))
    factors = prolong_weights(picked)
    pieces = [diagonal(blocks_of(outer_ref[i], factors[i]), 0) for i in range(len(factors))]
    half = iota((CDOF, LANES), 1) < DOF
    packs = [jnp.where(half, pieces[i], pieces[i + 1]) for i in range(0, len(pieces), 2)]
    tail = rows_of(packs + [label_ref[...]])
    count = AGGS * AGGS // group_size
    for shift, send in enumerate(sends, 1):
        target = lax.rem(gz + shift, group_size)
        block = inner_ref[pl.ds(pl.multiple_of(target * count, count), count)]
        send[:count] = block[:, :LANES]
        send[count : 2 * count] = block[:, LANES:]
        send[2 * count :] = tail


def outer_sums(tails, gz):
    count = len(tails)
    packs = [tail[k * CDOF : (k + 1) * CDOF] for k in range(5) for tail in tails]
    flat = flatten(packs)
    labels = [tail[5 * CDOF :].astype(jnp.int32) for tail in tails]
    sums = []
    for k in range(5):
        rows = (2 if k == 4 else 1) * AGGS * AGGS
        chosen = [choose(label[k : k + 1], gz * rows, rows) for label in labels for _ in range(2)]
        sums.append(dot(lanes_of(chosen), rows_of(flat[k * count : (k + 1) * count])))
    return sums


def own_kernel(group_size, inner_ref, send_ref, out_ref):
    gz = lax.axis_index("gz")
    rows_each = AGGS // group_size
    count = AGGS * AGGS // group_size
    mine = iota((AGGS, WIDE), 0) // rows_each == gz
    block = inner_ref[pl.ds(pl.multiple_of(gz * count, count), count)]
    for c in range(AGGS):
        part = rows_of([block[c * rows_each : (c + 1) * rows_each]] * group_size)
        out_ref[:, c * WIDE : (c + 1) * WIDE] = jnp.where(mine, part, 0.0)
    at = AGGS
    for value in outer_sums([send_ref[2 * count :]], gz):
        for c in range(value.shape[0] // AGGS):
            out_ref[:, at * WIDE : (at + 1) * WIDE] = value[c * AGGS : (c + 1) * AGGS]
            at += 1


def final_kernel(group_size, own_ref, *refs):
    received, out_hbm, out_ref, sems = refs[:-3], refs[-3], refs[-2], refs[-1]
    gz = lax.axis_index("gz")
    rows_each = AGGS // group_size
    count = AGGS * AGGS // group_size
    copies = []

    def send_out(face):
        part = pl.ds(face * AGGS * WIDE, AGGS * WIDE)
        copies.append(pltpu.make_async_copy(out_ref.at[:, part], out_hbm.at[:, part], sems.at[face]))
        copies[-1].start()

    brick = iota((AGGS, LANES), 0) // rows_each
    for c in range(AGGS):
        for h in range(2):
            at = slice((2 * c + h) * LANES, (2 * c + h + 1) * LANES)
            value = own_ref[:, at]
            for shift, ref in enumerate(received, 1):
                part = ref[h * count + c * rows_each : h * count + (c + 1) * rows_each]
                theirs = lax.rem(gz - shift + group_size, group_size)
                value = jnp.where(brick == theirs, rows_of([part] * group_size), value)
            out_ref[:, at] = value
    send_out(0)
    at = AGGS
    for value in outer_sums([ref[2 * count :] for ref in received], gz):
        for c in range(value.shape[0] // AGGS):
            cut = slice(at * WIDE, (at + 1) * WIDE)
            out_ref[:, cut] = own_ref[:, cut] + value[c * AGGS : (c + 1) * AGGS]
            at += 1
            if at % AGGS == 0:
                send_out(at // AGGS - 1)
    for copy in copies:
        copy.wait()


def rotation(count, step):
    return [(i, (i + step) % count) for i in range(count)]


def shards(fine_blocks, prolong, agg_map, owner_map):
    bx, by, bz = fine_blocks.shape[:3]
    columns = bx * by
    group_size = lax.axis_size("gz")
    fine = fine_blocks.transpose(0, 1, 3, 2, 4).reshape(columns * FACES, bz, 32, LANES)
    fine = fine.transpose(0, 2, 1, 3).reshape(columns * FACES, 32 * bz, LANES)
    base = prolong.reshape(columns, bz, 8, LANES).transpose(0, 2, 1, 3).reshape(columns, 8 * bz, LANES)
    halos = []
    for axis in ("gx", "gy", "gz"):
        count = lax.axis_size(axis)
        halos.append(lax.ppermute(base, axis, rotation(count, 1)))
        if axis != "gz" or count > 2:
            halos.append(lax.ppermute(base, axis, rotation(count, -1)))
    params = pltpu.CompilerParams(vmem_limit_bytes=32 * 1024 * 1024)
    shape = jax.ShapeDtypeStruct
    outer, inner, labels = pl.pallas_call(
        functools.partial(local_kernel, (bx, by, bz), group_size),
        out_shape=[shape((10, DOF, WIDE), BF16), shape((AGGS * AGGS, WIDE), F32), shape((8, LANES), F32)],
        in_specs=[HBM] * 4,
        out_specs=[VMEM] * 3,
        scratch_shapes=[
            pltpu.VMEM(agg_map.shape, jnp.int32),
            pltpu.VMEM(owner_map.shape, jnp.int32),
            pltpu.VMEM(base.shape, F32),
            pltpu.VMEM(fine.shape, F32),
            pltpu.VMEM((columns * FACES, DOF, WIDE), BF16),
            pltpu.SemaphoreType.DMA((3 + columns,)),
        ],
        compiler_params=params,
        cost_estimate=pl.CostEstimate(flops=int(2e9), bytes_accessed=int(4e6), transcendentals=0),
    )(*(pltpu.with_memory_space_constraint(a, pltpu.HBM) for a in (agg_map, owner_map, base, fine)))
    size = 2 * AGGS * AGGS // group_size + 5 * CDOF + 8
    sends = pl.pallas_call(
        functools.partial(outer_kernel, group_size, len(halos)),
        out_shape=[shape((size, LANES), F32)] * (group_size - 1),
        in_specs=[VMEM] * (3 + len(halos)),
        out_specs=[VMEM] * (group_size - 1),
        compiler_params=params,
    )(outer, inner, labels, *halos)
    received = [
        lax.ppermute(send, "gz", rotation(group_size, shift)) for shift, send in enumerate(sends, 1)
    ]
    full = shape((AGGS, FACES * AGGS * CDOF * CDOF), F32)
    own = pl.pallas_call(
        functools.partial(own_kernel, group_size),
        out_shape=full,
        in_specs=[VMEM, VMEM],
        out_specs=VMEM,
        compiler_params=params,
        cost_estimate=pl.CostEstimate(flops=int(1e9), bytes_accessed=int(2e6), transcendentals=0),
    )(inner, sends[0])
    out = pl.pallas_call(
        functools.partial(final_kernel, group_size),
        out_shape=full,
        in_specs=[VMEM] * group_size,
        out_specs=HBM,
        scratch_shapes=[pltpu.VMEM(full.shape, F32), pltpu.SemaphoreType.DMA((FACES,))],
        compiler_params=params,
    )(own, *received)
    return out[None, None]


def solution(mesh):
    placed = (P("gx", "gy", "gz", None, None), P("gx", "gy", "gz", None), P(), P("gx", "gy", "gz"))
    return jax.shard_map(
        shards, mesh=mesh, in_specs=placed, out_specs=P("gx", "gy", "gz", None), check_vma=False
    )
```

time: 85.5 us -> 20 us (0.23)
  the two profiles are of different devices: /device:TPU:10 before, /device:TPU:0 now
where the time goes in v2:
time: 20 us; the launch traced here: 19.8 us
  starting transfers between devices  7.65 us (38%)
  Pallas kernels  7.38 us (37%)
  waiting for transfers between devices  4.75 us (24%)
    pallas_call x1, Pallas kernels, shards(): pl.pallas_call(functools.partial(local_kernel, (bx, by, bz), group_size),...  4.29 us
    ppermute x2, starting transfers between devices, shards(): halos.append(lax.ppermute(base, axis, rotation(count, -1)))  3.97 us
    ppermute x1, waiting for transfers between devices, shards(): lax.ppermute(send, 'gz', rotation(group_size, shift))  3.29 us
    ppermute x3, starting transfers between devices, shards(): halos.append(lax.ppermute(base, axis, rotation(count, 1)))  3.11 us
    ppermute x3, waiting for transfers between devices, shards(): halos.append(lax.ppermute(base, axis, rotation(count, 1)))  1.45 us
    pallas_call x1, Pallas kernels, shards(): pl.pallas_call(functools.partial(final_kernel, group_size), out_shape=ful...  1.3 us
    pallas_call x1, Pallas kernels, shards(): pl.pallas_call(functools.partial(outer_kernel, group_size, len(halos)), o...  1.2 us
    pallas_call x1, Pallas kernels, shards(): pl.pallas_call(functools.partial(own_kernel, group_size), out_shape=full,...  0.6 us
  transfers between devices with their start and end apart: 6, of which 2 were waited for; matrix products, arithmetic and copies ran while one was open for 0% of the time, Pallas kernels for 25%

profile of v2, /device:TPU:0, one launch (start us, length us, event | category | flops | bytes accessed | tf_op | source)
XLA Modules:
  0.0 19.8 jit_solution(6029087854458879793)
XLA Ops:
  0.0 3.0 %collective-permute-start.4 = (f32[4,32,128]{2,1,0:T(8,128)}, f32[4,32,128]{2,1,0:T(8,128)S(1)}, u32[]{:S(2)}, u32[]{:S(2)}) collective-permute-start(f32[4,32,128]{2,1,0:T(8,128)} %bitcast.14), channel_id=1, source_target_pairs={{0,1},{1,0},{2,3},{3,2},{4,5},{5,4},{6,7},{7,6},{8,9},{9,8},{10,11... | collective-permute-start | bytes 196616 | tf_op jit(solution)/shard_map/ppermute | solution.py:361
  3.0 3.6 %collective-permute-start.3 = (f32[4,32,128]{2,1,0:T(8,128)}, f32[4,32,128]{2,1,0:T(8,128)S(1)}, u32[]{:S(2)}, u32[]{:S(2)}) collective-permute-start(f32[4,32,128]{2,1,0:T(8,128)} %bitcast.15), channel_id=1, source_target_pairs={{0,6},{2,0},{4,2},{6,4},{1,7},{3,1},{5,3},{7,5},{8,14},{10,8},{12,... | collective-permute-start | bytes 196616 | tf_op jit(solution)/shard_map/ppermute | solution.py:363
  6.6 0.0 collective-permute-start.2
  6.6 0.4 %collective-permute-start.1 = (f32[4,32,128]{2,1,0:T(8,128)}, f32[4,32,128]{2,1,0:T(8,128)S(1)}, u32[]{:S(2)}, u32[]{:S(2)}) collective-permute-start(f32[4,32,128]{2,1,0:T(8,128)} %bitcast.17), channel_id=1, source_target_pairs={{0,24},{8,0},{16,8},{24,16},{1,25},{9,1},{17,9},{25,17},{2,26},{10... | collective-permute-start | bytes 196616 | tf_op jit(solution)/shard_map/ppermute | solution.py:363
  6.9 0.1 collective-permute-start
  7.1 4.3 %shard_map.46 = (bf16[10,64,256]{2,1,0:T(8,128)(2,1)S(1)}, f32[64,256]{1,0:T(8,128)S(1)}, f32[8,128]{1,0:T(8,128)S(1)}) custom-call(s32[8,8,8]{2,1,0:T(8,128)} %agg_hbm.1, s32[1,1,8]{2,1,0:T(1,128)} %owner_hbm.1, f32[4,32,128]{2,1,0:T(8,128)} %bitcast.19, f32[28,128,128]{2,1,0:T(8,128)} %bitcast.13), custom_call_target="tpu_custom_call" | custom-call | flops 2000000000 | bytes 4000000 | tf_op jit(solution)/shard_map/pallas_call | solution.py:366
  11.4 0.0 collective-permute-done.4.refs_4_
  11.4 0.0 collective-permute-done.3.refs_3_
  11.4 1.4 %collective-permute-done.2.refs_2_ = f32[4,32,128]{2,1,0:T(8,128)S(1)} collective-permute-done((f32[4,32,128]{2,1,0:T(8,128)}, f32[4,32,128]{2,1,0:T(8,128)S(1)}, u32[]{:S(2)}, u32[]{:S(2)}) %collective-permute-start.2) | collective-permute-done | bytes 65568 | tf_op jit(solution)/shard_map/ppermute | solution.py:361
  12.8 0.0 collective-permute-done.1.refs_1_
  12.8 0.0 collective-permute-done.refs_0_
  12.9 1.2 %shard_map.47.send_ref = f32[152,128]{1,0:T(8,128)S(1)} custom-call(bf16[10,64,256]{2,1,0:T(8,128)(2,1)S(1)} %get-tuple-element.9.outer_ref, f32[64,256]{1,0:T(8,128)S(1)} %get-tuple-element.8.inner_ref, f32[8,128]{1,0:T(8,128)S(1)} %get-tuple-element.10.label_ref, f32[4,32,128]{2,1,0:T(8,128)S(1)} %collective-permute-done.refs_0_, ...), custom_call_target="tpu_custom_call" | custom-call | tf_op jit(solution)/shard_map/pallas_call | solution.py:383
  14.1 0.6 %collective-permute-start.5 = (f32[152,128]{1,0:T(8,128)S(1)}, f32[152,128]{1,0:T(8,128)S(1)}, u32[]{:S(2)}, u32[]{:S(2)}) collective-permute-start(f32[152,128]{1,0:T(8,128)S(1)} %shard_map.47.send_ref), channel_id=1, source_target_pairs={{0,1},{1,0},{2,3},{3,2},{4,5},{5,4},{6,7},{7,6},{8,9},{9,8},{10,11... | collective-permute-start | bytes 233480 | tf_op jit(solution)/shard_map/ppermute | solution.py:391
  14.6 0.6 %shard_map.48.own_ref = f32[8,14336]{1,0:T(8,128)S(1)} custom-call(f32[64,256]{1,0:T(8,128)S(1)} %get-tuple-element.8.inner_ref, f32[152,128]{1,0:T(8,128)S(1)} %shard_map.47.send_ref), custom_call_target="tpu_custom_call" | custom-call | flops 1000000000 | bytes 2000000 | tf_op jit(solution)/shard_map/pallas_call | solution.py:394
  15.2 3.3 %collective-permute-done.5.refs_0_ = f32[152,128]{1,0:T(8,128)S(1)} collective-permute-done((f32[152,128]{1,0:T(8,128)S(1)}, f32[152,128]{1,0:T(8,128)S(1)}, u32[]{:S(2)}, u32[]{:S(2)}) %collective-permute-start.5) | collective-permute-done | bytes 77856 | tf_op jit(solution)/shard_map/ppermute | solution.py:391
  18.5 1.3 %shard_map.49 = f32[8,14336]{1,0:T(8,128)} custom-call(f32[8,14336]{1,0:T(8,128)S(1)} %shard_map.48.own_ref, f32[152,128]{1,0:T(8,128)S(1)} %collective-permute-done.5.refs_0_), custom_call_target="tpu_custom_call" | custom-call | tf_op jit(solution)/shard_map/pallas_call | solution.py:402
Async XLA Ops:
  0.0 11.4 %collective-permute-start.4 = (f32[4,32,128]{2,1,0:T(8,128)}, f32[4,32,128]{2,1,0:T(8,128)S(1)}, u32[]{:S(2)}, u32[]{:S(2)}) collective-permute-start(f32[4,32,128]{2,1,0:T(8,128)} %bitcast.14), channel_id=1, source_target_pairs={{0,1},{1,0},{2,3},{3,2},{4,5},{5,4},{6,7},{7,6},{8,9},{9,8},{10,11... | collective-permute-start | bytes 196616 | tf_op jit(solution)/shard_map/ppermute | solution.py:361
  3.0 8.4 %collective-permute-start.3 = (f32[4,32,128]{2,1,0:T(8,128)}, f32[4,32,128]{2,1,0:T(8,128)S(1)}, u32[]{:S(2)}, u32[]{:S(2)}) collective-permute-start(f32[4,32,128]{2,1,0:T(8,128)} %bitcast.15), channel_id=1, source_target_pairs={{0,6},{2,0},{4,2},{6,4},{1,7},{3,1},{5,3},{7,5},{8,14},{10,8},{12,... | collective-permute-start | bytes 196616 | tf_op jit(solution)/shard_map/ppermute | solution.py:363
  6.6 6.3 %collective-permute-start.2 = (f32[4,32,128]{2,1,0:T(8,128)}, f32[4,32,128]{2,1,0:T(8,128)S(1)}, u32[]{:S(2)}, u32[]{:S(2)}) collective-permute-start(f32[4,32,128]{2,1,0:T(8,128)} %bitcast.16), channel_id=1, source_target_pairs={{0,2},{2,4},{4,6},{6,0},{1,3},{3,5},{5,7},{7,1},{8,10},{10,12},{12... | collective-permute-start | bytes 196616 | tf_op jit(solution)/shard_map/ppermute | solution.py:361
  6.6 6.3 %collective-permute-start.1 = (f32[4,32,128]{2,1,0:T(8,128)}, f32[4,32,128]{2,1,0:T(8,128)S(1)}, u32[]{:S(2)}, u32[]{:S(2)}) collective-permute-start(f32[4,32,128]{2,1,0:T(8,128)} %bitcast.17), channel_id=1, source_target_pairs={{0,24},{8,0},{16,8},{24,16},{1,25},{9,1},{17,9},{25,17},{2,26},{10... | collective-permute-start | bytes 196616 | tf_op jit(solution)/shard_map/ppermute | solution.py:363
  6.9 5.9 %collective-permute-start = (f32[4,32,128]{2,1,0:T(8,128)}, f32[4,32,128]{2,1,0:T(8,128)S(1)}, u32[]{:S(2)}, u32[]{:S(2)}) collective-permute-start(f32[4,32,128]{2,1,0:T(8,128)} %bitcast.18), channel_id=1, source_target_pairs={{0,8},{8,16},{16,24},{24,0},{1,9},{9,17},{17,25},{25,1},{2,10},{10... | collective-permute-start | bytes 196616 | tf_op jit(solution)/shard_map/ppermute | solution.py:361
  14.1 4.5 %collective-permute-start.5 = (f32[152,128]{1,0:T(8,128)S(1)}, f32[152,128]{1,0:T(8,128)S(1)}, u32[]{:S(2)}, u32[]{:S(2)}) collective-permute-start(f32[152,128]{1,0:T(8,128)S(1)} %shard_map.47.send_ref), channel_id=1, source_target_pairs={{0,1},{1,0},{2,3},{3,2},{4,5},{5,4},{6,7},{7,6},{8,9},{9,8},{10,11... | collective-permute-start | bytes 233480 | tf_op jit(solution)/shard_map/ppermute | solution.py:391

commit v3 on v2

--- a/solution.py
+++ b/solution.py
@@ -99,25 +99,24 @@
     return ones_where(iota((count, LANES), 0) + base == labels)
 
 
-def local_kernel(shape, group_size, agg_hbm, owner_hbm, prolong_hbm, fine_hbm, outer_ref, inner_ref, label_ref,
-                 agg_ref, owner_ref, prolong_ref, fine_ref, rows_scr, sems):
+def tick_kernel(out_ref):
+    out_ref[...] = jnp.ones(out_ref.shape, F32)
+
+
+def local_kernel(shape, group_size, agg_hbm, owner_hbm, prolong_ref, fine_ref, tick_ref, outer_ref, inner_ref, label_ref,
+                 agg_ref, owner_ref, rows_scr, sems):
     bx, by, bz = shape
     columns = bx * by
     rows_each = AGGS // group_size
     copies = [
-        pltpu.make_async_copy(prolong_hbm, prolong_ref, sems.at[0]),
-        pltpu.make_async_copy(agg_hbm, agg_ref, sems.at[1]),
-        pltpu.make_async_copy(owner_hbm, owner_ref, sems.at[2]),
+        pltpu.make_async_copy(agg_hbm, agg_ref, sems.at[0]),
+        pltpu.make_async_copy(owner_hbm, owner_ref, sems.at[1]),
     ]
-    for i in range(columns):
-        part = pl.ds(i * FACES, FACES)
-        copies.append(pltpu.make_async_copy(fine_hbm.at[part], fine_ref.at[part], sems.at[3 + i]))
     for copy in copies:
         copy.start()
     gx, gy, gz = lax.axis_index("gx"), lax.axis_index("gy"), lax.axis_index("gz")
     nx, ny, nz = agg_ref.shape
 
-    copies[0].wait()
     lane = iota((32, LANES), 1)
     sub = iota((32, LANES), 0) % 4
     p0, p1 = iota((LANES, LANES), 0), iota((LANES, LANES), 1)
@@ -139,7 +138,6 @@
 
     wide_lane = iota((4, CDOF, WIDE), 2) % LANES
     for xy in range(columns):
-        copies[3 + xy].wait()
         high = lefts[xy * WIDE : xy * WIDE + LANES]
         low = lefts[xy * WIDE + LANES : (xy + 1) * WIDE]
         left = rows_of([lanes_of([high, high]), lanes_of([low, jnp.zeros_like(low)])])
@@ -166,8 +164,8 @@
         outer_ref[8, at] = rows_scr[xy * FACES + 5, :CDOF]
         outer_ref[9, at] = rows_scr[xy * FACES + 6, DOF - CDOF :]
 
+    copies[0].wait()
     copies[1].wait()
-    copies[2].wait()
     aggs = (agg_ref[...] + 1).reshape(nx * ny, nz).astype(F32).astype(BF16)
     width = 5 * LANES
     z_row, z_lane = iota((nz, width), 0), iota((nz, width), 1)
@@ -258,12 +256,15 @@
 
 def outer_kernel(group_size, links, outer_ref, inner_ref, label_ref, *refs):
     halos, sends = refs[:links], refs[links:]
-    low_x, high_x, low_y, high_y = halos[:4]
     low_z, high_z = halos[4], halos[-1]
     gz = lax.axis_index("gz")
-    sources = ((low_x, 2), (low_x, 3), (high_x, 0), (high_x, 1), (low_y, 1), (low_y, 3), (high_y, 0), (high_y, 2))
-    picked = dot(column_picker(), lanes_of([h for ref, xy in sources for h in split(ref[xy])]))
-    picked = [picked[:, i * WIDE : (i + 1) * WIDE] for i in range(len(sources))]
+    values = []
+    for axis, (even, odd), low, high in (("gx", halos[:2], (2, 3), (0, 1)), ("gy", halos[2:4], (1, 3), (0, 2))):
+        second = lax.rem(lax.axis_index(axis), 2) == 1
+        values += [jnp.where(second, even[xy], odd[xy]) for xy in low]
+        values += [jnp.where(second, odd[xy], even[xy]) for xy in high]
+    picked = dot(column_picker(), lanes_of([h for value in values for h in split(value)]))
+    picked = [picked[:, i * WIDE : (i + 1) * WIDE] for i in range(len(values))]
     for ref, z in ((low_z, 3), (high_z, 0)):
         picked.append(dot(layer_picker(z), lanes_of(split(ref[...].reshape(LANES, LANES)))))
     factors = prolong_weights(picked)
@@ -344,6 +345,19 @@
         copy.wait()
 
 
+def matching(sizes, along, first):
+    def partner(place):
+        i = (place[along] - first) ^ 1
+        moved = list(place)
+        if 0 <= i + first < sizes[along] and place[along] >= first:
+            moved[along] = i + first
+        elif place[1 - along] ^ 1 < sizes[1 - along]:
+            moved[1 - along] = place[1 - along] ^ 1
+        return moved[0] * sizes[1] + moved[1]
+
+    return [(x * sizes[1] + y, partner((x, y))) for x in range(sizes[0]) for y in range(sizes[1])]
+
+
 def rotation(count, step):
     return [(i, (i + step) % count) for i in range(count)]
 
@@ -355,30 +369,37 @@
     fine = fine_blocks.transpose(0, 1, 3, 2, 4).reshape(columns * FACES, bz, 32, LANES)
     fine = fine.transpose(0, 2, 1, 3).reshape(columns * FACES, 32 * bz, LANES)
     base = prolong.reshape(columns, bz, 8, LANES).transpose(0, 2, 1, 3).reshape(columns, 8 * bz, LANES)
-    halos = []
-    for axis in ("gx", "gy", "gz"):
-        count = lax.axis_size(axis)
-        halos.append(lax.ppermute(base, axis, rotation(count, 1)))
-        if axis != "gz" or count > 2:
-            halos.append(lax.ppermute(base, axis, rotation(count, -1)))
+    tick = pl.pallas_call(
+        tick_kernel,
+        out_shape=pltpu.VMEM((8, LANES), F32),
+        out_specs=VMEM,
+        cost_estimate=pl.CostEstimate(flops=int(5e9), bytes_accessed=int(5e7), transcendentals=0),
+    )()
+    sizes = lax.axis_size("gx"), lax.axis_size("gy")
+    layers = [lax.ppermute(base, "gz", rotation(group_size, step)) for step in ((1, -1) if group_size > 2 else (1,))]
+    halos = [
+        lax.ppermute(base, ("gx", "gy"), matching(sizes, along, first)) for along in range(2) for first in range(2)
+    ] + layers
     params = pltpu.CompilerParams(vmem_limit_bytes=32 * 1024 * 1024)
     shape = jax.ShapeDtypeStruct
     outer, inner, labels = pl.pallas_call(
         functools.partial(local_kernel, (bx, by, bz), group_size),
         out_shape=[shape((10, DOF, WIDE), BF16), shape((AGGS * AGGS, WIDE), F32), shape((8, LANES), F32)],
-        in_specs=[HBM] * 4,
+        in_specs=[HBM] * 2 + [VMEM] * 3,
         out_specs=[VMEM] * 3,
         scratch_shapes=[
             pltpu.VMEM(agg_map.shape, jnp.int32),
             pltpu.VMEM(owner_map.shape, jnp.int32),
-            pltpu.VMEM(base.shape, F32),
-            pltpu.VMEM(fine.shape, F32),
             pltpu.VMEM((columns * FACES, DOF, WIDE), BF16),
-            pltpu.SemaphoreType.DMA((3 + columns,)),
+            pltpu.SemaphoreType.DMA((2,)),
         ],
         compiler_params=params,
         cost_estimate=pl.CostEstimate(flops=int(2e9), bytes_accessed=int(4e6), transcendentals=0),
-    )(*(pltpu.with_memory_space_constraint(a, pltpu.HBM) for a in (agg_map, owner_map, base, fine)))
+    )(
+        *(pltpu.with_memory_space_constraint(a, pltpu.HBM) for a in (agg_map, owner_map)),
+        *(pltpu.with_memory_space_constraint(a, pltpu.VMEM) for a in (base, fine)),
+        tick,
+    )
     size = 2 * AGGS * AGGS // group_size + 5 * CDOF + 8
     sends = pl.pallas_call(
         functools.partial(outer_kernel, group_size, len(halos)),

time: 20 us -> 17.7 us (0.89)
  Pallas kernels: 7.38 us -> 5.7 us
  waiting for transfers between devices: 4.75 us -> 3.52 us
  starting transfers between devices: 7.65 us -> 8.3 us
    pallas_call x1, Pallas kernels: 4.29 us -> 2.6 us  [shards(): pl.pallas_call(functools.partial(local_kernel, (bx, by, bz), group_size),...]
    ppermute x5, waiting for transfers between devices: 1.46 us -> 0.23 us  [the longest x4 0.23 us: shards(): lax.ppermute(base, ('gx', 'gy'), matching(sizes, along, first))]
    ppermute x5, starting transfers between devices: 7.08 us -> 7.73 us  [the longest x4 4.76 us: shards(): lax.ppermute(base, ('gx', 'gy'), matching(sizes, along, first))]
  transfers between devices with their start and end apart: 6 -> 6, of which waited for: 2 -> 2; matrix products, arithmetic and copies ran while one was open for 0% -> 0% of each run, Pallas kernels for 25% -> 18%
where the time goes in v3:
time: 17.7 us; the launch traced here: 17.6 us
  starting transfers between devices  8.3 us (47%)
  Pallas kernels  5.7 us (32%)
  waiting for transfers between devices  3.52 us (20%)
    ppermute x4, starting transfers between devices, shards(): lax.ppermute(base, ('gx', 'gy'), matching(sizes, along, first))  4.76 us
    ppermute x1, waiting for transfers between devices, shards(): lax.ppermute(send, 'gz', rotation(group_size, shift))  3.29 us
    ppermute x1, starting transfers between devices, shards(): lax.ppermute(base, 'gz', rotation(group_size, step))  2.97 us
    pallas_call x1, Pallas kernels, shards(): pl.pallas_call(functools.partial(local_kernel, (bx, by, bz), group_size),...  2.6 us
    pallas_call x1, Pallas kernels, shards(): pl.pallas_call(functools.partial(final_kernel, group_size), out_shape=ful...  1.3 us
    pallas_call x1, Pallas kernels, shards(): pl.pallas_call(functools.partial(outer_kernel, group_size, len(halos)), o...  1.2 us
    pallas_call x1, Pallas kernels, shards(): pl.pallas_call(functools.partial(own_kernel, group_size), out_shape=full,...  0.6 us
    ppermute x1, starting transfers between devices, shards(): lax.ppermute(send, 'gz', rotation(group_size, shift))  0.57 us
  transfers between devices with their start and end apart: 6, of which 2 were waited for; matrix products, arithmetic and copies ran while one was open for 0% of the time, Pallas kernels for 18%

profile of v3, /device:TPU:0, one launch (start us, length us, event | category | flops | bytes accessed | tf_op | source)
XLA Modules:
  0.0 17.6 jit_solution(14760592351274728517)
XLA Ops:
  0.0 0.0 copy-start
  0.0 0.0 copy-start.1
  0.0 3.0 %collective-permute-start.4 = (f32[4,32,128]{2,1,0:T(8,128)}, f32[4,32,128]{2,1,0:T(8,128)S(1)}, u32[]{:S(2)}, u32[]{:S(2)}) collective-permute-start(f32[4,32,128]{2,1,0:T(8,128)} %bitcast.14), channel_id=1, source_target_pairs={{0,1},{1,0},{2,3},{3,2},{4,5},{5,4},{6,7},{7,6},{8,9},{9,8},{10,11... | collective-permute-start | bytes 196616 | tf_op jit(solution)/shard_map/ppermute | solution.py:379
  3.0 0.0 collective-permute-start.3
  3.0 3.1 %collective-permute-start.2 = (f32[4,32,128]{2,1,0:T(8,128)}, f32[4,32,128]{2,1,0:T(8,128)S(1)}, u32[]{:S(2)}, u32[]{:S(2)}) collective-permute-start(f32[4,32,128]{2,1,0:T(8,128)} %bitcast.16), channel_id=1, source_target_pairs={{0,2},{2,0},{4,6},{6,4},{8,10},{10,8},{12,14},{14,12},{16,18},{18,... | collective-permute-start | bytes 196616 | tf_op jit(solution)/shard_map/ppermute | solution.py:381
  6.1 0.0 collective-permute-start.1
  6.2 1.6 %collective-permute-start = (f32[4,32,128]{2,1,0:T(8,128)}, f32[4,32,128]{2,1,0:T(8,128)S(1)}, u32[]{:S(2)}, u32[]{:S(2)}) collective-permute-start(f32[4,32,128]{2,1,0:T(8,128)} %bitcast.18), channel_id=1, source_target_pairs={{0,8},{2,10},{4,12},{6,14},{8,0},{10,2},{12,4},{14,6},{16,24},{18,... | collective-permute-start | bytes 196616 | tf_op jit(solution)/shard_map/ppermute | solution.py:381
  7.7 0.0 copy-done
  7.7 0.0 copy-done.1
  7.7 2.6 %shard_map.47 = (bf16[10,64,256]{2,1,0:T(8,128)(2,1)S(1)}, f32[64,256]{1,0:T(8,128)S(1)}, f32[8,128]{1,0:T(8,128)S(1)}) custom-call(s32[8,8,8]{2,1,0:T(8,128)} %agg_hbm.1, s32[1,1,8]{2,1,0:T(1,128)} %owner_hbm.1, f32[4,32,128]{2,1,0:T(8,128)S(1)} %bitcast.19, f32[28,128,128]{2,1,0:T(8,128)S(1)} %bitcast.13, f32[8,128]{1,0:T(8,128)S(1)} %shard_map.46.tick_ref), custom_call_target="tpu_custom_call" | custom-call | flops 2000000000 | bytes 4000000 | tf_op jit(solution)/shard_map/pallas_call | solution.py:385
  10.3 0.0 collective-permute-done.4.refs_4_
  10.4 0.0 collective-permute-done.3.refs_3_
  10.4 0.0 collective-permute-done.2.refs_2_
  10.4 0.2 %collective-permute-done.1.refs_1_ = f32[4,32,128]{2,1,0:T(8,128)S(1)} collective-permute-done((f32[4,32,128]{2,1,0:T(8,128)}, f32[4,32,128]{2,1,0:T(8,128)S(1)}, u32[]{:S(2)}, u32[]{:S(2)}) %collective-permute-start.1) | collective-permute-done | bytes 65568 | tf_op jit(solution)/shard_map/ppermute | solution.py:381
  10.6 0.0 collective-permute-done.refs_0_
  10.6 1.2 %shard_map.48.send_ref = f32[152,128]{1,0:T(8,128)S(1)} custom-call(bf16[10,64,256]{2,1,0:T(8,128)(2,1)S(1)} %get-tuple-element.9.outer_ref, f32[64,256]{1,0:T(8,128)S(1)} %get-tuple-element.8.inner_ref, f32[8,128]{1,0:T(8,128)S(1)} %get-tuple-element.10.label_ref, f32[4,32,128]{2,1,0:T(8,128)S(1)} %collective-permute-done.refs_0_, ...), custom_call_target="tpu_custom_call" | custom-call | tf_op jit(solution)/shard_map/pallas_call | solution.py:404
  11.8 0.6 %collective-permute-start.5 = (f32[152,128]{1,0:T(8,128)S(1)}, f32[152,128]{1,0:T(8,128)S(1)}, u32[]{:S(2)}, u32[]{:S(2)}) collective-permute-start(f32[152,128]{1,0:T(8,128)S(1)} %shard_map.48.send_ref), channel_id=1, source_target_pairs={{0,1},{1,0},{2,3},{3,2},{4,5},{5,4},{6,7},{7,6},{8,9},{9,8},{10,11... | collective-permute-start | bytes 233480 | tf_op jit(solution)/shard_map/ppermute | solution.py:412
  12.4 0.6 %shard_map.49.own_ref = f32[8,14336]{1,0:T(8,128)S(1)} custom-call(f32[64,256]{1,0:T(8,128)S(1)} %get-tuple-element.8.inner_ref, f32[152,128]{1,0:T(8,128)S(1)} %shard_map.48.send_ref), custom_call_target="tpu_custom_call" | custom-call | flops 1000000000 | bytes 2000000 | tf_op jit(solution)/shard_map/pallas_call | solution.py:415
  13.0 3.3 %collective-permute-done.5.refs_0_ = f32[152,128]{1,0:T(8,128)S(1)} collective-permute-done((f32[152,128]{1,0:T(8,128)S(1)}, f32[152,128]{1,0:T(8,128)S(1)}, u32[]{:S(2)}, u32[]{:S(2)}) %collective-permute-start.5) | collective-permute-done | bytes 77856 | tf_op jit(solution)/shard_map/ppermute | solution.py:412
  16.3 1.3 %shard_map.50 = f32[8,14336]{1,0:T(8,128)} custom-call(f32[8,14336]{1,0:T(8,128)S(1)} %shard_map.49.own_ref, f32[152,128]{1,0:T(8,128)S(1)} %collective-permute-done.5.refs_0_), custom_call_target="tpu_custom_call" | custom-call | tf_op jit(solution)/shard_map/pallas_call | solution.py:423
  (1 shorter events, 0.0 us)
Async XLA Ops:
  0.0 7.7 %copy-start = (f32[2,2,4,7,4096]{4,2,3,1,0:T(4,128)S(1)}, f32[2,2,4,7,4096]{4,2,3,1,0:T(4,128)}, u32[]{:S(2)}) copy-start(f32[2,2,4,7,4096]{4,2,3,1,0:T(4,128)} %param.4) | copy-start | bytes 5505028
  0.0 7.7 %copy-start.1 = (f32[2,2,4,1024]{3,2,1,0:T(4,128)S(1)}, f32[2,2,4,1024]{3,2,1,0:T(4,128)}, u32[]{:S(2)}) copy-start(f32[2,2,4,1024]{3,2,1,0:T(4,128)} %param.5) | copy-start | bytes 196612
  0.0 10.3 %collective-permute-start.4 = (f32[4,32,128]{2,1,0:T(8,128)}, f32[4,32,128]{2,1,0:T(8,128)S(1)}, u32[]{:S(2)}, u32[]{:S(2)}) collective-permute-start(f32[4,32,128]{2,1,0:T(8,128)} %bitcast.14), channel_id=1, source_target_pairs={{0,1},{1,0},{2,3},{3,2},{4,5},{5,4},{6,7},{7,6},{8,9},{9,8},{10,11... | collective-permute-start | bytes 196616 | tf_op jit(solution)/shard_map/ppermute | solution.py:379
  3.0 7.4 %collective-permute-start.3 = (f32[4,32,128]{2,1,0:T(8,128)}, f32[4,32,128]{2,1,0:T(8,128)S(1)}, u32[]{:S(2)}, u32[]{:S(2)}) collective-permute-start(f32[4,32,128]{2,1,0:T(8,128)} %bitcast.15), channel_id=1, source_target_pairs={{0,8},{2,4},{4,2},{6,14},{8,0},{10,12},{12,10},{14,6},{16,24},{18,... | collective-permute-start | bytes 196616 | tf_op jit(solution)/shard_map/ppermute | solution.py:381
  3.0 7.4 %collective-permute-start.2 = (f32[4,32,128]{2,1,0:T(8,128)}, f32[4,32,128]{2,1,0:T(8,128)S(1)}, u32[]{:S(2)}, u32[]{:S(2)}) collective-permute-start(f32[4,32,128]{2,1,0:T(8,128)} %bitcast.16), channel_id=1, source_target_pairs={{0,2},{2,0},{4,6},{6,4},{8,10},{10,8},{12,14},{14,12},{16,18},{18,... | collective-permute-start | bytes 196616 | tf_op jit(solution)/shard_map/ppermute | solution.py:381
  6.1 4.5 %collective-permute-start.1 = (f32[4,32,128]{2,1,0:T(8,128)}, f32[4,32,128]{2,1,0:T(8,128)S(1)}, u32[]{:S(2)}, u32[]{:S(2)}) collective-permute-start(f32[4,32,128]{2,1,0:T(8,128)} %bitcast.17), channel_id=1, source_target_pairs={{0,2},{2,0},{4,6},{6,4},{8,16},{10,18},{12,20},{14,22},{16,8},{18,... | collective-permute-start | bytes 196616 | tf_op jit(solution)/shard_map/ppermute | solution.py:381
  6.2 4.4 %collective-permute-start = (f32[4,32,128]{2,1,0:T(8,128)}, f32[4,32,128]{2,1,0:T(8,128)S(1)}, u32[]{:S(2)}, u32[]{:S(2)}) collective-permute-start(f32[4,32,128]{2,1,0:T(8,128)} %bitcast.18), channel_id=1, source_target_pairs={{0,8},{2,10},{4,12},{6,14},{8,0},{10,2},{12,4},{14,6},{16,24},{18,... | collective-permute-start | bytes 196616 | tf_op jit(solution)/shard_map/ppermute | solution.py:381
  11.8 4.5 %collective-permute-start.5 = (f32[152,128]{1,0:T(8,128)S(1)}, f32[152,128]{1,0:T(8,128)S(1)}, u32[]{:S(2)}, u32[]{:S(2)}) collective-permute-start(f32[152,128]{1,0:T(8,128)S(1)} %shard_map.48.send_ref), channel_id=1, source_target_pairs={{0,1},{1,0},{2,3},{3,2},{4,5},{5,4},{6,7},{7,6},{8,9},{9,8},{10,11... | collective-permute-start | bytes 233480 | tf_op jit(solution)/shard_map/ppermute | solution.py:412

commit v4 on v3

--- a/solution.py
+++ b/solution.py
@@ -255,11 +255,11 @@
 
 
 def outer_kernel(group_size, links, outer_ref, inner_ref, label_ref, *refs):
-    halos, sends = refs[:links], refs[links:]
-    low_z, high_z = halos[4], halos[-1]
+    (odd_y, *layers, even_y, odd_x, even_x), sends = refs[:links], refs[links:]
+    low_z, high_z = layers[0], layers[-1]
     gz = lax.axis_index("gz")
     values = []
-    for axis, (even, odd), low, high in (("gx", halos[:2], (2, 3), (0, 1)), ("gy", halos[2:4], (1, 3), (0, 2))):
+    for axis, even, odd, low, high in (("gx", even_x, odd_x, (2, 3), (0, 1)), ("gy", even_y, odd_y, (1, 3), (0, 2))):
         second = lax.rem(lax.axis_index(axis), 2) == 1
         values += [jnp.where(second, even[xy], odd[xy]) for xy in low]
         values += [jnp.where(second, odd[xy], even[xy]) for xy in high]
@@ -377,9 +377,10 @@
     )()
     sizes = lax.axis_size("gx"), lax.axis_size("gy")
     layers = [lax.ppermute(base, "gz", rotation(group_size, step)) for step in ((1, -1) if group_size > 2 else (1,))]
-    halos = [
+    even_x, odd_x, even_y, odd_y = [
         lax.ppermute(base, ("gx", "gy"), matching(sizes, along, first)) for along in range(2) for first in range(2)
-    ] + layers
+    ]
+    halos = [odd_y, *layers, even_y, odd_x, even_x]
     params = pltpu.CompilerParams(vmem_limit_bytes=32 * 1024 * 1024)
     shape = jax.ShapeDtypeStruct
     outer, inner, labels = pl.pallas_call(

time: 17.7 us -> 15.5 us (0.88)
  waiting for transfers between devices: 3.52 us -> 1.99 us
  starting transfers between devices: 8.3 us -> 7.55 us
    ppermute x1, waiting for transfers between devices: 3.29 us -> 1.97 us  [shards(): lax.ppermute(send, 'gz', rotation(group_size, shift))]
    ppermute x1, starting transfers between devices: 0.57 us -> 1.89 us  [shards(): lax.ppermute(send, 'gz', rotation(group_size, shift))]
    ppermute x1, starting transfers between devices: 2.97 us -> 1.89 us  [shards(): lax.ppermute(base, 'gz', rotation(group_size, step))]
    ppermute x4, starting transfers between devices: 4.76 us -> 3.77 us  [shards(): lax.ppermute(base, ('gx', 'gy'), matching(sizes, along, first))]
    ppermute x4, waiting for transfers between devices: 0.23 us -> 0.01 us  [shards(): lax.ppermute(base, ('gx', 'gy'), matching(sizes, along, first))]
  transfers between devices with their start and end apart: 6 -> 6, of which waited for: 2 -> 1; matrix products, arithmetic and copies ran while one was open for 0% -> 0% of each run, Pallas kernels for 18% -> 21%
where the time goes in v4:
time: 15.5 us; the launch traced here: 15.3 us
  starting transfers between devices  7.55 us (49%)
  Pallas kernels  5.71 us (37%)
  waiting for transfers between devices  1.99 us (13%)
    ppermute x4, starting transfers between devices, shards(): lax.ppermute(base, ('gx', 'gy'), matching(sizes, along, first))  3.77 us
    pallas_call x1, Pallas kernels, shards(): pl.pallas_call(functools.partial(local_kernel, (bx, by, bz), group_size),...  2.6 us
    ppermute x1, waiting for transfers between devices, shards(): lax.ppermute(send, 'gz', rotation(group_size, shift))  1.97 us
    ppermute x1, starting transfers between devices, shards(): lax.ppermute(base, 'gz', rotation(group_size, step))  1.89 us
    ppermute x1, starting transfers between devices, shards(): lax.ppermute(send, 'gz', rotation(group_size, shift))  1.89 us
    pallas_call x1, Pallas kernels, shards(): pl.pallas_call(functools.partial(final_kernel, group_size), out_shape=ful...  1.3 us
    pallas_call x1, Pallas kernels, shards(): pl.pallas_call(functools.partial(outer_kernel, group_size, len(halos)), o...  1.2 us
    pallas_call x1, Pallas kernels, shards(): pl.pallas_call(functools.partial(own_kernel, group_size), out_shape=full,...  0.6 us
  transfers between devices with their start and end apart: 6, of which 1 were waited for; matrix products, arithmetic and copies ran while one was open for 0% of the time, Pallas kernels for 21%

profile of v4, /device:TPU:0, one launch (start us, length us, event | category | flops | bytes accessed | tf_op | source)
XLA Modules:
  0.0 15.3 jit_solution(11698939986058575805)
XLA Ops:
  0.0 0.0 copy-start
  0.0 0.0 copy-start.1
  0.0 0.5 %collective-permute-start.4 = (f32[4,32,128]{2,1,0:T(8,128)}, f32[4,32,128]{2,1,0:T(8,128)S(1)}, u32[]{:S(2)}, u32[]{:S(2)}) collective-permute-start(f32[4,32,128]{2,1,0:T(8,128)} %bitcast.14), channel_id=1, source_target_pairs={{0,8},{2,10},{4,12},{6,14},{8,0},{10,2},{12,4},{14,6},{16,24},{18,... | collective-permute-start | bytes 196616 | tf_op jit(solution)/shard_map/ppermute | solution.py:381
  0.5 2.6 %collective-permute-start.3 = (f32[4,32,128]{2,1,0:T(8,128)}, f32[4,32,128]{2,1,0:T(8,128)S(1)}, u32[]{:S(2)}, u32[]{:S(2)}) collective-permute-start(f32[4,32,128]{2,1,0:T(8,128)} %bitcast.15), channel_id=1, source_target_pairs={{0,2},{2,0},{4,6},{6,4},{8,16},{10,18},{12,20},{14,22},{16,8},{18,... | collective-permute-start | bytes 196616 | tf_op jit(solution)/shard_map/ppermute | solution.py:381
  3.1 0.1 collective-permute-start.2
  3.2 1.9 %collective-permute-start.1 = (f32[4,32,128]{2,1,0:T(8,128)}, f32[4,32,128]{2,1,0:T(8,128)S(1)}, u32[]{:S(2)}, u32[]{:S(2)}) collective-permute-start(f32[4,32,128]{2,1,0:T(8,128)} %bitcast.17), channel_id=1, source_target_pairs={{0,1},{1,0},{2,3},{3,2},{4,5},{5,4},{6,7},{7,6},{8,9},{9,8},{10,11... | collective-permute-start | bytes 196616 | tf_op jit(solution)/shard_map/ppermute | solution.py:379
  5.1 0.6 %collective-permute-start = (f32[4,32,128]{2,1,0:T(8,128)}, f32[4,32,128]{2,1,0:T(8,128)S(1)}, u32[]{:S(2)}, u32[]{:S(2)}) collective-permute-start(f32[4,32,128]{2,1,0:T(8,128)} %bitcast.18), channel_id=1, source_target_pairs={{0,8},{2,4},{4,2},{6,14},{8,0},{10,12},{12,10},{14,6},{16,24},{18,... | collective-permute-start | bytes 196616 | tf_op jit(solution)/shard_map/ppermute | solution.py:381
  5.7 0.0 copy-done
  5.7 0.0 copy-done.1
  5.7 2.6 %shard_map.47 = (bf16[10,64,256]{2,1,0:T(8,128)(2,1)S(1)}, f32[64,256]{1,0:T(8,128)S(1)}, f32[8,128]{1,0:T(8,128)S(1)}) custom-call(s32[8,8,8]{2,1,0:T(8,128)} %agg_hbm.1, s32[1,1,8]{2,1,0:T(1,128)} %owner_hbm.1, f32[4,32,128]{2,1,0:T(8,128)S(1)} %bitcast.19, f32[28,128,128]{2,1,0:T(8,128)S(1)} %bitcast.13, f32[8,128]{1,0:T(8,128)S(1)} %shard_map.46.tick_ref), custom_call_target="tpu_custom_call" | custom-call | flops 2000000000 | bytes 4000000 | tf_op jit(solution)/shard_map/pallas_call | solution.py:386
  8.3 0.0 collective-permute-done.4.refs_4_
  8.3 0.0 collective-permute-done.3.refs_3_
  8.3 0.0 collective-permute-done.2.refs_2_
  8.3 0.0 collective-permute-done.1.refs_1_
  8.3 0.0 collective-permute-done.refs_0_
  8.3 1.2 %shard_map.48.send_ref = f32[152,128]{1,0:T(8,128)S(1)} custom-call(bf16[10,64,256]{2,1,0:T(8,128)(2,1)S(1)} %get-tuple-element.9.outer_ref, f32[64,256]{1,0:T(8,128)S(1)} %get-tuple-element.8.inner_ref, f32[8,128]{1,0:T(8,128)S(1)} %get-tuple-element.10.label_ref, f32[4,32,128]{2,1,0:T(8,128)S(1)} %collective-permute-done.refs_0_, ...), custom_call_target="tpu_custom_call" | custom-call | tf_op jit(solution)/shard_map/pallas_call | solution.py:405
  9.5 1.9 %collective-permute-start.5 = (f32[152,128]{1,0:T(8,128)S(1)}, f32[152,128]{1,0:T(8,128)S(1)}, u32[]{:S(2)}, u32[]{:S(2)}) collective-permute-start(f32[152,128]{1,0:T(8,128)S(1)} %shard_map.48.send_ref), channel_id=1, source_target_pairs={{0,1},{1,0},{2,3},{3,2},{4,5},{5,4},{6,7},{7,6},{8,9},{9,8},{10,11... | collective-permute-start | bytes 233480 | tf_op jit(solution)/shard_map/ppermute | solution.py:413
  11.4 0.6 %shard_map.49.own_ref = f32[8,14336]{1,0:T(8,128)S(1)} custom-call(f32[64,256]{1,0:T(8,128)S(1)} %get-tuple-element.8.inner_ref, f32[152,128]{1,0:T(8,128)S(1)} %shard_map.48.send_ref), custom_call_target="tpu_custom_call" | custom-call | flops 1000000000 | bytes 2000000 | tf_op jit(solution)/shard_map/pallas_call | solution.py:416
  12.0 2.0 %collective-permute-done.5.refs_0_ = f32[152,128]{1,0:T(8,128)S(1)} collective-permute-done((f32[152,128]{1,0:T(8,128)S(1)}, f32[152,128]{1,0:T(8,128)S(1)}, u32[]{:S(2)}, u32[]{:S(2)}) %collective-permute-start.5) | collective-permute-done | bytes 77856 | tf_op jit(solution)/shard_map/ppermute | solution.py:413
  14.0 1.3 %shard_map.50 = f32[8,14336]{1,0:T(8,128)} custom-call(f32[8,14336]{1,0:T(8,128)S(1)} %shard_map.49.own_ref, f32[152,128]{1,0:T(8,128)S(1)} %collective-permute-done.5.refs_0_), custom_call_target="tpu_custom_call" | custom-call | tf_op jit(solution)/shard_map/pallas_call | solution.py:424
  (1 shorter events, 0.0 us)
Async XLA Ops:
  0.0 5.7 %copy-start = (f32[2,2,4,7,4096]{4,2,3,1,0:T(4,128)S(1)}, f32[2,2,4,7,4096]{4,2,3,1,0:T(4,128)}, u32[]{:S(2)}) copy-start(f32[2,2,4,7,4096]{4,2,3,1,0:T(4,128)} %param.4) | copy-start | bytes 5505028
  0.0 5.7 %copy-start.1 = (f32[2,2,4,1024]{3,2,1,0:T(4,128)S(1)}, f32[2,2,4,1024]{3,2,1,0:T(4,128)}, u32[]{:S(2)}) copy-start(f32[2,2,4,1024]{3,2,1,0:T(4,128)} %param.5) | copy-start | bytes 196612
  0.0 8.3 %collective-permute-start.4 = (f32[4,32,128]{2,1,0:T(8,128)}, f32[4,32,128]{2,1,0:T(8,128)S(1)}, u32[]{:S(2)}, u32[]{:S(2)}) collective-permute-start(f32[4,32,128]{2,1,0:T(8,128)} %bitcast.14), channel_id=1, source_target_pairs={{0,8},{2,10},{4,12},{6,14},{8,0},{10,2},{12,4},{14,6},{16,24},{18,... | collective-permute-start | bytes 196616 | tf_op jit(solution)/shard_map/ppermute | solution.py:381
  0.5 7.8 %collective-permute-start.3 = (f32[4,32,128]{2,1,0:T(8,128)}, f32[4,32,128]{2,1,0:T(8,128)S(1)}, u32[]{:S(2)}, u32[]{:S(2)}) collective-permute-start(f32[4,32,128]{2,1,0:T(8,128)} %bitcast.15), channel_id=1, source_target_pairs={{0,2},{2,0},{4,6},{6,4},{8,16},{10,18},{12,20},{14,22},{16,8},{18,... | collective-permute-start | bytes 196616 | tf_op jit(solution)/shard_map/ppermute | solution.py:381
  3.1 5.2 %collective-permute-start.2 = (f32[4,32,128]{2,1,0:T(8,128)}, f32[4,32,128]{2,1,0:T(8,128)S(1)}, u32[]{:S(2)}, u32[]{:S(2)}) collective-permute-start(f32[4,32,128]{2,1,0:T(8,128)} %bitcast.16), channel_id=1, source_target_pairs={{0,2},{2,0},{4,6},{6,4},{8,10},{10,8},{12,14},{14,12},{16,18},{18,... | collective-permute-start | bytes 196616 | tf_op jit(solution)/shard_map/ppermute | solution.py:381
  3.2 5.1 %collective-permute-start.1 = (f32[4,32,128]{2,1,0:T(8,128)}, f32[4,32,128]{2,1,0:T(8,128)S(1)}, u32[]{:S(2)}, u32[]{:S(2)}) collective-permute-start(f32[4,32,128]{2,1,0:T(8,128)} %bitcast.17), channel_id=1, source_target_pairs={{0,1},{1,0},{2,3},{3,2},{4,5},{5,4},{6,7},{7,6},{8,9},{9,8},{10,11... | collective-permute-start | bytes 196616 | tf_op jit(solution)/shard_map/ppermute | solution.py:379
  5.1 3.3 %collective-permute-start = (f32[4,32,128]{2,1,0:T(8,128)}, f32[4,32,128]{2,1,0:T(8,128)S(1)}, u32[]{:S(2)}, u32[]{:S(2)}) collective-permute-start(f32[4,32,128]{2,1,0:T(8,128)} %bitcast.18), channel_id=1, source_target_pairs={{0,8},{2,4},{4,2},{6,14},{8,0},{10,12},{12,10},{14,6},{16,24},{18,... | collective-permute-start | bytes 196616 | tf_op jit(solution)/shard_map/ppermute | solution.py:381
  9.5 4.5 %collective-permute-start.5 = (f32[152,128]{1,0:T(8,128)S(1)}, f32[152,128]{1,0:T(8,128)S(1)}, u32[]{:S(2)}, u32[]{:S(2)}) collective-permute-start(f32[152,128]{1,0:T(8,128)S(1)} %shard_map.48.send_ref), channel_id=1, source_target_pairs={{0,1},{1,0},{2,3},{3,2},{4,5},{5,4},{6,7},{7,6},{8,9},{9,8},{10,11... | collective-permute-start | bytes 233480 | tf_op jit(solution)/shard_map/ppermute | solution.py:413

commit v5 on v4

--- a/solution.py
+++ b/solution.py
@@ -49,30 +49,42 @@
     return ones_where(q == r // 8 % 8 * 4 + r // DOF)
 
 
-def layer_picker(z):
-    r, q = iota((WIDE, LANES), 0), iota((WIDE, LANES), 1)
-    return ones_where(q == r // DOF * 32 + r // 8 % 8 * 4 + z)
-
-
-def prolong_weights(picked):
-    count = len(picked)
+def layer_picker():
+    r, q = iota((WIDE, 32), 0), iota((WIDE, 32), 1)
+    return ones_where(q == r // 8)
+
+
+def spread_blocks(picked):
     keep = iota((WIDE, WIDE), 0) % 8 == iota((WIDE, WIDE), 1) // CDOF % 8
     kept = [jnp.where(keep, p, 0.0).astype(BF16) for p in picked]
     collapse = ones_where(iota((WIDE, LANES), 0) % CDOF == iota((WIDE, LANES), 1) % CDOF)
-    spread = dot(rows_of(kept), collapse).reshape(count, 4, DOF, LANES)
-    lane = iota((DOF, LANES), 1)
-    slot = lane // CDOF % 4
-    left = lane < DOF
-    factors = []
-    for c in range(count):
+    spread = dot(rows_of(kept), collapse).reshape(len(picked), 4, DOF, LANES)
+    slot = iota((DOF, LANES), 1) // CDOF % 4
+    blocks = []
+    for c in range(len(picked)):
         full = spread[c, 0]
         for i in range(1, 4):
             full = jnp.where(slot == i, spread[c, i], full)
-        high = full.astype(BF16).astype(F32)
-        both = jnp.where(left, high, full - high).astype(BF16)
-        first = jnp.where(left, high, 0.0).astype(BF16)
-        factors.append(rows_of([both, both, first, first]))
-    return factors
+        blocks.append(full)
+    return blocks
+
+
+def factor_of(full):
+    left = iota((DOF, LANES), 1) < DOF
+    high = full.astype(BF16).astype(F32)
+    both = jnp.where(left, high, full - high).astype(BF16)
+    first = jnp.where(left, high, 0.0).astype(BF16)
+    return rows_of([both, both, first, first])
+
+
+def folded(full):
+    return jnp.where(iota((DOF // 2, LANES), 1) < DOF, full[: DOF // 2], full[DOF // 2 :])
+
+
+def unfolded(part):
+    left = iota((DOF // 2, LANES), 1) < DOF
+    turned = pltpu.roll(part, DOF, 1)
+    return rows_of([jnp.where(left, part, turned), jnp.where(left, turned, part)])
 
 
 def blocks_of(rows, factor):
@@ -103,17 +115,11 @@
     out_ref[...] = jnp.ones(out_ref.shape, F32)
 
 
-def local_kernel(shape, group_size, agg_hbm, owner_hbm, prolong_ref, fine_ref, tick_ref, outer_ref, inner_ref, label_ref,
-                 agg_ref, owner_ref, rows_scr, sems):
+def local_kernel(shape, group_size, agg_ref, owner_ref, prolong_ref, fine_ref, tick_ref,
+                 outer_ref, inner_ref, label_ref, layer_ref, layer_send, rows_scr):
     bx, by, bz = shape
     columns = bx * by
     rows_each = AGGS // group_size
-    copies = [
-        pltpu.make_async_copy(agg_hbm, agg_ref, sems.at[0]),
-        pltpu.make_async_copy(owner_hbm, owner_ref, sems.at[1]),
-    ]
-    for copy in copies:
-        copy.start()
     gx, gy, gz = lax.axis_index("gx"), lax.axis_index("gy"), lax.axis_index("gz")
     nx, ny, nz = agg_ref.shape
 
@@ -134,7 +140,14 @@
         turned += split(rows_of(stacked).T)
     lefts = dot(rows_of(turned), permute).astype(BF16)
     picked = dot(column_picker(), lanes_of([h for xy in range(columns) for h in split(prolong_ref[xy])]))
-    factors = prolong_weights([picked[:, xy * WIDE : (xy + 1) * WIDE] for xy in range(columns)])
+    picked = [picked[:, xy * WIDE : (xy + 1) * WIDE] for xy in range(columns)]
+    low, high = (
+        rows_of([prolong_ref[xy, pl.ds(z, 8, stride=bz), :] for xy in range(columns)]) for z in (0, bz - 1)
+    )
+    layers = [jnp.where(gz == 0, high, low)] if group_size == 2 else [low, high]
+    picked += [dot(layer_picker(), lanes_of(split(layer))) for layer in layers]
+    blocks = spread_blocks(picked)
+    factors = [factor_of(full) for full in blocks[:columns]]
 
     wide_lane = iota((4, CDOF, WIDE), 2) % LANES
     for xy in range(columns):
@@ -159,18 +172,20 @@
         outer_ref[2 + side] = rows_scr[(2 + side) * FACES + 2]
         outer_ref[4 + side] = rows_scr[2 * side * FACES + 3]
         outer_ref[6 + side] = rows_scr[(2 * side + 1) * FACES + 4]
-    for xy in range(columns):
-        at = slice(xy * CDOF, (xy + 1) * CDOF)
-        outer_ref[8, at] = rows_scr[xy * FACES + 5, :CDOF]
-        outer_ref[9, at] = rows_scr[xy * FACES + 6, DOF - CDOF :]
-
-    copies[0].wait()
-    copies[1].wait()
+    low = rows_of([rows_scr[xy * FACES + 5, :CDOF] for xy in range(columns)])
+    high = rows_of([rows_scr[xy * FACES + 6, DOF - CDOF :] for xy in range(columns)])
+    layers = [jnp.where(gz == 0, high, low)] if group_size == 2 else [low, high]
+    for i, layer in enumerate(layers):
+        layer_ref[i] = layer
+        both = layer[:, :LANES].astype(F32) + layer[:, LANES:].astype(F32)
+        layer_send[i * DOF : i * DOF + DOF // 2] = folded(both + pltpu.roll(both, DOF, 1))
+        layer_send[i * DOF + DOF // 2 : (i + 1) * DOF] = folded(blocks[columns + i])
+
     aggs = (agg_ref[...] + 1).reshape(nx * ny, nz).astype(F32).astype(BF16)
     width = 5 * LANES
     z_row, z_lane = iota((nz, width), 0), iota((nz, width), 1)
     kind, place = z_lane // LANES, z_lane % LANES
-    slot, face = place // CDOF % 4, place // DOF
+    slot, face = place // CDOF % 4, (1 - gz) if group_size == 2 else place // DOF
     z_off = jnp.where(kind == 0, slot, jnp.where(kind == 1, slot + 1, slot - 1))
     z_off = jnp.where(kind == 3, face * (bz - 1), jnp.where(kind == 4, face * (bz + 1) - 1, z_off))
     by_lane = dot(aggs, ones_where(z_row == gz * bz + z_off)).astype(BF16)
@@ -229,7 +244,7 @@
 
     other = by_column(table, 4)
     label = by_column(outer_base + owner * (AGGS * AGGS), 3) + (other - 1) * AGGS
-    label += jnp.where(first_half, 0, AGGS * AGGS)
+    label += (1 - gz) * AGGS * AGGS if group_size == 2 else jnp.where(first_half, 0, AGGS * AGGS)
     outer_labels.append(jnp.where(other > 0, label, -1))
     label_ref[...] = rows_of(outer_labels + [jnp.full((3, LANES), -1, jnp.int32)]).astype(F32)
 
@@ -254,9 +269,7 @@
     inner_ref[...] = dot(lanes_of([c for c in chosen for _ in range(2)]), rows_of(flat))
 
 
-def outer_kernel(group_size, links, outer_ref, inner_ref, label_ref, *refs):
-    (odd_y, *layers, even_y, odd_x, even_x), sends = refs[:links], refs[links:]
-    low_z, high_z = layers[0], layers[-1]
+def outer_kernel(group_size, outer_ref, inner_ref, label_ref, layer_send, odd_y, even_y, odd_x, even_x, *sends):
     gz = lax.axis_index("gz")
     values = []
     for axis, even, odd, low, high in (("gx", even_x, odd_x, (2, 3), (0, 1)), ("gy", even_y, odd_y, (1, 3), (0, 2))):
@@ -264,14 +277,11 @@
         values += [jnp.where(second, even[xy], odd[xy]) for xy in low]
         values += [jnp.where(second, odd[xy], even[xy]) for xy in high]
     picked = dot(column_picker(), lanes_of([h for value in values for h in split(value)]))
-    picked = [picked[:, i * WIDE : (i + 1) * WIDE] for i in range(len(values))]
-    for ref, z in ((low_z, 3), (high_z, 0)):
-        picked.append(dot(layer_picker(z), lanes_of(split(ref[...].reshape(LANES, LANES)))))
-    factors = prolong_weights(picked)
-    pieces = [diagonal(blocks_of(outer_ref[i], factors[i]), 0) for i in range(len(factors))]
+    blocks = spread_blocks([picked[:, i * WIDE : (i + 1) * WIDE] for i in range(len(values))])
+    pieces = [diagonal(blocks_of(outer_ref[i], factor_of(full)), 0) for i, full in enumerate(blocks)]
     half = iota((CDOF, LANES), 1) < DOF
     packs = [jnp.where(half, pieces[i], pieces[i + 1]) for i in range(0, len(pieces), 2)]
-    tail = rows_of(packs + [label_ref[...]])
+    tail = rows_of(packs + [label_ref[...], layer_send[...]])
     count = AGGS * AGGS // group_size
     for shift, send in enumerate(sends, 1):
         target = lax.rem(gz + shift, group_size)
@@ -281,20 +291,14 @@
         send[2 * count :] = tail
 
 
-def outer_sums(tails, gz):
-    count = len(tails)
-    packs = [tail[k * CDOF : (k + 1) * CDOF] for k in range(5) for tail in tails]
-    flat = flatten(packs)
-    labels = [tail[5 * CDOF :].astype(jnp.int32) for tail in tails]
-    sums = []
-    for k in range(5):
-        rows = (2 if k == 4 else 1) * AGGS * AGGS
-        chosen = [choose(label[k : k + 1], gz * rows, rows) for label in labels for _ in range(2)]
-        sums.append(dot(lanes_of(chosen), rows_of(flat[k * count : (k + 1) * count])))
-    return sums
-
-
-def own_kernel(group_size, inner_ref, send_ref, out_ref):
+def parts_of(tail):
+    packs = [tail[k * CDOF : (k + 1) * CDOF] for k in range(4)]
+    labels = tail[DOF : DOF + 8].astype(jnp.int32)
+    halves = [tail[at : at + DOF // 2] for at in range(DOF + 8, tail.shape[0], DOF // 2)]
+    return packs, labels, halves[::2], halves[1::2]
+
+
+def own_kernel(group_size, inner_ref, send_ref, out_ref, factor_ref):
     gz = lax.axis_index("gz")
     rows_each = AGGS // group_size
     count = AGGS * AGGS // group_size
@@ -303,14 +307,19 @@
     for c in range(AGGS):
         part = rows_of([block[c * rows_each : (c + 1) * rows_each]] * group_size)
         out_ref[:, c * WIDE : (c + 1) * WIDE] = jnp.where(mine, part, 0.0)
-    at = AGGS
-    for value in outer_sums([send_ref[2 * count :]], gz):
-        for c in range(value.shape[0] // AGGS):
-            out_ref[:, at * WIDE : (at + 1) * WIDE] = value[c * AGGS : (c + 1) * AGGS]
-            at += 1
-
-
-def final_kernel(group_size, own_ref, *refs):
+    packs, labels, _, blocks = parts_of(send_ref[2 * count :])
+    for i, part in enumerate(blocks):
+        factor_ref[i] = factor_of(unfolded(part))
+    for k, flat in enumerate(flatten(packs)):
+        chosen = choose(labels[k : k + 1], gz * AGGS * AGGS, AGGS * AGGS)
+        value = dot(lanes_of([chosen] * 2), flat)
+        for c in range(AGGS):
+            at = ((k + 1) * AGGS + c) * WIDE
+            out_ref[:, at : at + WIDE] = value[c * AGGS : (c + 1) * AGGS]
+    out_ref[:, 5 * AGGS * WIDE :] = jnp.zeros((AGGS, 2 * AGGS * WIDE), F32)
+
+
+def final_kernel(group_size, own_ref, factor_ref, layer_ref, label_ref, *refs):
     received, out_hbm, out_ref, sems = refs[:-3], refs[-3], refs[-2], refs[-1]
     gz = lax.axis_index("gz")
     rows_each = AGGS // group_size
@@ -321,6 +330,27 @@
         part = pl.ds(face * AGGS * WIDE, AGGS * WIDE)
         copies.append(pltpu.make_async_copy(out_ref.at[:, part], out_hbm.at[:, part], sems.at[face]))
         copies[-1].start()
+
+    tails = [parts_of(ref[2 * count :]) for ref in received]
+    left = iota((DOF, LANES), 1) < DOF
+    rows = [[layer_ref[i] for i in range(layer_ref.shape[0])]]
+    factors = [[factor_ref[i] for i in range(layer_ref.shape[0])]]
+    for _, _, layers, blocks in tails:
+        rows.append([lanes_of(split(jnp.where(left, unfolded(layer), 0.0))) for layer in layers])
+        factors.append([factor_of(unfolded(part)) for part in blocks])
+    layer_labels = [label_ref[4:5].astype(jnp.int32)] + [labels[4:5] for _, labels, _, _ in tails]
+    half = iota((CDOF, LANES), 1) < DOF
+    if group_size == 2:
+        pieces = [diagonal(blocks_of(rows[i][0], factors[1 - i][0]), 0) for i in range(2)]
+        layer_packs = [jnp.where(half, *pieces)]
+        layer_labels = [jnp.where(half[:1], *layer_labels)]
+    else:
+        low, high = {}, {}
+        for i in range(group_size):
+            above = (i - 1) % group_size
+            high[i] = diagonal(blocks_of(rows[i][1], factors[above][0]), 0)
+            low[above] = diagonal(blocks_of(rows[above][0], factors[i][1]), 0)
+        layer_packs = [jnp.where(half, low[i], high[i]) for i in range(group_size)]
 
     brick = iota((AGGS, LANES), 0) // rows_each
     for c in range(AGGS):
@@ -333,14 +363,23 @@
                 value = jnp.where(brick == theirs, rows_of([part] * group_size), value)
             out_ref[:, at] = value
     send_out(0)
-    at = AGGS
-    for value in outer_sums([ref[2 * count :] for ref in received], gz):
-        for c in range(value.shape[0] // AGGS):
-            cut = slice(at * WIDE, (at + 1) * WIDE)
+    flat = flatten([packs[k] for k in range(4) for packs, _, _, _ in tails] + layer_packs)
+    size = AGGS * AGGS
+    for k in range(4):
+        chosen = [choose(labels[k : k + 1], gz * size, size) for _, labels, _, _ in tails]
+        parts = flat[k * len(tails) : (k + 1) * len(tails)]
+        value = dot(lanes_of([c for c in chosen for _ in range(2)]), rows_of(parts))
+        for c in range(AGGS):
+            cut = slice(((k + 1) * AGGS + c) * WIDE, ((k + 1) * AGGS + c + 1) * WIDE)
             out_ref[:, cut] = own_ref[:, cut] + value[c * AGGS : (c + 1) * AGGS]
-            at += 1
-            if at % AGGS == 0:
-                send_out(at // AGGS - 1)
+        send_out(k + 1)
+    chosen = [choose(label, gz * 2 * size, 2 * size) for label in layer_labels]
+    value = dot(lanes_of([c for c in chosen for _ in range(2)]), rows_of(flat[4 * len(tails) :]))
+    for c in range(2 * AGGS):
+        cut = slice((5 * AGGS + c) * WIDE, (5 * AGGS + c + 1) * WIDE)
+        out_ref[:, cut] = value[c * AGGS : (c + 1) * AGGS]
+    send_out(5)
+    send_out(6)
     for copy in copies:
         copy.wait()
 
@@ -376,59 +415,59 @@
         cost_estimate=pl.CostEstimate(flops=int(5e9), bytes_accessed=int(5e7), transcendentals=0),
     )()
     sizes = lax.axis_size("gx"), lax.axis_size("gy")
-    layers = [lax.ppermute(base, "gz", rotation(group_size, step)) for step in ((1, -1) if group_size > 2 else (1,))]
     even_x, odd_x, even_y, odd_y = [
         lax.ppermute(base, ("gx", "gy"), matching(sizes, along, first)) for along in range(2) for first in range(2)
     ]
-    halos = [odd_y, *layers, even_y, odd_x, even_x]
+    halos = [odd_y, even_y, odd_x, even_x]
+    layers = 1 if group_size == 2 else 2
     params = pltpu.CompilerParams(vmem_limit_bytes=32 * 1024 * 1024)
     shape = jax.ShapeDtypeStruct
-    outer, inner, labels = pl.pallas_call(
+    outer, inner, labels, layer_rows, layer_send = pl.pallas_call(
         functools.partial(local_kernel, (bx, by, bz), group_size),
-        out_shape=[shape((10, DOF, WIDE), BF16), shape((AGGS * AGGS, WIDE), F32), shape((8, LANES), F32)],
-        in_specs=[HBM] * 2 + [VMEM] * 3,
-        out_specs=[VMEM] * 3,
-        scratch_shapes=[
-            pltpu.VMEM(agg_map.shape, jnp.int32),
-            pltpu.VMEM(owner_map.shape, jnp.int32),
-            pltpu.VMEM((columns * FACES, DOF, WIDE), BF16),
-            pltpu.SemaphoreType.DMA((2,)),
+        out_shape=[
+            shape((8, DOF, WIDE), BF16),
+            shape((AGGS * AGGS, WIDE), F32),
+            shape((8, LANES), F32),
+            shape((layers, DOF, WIDE), BF16),
+            shape((layers * DOF, LANES), F32),
         ],
+        in_specs=[VMEM] * 5,
+        out_specs=[VMEM] * 5,
+        scratch_shapes=[pltpu.VMEM((columns * FACES, DOF, WIDE), BF16)],
         compiler_params=params,
         cost_estimate=pl.CostEstimate(flops=int(2e9), bytes_accessed=int(4e6), transcendentals=0),
     )(
-        *(pltpu.with_memory_space_constraint(a, pltpu.HBM) for a in (agg_map, owner_map)),
-        *(pltpu.with_memory_space_constraint(a, pltpu.VMEM) for a in (base, fine)),
+        *(pltpu.with_memory_space_constraint(a, pltpu.VMEM) for a in (agg_map, owner_map, base, fine)),
         tick,
     )
-    size = 2 * AGGS * AGGS // group_size + 5 * CDOF + 8
+    size = 2 * AGGS * AGGS // group_size + 4 * CDOF + 8 + layers * DOF
     sends = pl.pallas_call(
-        functools.partial(outer_kernel, group_size, len(halos)),
+        functools.partial(outer_kernel, group_size),
         out_shape=[shape((size, LANES), F32)] * (group_size - 1),
-        in_specs=[VMEM] * (3 + len(halos)),
+        in_specs=[VMEM] * 8,
         out_specs=[VMEM] * (group_size - 1),
         compiler_params=params,
-    )(outer, inner, labels, *halos)
+    )(outer, inner, labels, layer_send, *halos)
     received = [
         lax.ppermute(send, "gz", rotation(group_size, shift)) for shift, send in enumerate(sends, 1)
     ]
     full = shape((AGGS, FACES * AGGS * CDOF * CDOF), F32)
-    own = pl.pallas_call(
+    own, factor = pl.pallas_call(
         functools.partial(own_kernel, group_size),
-        out_shape=full,
+        out_shape=[full, shape((layers, WIDE, LANES), BF16)],
         in_specs=[VMEM, VMEM],
-        out_specs=VMEM,
+        out_specs=[VMEM, VMEM],
         compiler_params=params,
         cost_estimate=pl.CostEstimate(flops=int(1e9), bytes_accessed=int(2e6), transcendentals=0),
     )(inner, sends[0])
     out = pl.pallas_call(
         functools.partial(final_kernel, group_size),
         out_shape=full,
-        in_specs=[VMEM] * group_size,
+        in_specs=[VMEM] * (3 + group_size),
         out_specs=HBM,
         scratch_shapes=[pltpu.VMEM(full.shape, F32), pltpu.SemaphoreType.DMA((FACES,))],
         compiler_params=params,
-    )(own, *received)
+    )(own, factor, layer_rows, labels, *received)
     return out[None, None]
 
 

time: 15.5 us -> 15 us (0.968)
  starting transfers between devices: 7.55 us -> 6.09 us
  waiting for transfers between devices: 1.99 us -> 3.05 us
    ppermute x1 -> x0, starting transfers between devices: 1.89 us -> none  [shards(): lax.ppermute(base, 'gz', rotation(group_size, step))]
    ppermute x4, starting transfers between devices: 3.77 us -> 4.5 us  [shards(): lax.ppermute(base, ('gx', 'gy'), matching(sizes, along, first))]
    ppermute x1, waiting for transfers between devices: 1.97 us -> 2.62 us  [shards(): lax.ppermute(send, 'gz', rotation(group_size, shift))]
    ppermute x4, waiting for transfers between devices: 0.01 us -> 0.43 us  [shards(): lax.ppermute(base, ('gx', 'gy'), matching(sizes, along, first))]
    ppermute x1, starting transfers between devices: 1.89 us -> 1.58 us  [shards(): lax.ppermute(send, 'gz', rotation(group_size, shift))]
    pallas_call x2, Pallas kernels: 1.81 us -> 1.56 us  [the longest x1 1.05 us: shards(): pl.pallas_call(functools.partial(outer_kernel, group_size), out_shape=[sh...]
  transfers between devices with their start and end apart: 6 -> 5, of which waited for: 1 -> 2; matrix products, arithmetic and copies ran while one was open for 0% -> 0% of each run, Pallas kernels for 21% -> 21%
where the time goes in v5:
time: 15 us; the launch traced here: 14.9 us
  starting transfers between devices  6.09 us (41%)
  Pallas kernels  5.64 us (38%)
  waiting for transfers between devices  3.05 us (20%)
    ppermute x4, starting transfers between devices, shards(): lax.ppermute(base, ('gx', 'gy'), matching(sizes, along, first))  4.5 us
    pallas_call x1, Pallas kernels, shards(): pl.pallas_call(functools.partial(local_kernel, (bx, by, bz), group_size),...  2.68 us
    ppermute x1, waiting for transfers between devices, shards(): lax.ppermute(send, 'gz', rotation(group_size, shift))  2.62 us
    ppermute x1, starting transfers between devices, shards(): lax.ppermute(send, 'gz', rotation(group_size, shift))  1.58 us
    pallas_call x1, Pallas kernels, shards(): pl.pallas_call(functools.partial(final_kernel, group_size), out_shape=ful...  1.41 us
    pallas_call x1, Pallas kernels, shards(): pl.pallas_call(functools.partial(outer_kernel, group_size), out_shape=[sh...  1.05 us
    pallas_call x1, Pallas kernels, shards(): pl.pallas_call(functools.partial(own_kernel, group_size), out_shape=[full...  0.51 us
    ppermute x4, waiting for transfers between devices, shards(): lax.ppermute(base, ('gx', 'gy'), matching(sizes, along, first))  0.43 us
  transfers between devices with their start and end apart: 5, of which 2 were waited for; matrix products, arithmetic and copies ran while one was open for 0% of the time, Pallas kernels for 21%

profile of v5, /device:TPU:0, one launch (start us, length us, event | category | flops | bytes accessed | tf_op | source)
XLA Modules:
  0.0 14.9 jit_solution(11205727370953672439)
XLA Ops:
  0.0 0.0 copy-start
  0.0 0.0 copy-start.1
  0.0 0.0 copy-start.2
  0.0 0.0 copy-start.3
  0.0 0.5 %collective-permute-start.3 = (f32[4,32,128]{2,1,0:T(8,128)}, f32[4,32,128]{2,1,0:T(8,128)S(1)}, u32[]{:S(2)}, u32[]{:S(2)}) collective-permute-start(f32[4,32,128]{2,1,0:T(8,128)} %bitcast.14), channel_id=1, source_target_pairs={{0,8},{2,10},{4,12},{6,14},{8,0},{10,2},{12,4},{14,6},{16,24},{18,... | collective-permute-start | bytes 196616 | tf_op jit(solution)/shard_map/ppermute | solution.py:419
  0.5 2.6 %collective-permute-start.2 = (f32[4,32,128]{2,1,0:T(8,128)}, f32[4,32,128]{2,1,0:T(8,128)S(1)}, u32[]{:S(2)}, u32[]{:S(2)}) collective-permute-start(f32[4,32,128]{2,1,0:T(8,128)} %bitcast.15), channel_id=1, source_target_pairs={{0,2},{2,0},{4,6},{6,4},{8,16},{10,18},{12,20},{14,22},{16,8},{18,... | collective-permute-start | bytes 196616 | tf_op jit(solution)/shard_map/ppermute | solution.py:419
  3.2 0.1 collective-permute-start.1
  3.3 1.2 %collective-permute-start = (f32[4,32,128]{2,1,0:T(8,128)}, f32[4,32,128]{2,1,0:T(8,128)S(1)}, u32[]{:S(2)}, u32[]{:S(2)}) collective-permute-start(f32[4,32,128]{2,1,0:T(8,128)} %bitcast.17), channel_id=1, source_target_pairs={{0,8},{2,4},{4,2},{6,14},{8,0},{10,12},{12,10},{14,6},{16,24},{18,... | collective-permute-start | bytes 196616 | tf_op jit(solution)/shard_map/ppermute | solution.py:419
  4.5 0.0 copy-done
  4.5 0.0 copy-done.1
  4.5 0.0 copy-done.2
  4.5 0.0 copy-done.3
  4.5 2.7 %shard_map.47 = (bf16[8,64,256]{2,1,0:T(8,128)(2,1)S(1)}, f32[64,256]{1,0:T(8,128)S(1)}, f32[8,128]{1,0:T(8,128)S(1)}, bf16[1,64,256]{2,1,0:T(8,128)(2,1)S(1)}, f32[64,128]{1,0:T(8,128)S(1)}) custom-call(s32[8,8,8]{2,1,0:T(8,128)S(1)} %copy-done.2, s32[1,1,8]{2,1,0:T(1,128)S(1)} %copy-done.3, f32[4,32,128]{2,1,0:T(8,128)S(1)} %bitcast.18, ...), custom_call_target="tpu_custom_call" | custom-call | flops 2000000000 | bytes 4000000 | tf_op jit(solution)/shard_map/pallas_call | solution.py:425
  7.2 0.0 collective-permute-done.3.even_x
  7.2 0.0 collective-permute-done.2.odd_x
  7.2 0.4 %collective-permute-done.1.even_y = f32[4,32,128]{2,1,0:T(8,128)S(1)} collective-permute-done((f32[4,32,128]{2,1,0:T(8,128)}, f32[4,32,128]{2,1,0:T(8,128)S(1)}, u32[]{:S(2)}, u32[]{:S(2)}) %collective-permute-start.1) | collective-permute-done | bytes 65568 | tf_op jit(solution)/shard_map/ppermute | solution.py:419
  7.7 0.0 collective-permute-done.odd_y
  7.7 1.0 %shard_map.48.send_ref = f32[200,128]{1,0:T(8,128)S(1)} custom-call(bf16[8,64,256]{2,1,0:T(8,128)(2,1)S(1)} %get-tuple-element.13.outer_ref, f32[64,256]{1,0:T(8,128)S(1)} %get-tuple-element.12.inner_ref, f32[8,128]{1,0:T(8,128)S(1)} %get-tuple-element.14.label_ref, f32[64,128]{1,0:T(8,128)S(1)} %get-tuple-element.15.layer_send, ...), custom_call_target="tpu_custom_call" | custom-call | tf_op jit(solution)/shard_map/pallas_call | solution.py:444
  8.7 1.6 %collective-permute-start.4 = (f32[200,128]{1,0:T(8,128)S(1)}, f32[200,128]{1,0:T(8,128)S(1)}, u32[]{:S(2)}, u32[]{:S(2)}) collective-permute-start(f32[200,128]{1,0:T(8,128)S(1)} %shard_map.48.send_ref), channel_id=1, source_target_pairs={{0,1},{1,0},{2,3},{3,2},{4,5},{5,4},{6,7},{7,6},{8,9},{9,8},{10,11... | collective-permute-start | bytes 307208 | tf_op jit(solution)/shard_map/ppermute | solution.py:452
  10.3 0.5 %shard_map.49 = (f32[8,14336]{1,0:T(8,128)S(1)}, bf16[1,256,128]{2,1,0:T(8,128)(2,1)S(1)}) custom-call(f32[64,256]{1,0:T(8,128)S(1)} %get-tuple-element.12.inner_ref, f32[200,128]{1,0:T(8,128)S(1)} %shard_map.48.send_ref), custom_call_target="tpu_custom_call" | custom-call | flops 1000000000 | bytes 2000000 | tf_op jit(solution)/shard_map/pallas_call | solution.py:455
  10.8 2.6 %collective-permute-done.4.refs_0_ = f32[200,128]{1,0:T(8,128)S(1)} collective-permute-done((f32[200,128]{1,0:T(8,128)S(1)}, f32[200,128]{1,0:T(8,128)S(1)}, u32[]{:S(2)}, u32[]{:S(2)}) %collective-permute-start.4) | collective-permute-done | bytes 102432 | tf_op jit(solution)/shard_map/ppermute | solution.py:452
  13.4 1.4 %shard_map.50 = f32[8,14336]{1,0:T(8,128)} custom-call(f32[8,14336]{1,0:T(8,128)S(1)} %get-tuple-element.16.own_ref, bf16[1,256,128]{2,1,0:T(8,128)(2,1)S(1)} %get-tuple-element.17.factor_ref, bf16[1,64,256]{2,1,0:T(8,128)(2,1)S(1)} %get-tuple-element.18.layer_ref, f32[8,128]{1,0:T(8,128)S(1)} %get-tuple-element.14.label_ref, ...), custom_call_target="tpu_custom_call" | custom-call | tf_op jit(solution)/shard_map/pallas_call | solution.py:463
  (1 shorter events, 0.0 us)
Async XLA Ops:
  0.0 4.5 %copy-start = (f32[2,2,4,7,4096]{4,2,3,1,0:T(4,128)S(1)}, f32[2,2,4,7,4096]{4,2,3,1,0:T(4,128)}, u32[]{:S(2)}) copy-start(f32[2,2,4,7,4096]{4,2,3,1,0:T(4,128)} %param.4) | copy-start | bytes 5505028
  0.0 4.5 %copy-start.1 = (f32[2,2,4,1024]{3,2,1,0:T(4,128)S(1)}, f32[2,2,4,1024]{3,2,1,0:T(4,128)}, u32[]{:S(2)}) copy-start(f32[2,2,4,1024]{3,2,1,0:T(4,128)} %param.5) | copy-start | bytes 196612
  0.0 4.5 %copy-start.2 = (s32[8,8,8]{2,1,0:T(8,128)S(1)}, s32[8,8,8]{2,1,0:T(8,128)}, u32[]{:S(2)}) copy-start(s32[8,8,8]{2,1,0:T(8,128)} %agg_ref.1) | copy-start | bytes 6148
  0.0 4.5 %copy-start.3 = (s32[1,1,8]{2,1,0:T(1,128)S(1)}, s32[1,1,8]{2,1,0:T(1,128)}, u32[]{:S(2)}) copy-start(s32[1,1,8]{2,1,0:T(1,128)} %owner_ref.1) | copy-start | bytes 100
  0.0 7.2 %collective-permute-start.3 = (f32[4,32,128]{2,1,0:T(8,128)}, f32[4,32,128]{2,1,0:T(8,128)S(1)}, u32[]{:S(2)}, u32[]{:S(2)}) collective-permute-start(f32[4,32,128]{2,1,0:T(8,128)} %bitcast.14), channel_id=1, source_target_pairs={{0,8},{2,10},{4,12},{6,14},{8,0},{10,2},{12,4},{14,6},{16,24},{18,... | collective-permute-start | bytes 196616 | tf_op jit(solution)/shard_map/ppermute | solution.py:419
  0.5 6.7 %collective-permute-start.2 = (f32[4,32,128]{2,1,0:T(8,128)}, f32[4,32,128]{2,1,0:T(8,128)S(1)}, u32[]{:S(2)}, u32[]{:S(2)}) collective-permute-start(f32[4,32,128]{2,1,0:T(8,128)} %bitcast.15), channel_id=1, source_target_pairs={{0,2},{2,0},{4,6},{6,4},{8,16},{10,18},{12,20},{14,22},{16,8},{18,... | collective-permute-start | bytes 196616 | tf_op jit(solution)/shard_map/ppermute | solution.py:419
  3.2 4.5 %collective-permute-start.1 = (f32[4,32,128]{2,1,0:T(8,128)}, f32[4,32,128]{2,1,0:T(8,128)S(1)}, u32[]{:S(2)}, u32[]{:S(2)}) collective-permute-start(f32[4,32,128]{2,1,0:T(8,128)} %bitcast.16), channel_id=1, source_target_pairs={{0,2},{2,0},{4,6},{6,4},{8,10},{10,8},{12,14},{14,12},{16,18},{18,... | collective-permute-start | bytes 196616 | tf_op jit(solution)/shard_map/ppermute | solution.py:419
  3.3 4.4 %collective-permute-start = (f32[4,32,128]{2,1,0:T(8,128)}, f32[4,32,128]{2,1,0:T(8,128)S(1)}, u32[]{:S(2)}, u32[]{:S(2)}) collective-permute-start(f32[4,32,128]{2,1,0:T(8,128)} %bitcast.17), channel_id=1, source_target_pairs={{0,8},{2,4},{4,2},{6,14},{8,0},{10,12},{12,10},{14,6},{16,24},{18,... | collective-permute-start | bytes 196616 | tf_op jit(solution)/shard_map/ppermute | solution.py:419
  8.7 4.7 %collective-permute-start.4 = (f32[200,128]{1,0:T(8,128)S(1)}, f32[200,128]{1,0:T(8,128)S(1)}, u32[]{:S(2)}, u32[]{:S(2)}) collective-permute-start(f32[200,128]{1,0:T(8,128)S(1)} %shard_map.48.send_ref), channel_id=1, source_target_pairs={{0,1},{1,0},{2,3},{3,2},{4,5},{5,4},{6,7},{7,6},{8,9},{9,8},{10,11... | collective-permute-start | bytes 307208 | tf_op jit(solution)/shard_map/ppermute | solution.py:452

commit v6 on v5

--- a/solution.py
+++ b/solution.py
@@ -44,41 +44,26 @@
     return jnp.concatenate(parts, axis=1)
 
 
-def column_picker():
-    r, q = iota((WIDE, 32), 0), iota((WIDE, 32), 1)
-    return ones_where(q == r // 8 % 8 * 4 + r // DOF)
-
-
-def layer_picker():
-    r, q = iota((WIDE, 32), 0), iota((WIDE, 32), 1)
-    return ones_where(q == r // 8)
-
-
-def spread_blocks(picked):
-    keep = iota((WIDE, WIDE), 0) % 8 == iota((WIDE, WIDE), 1) // CDOF % 8
-    kept = [jnp.where(keep, p, 0.0).astype(BF16) for p in picked]
-    collapse = ones_where(iota((WIDE, LANES), 0) % CDOF == iota((WIDE, LANES), 1) % CDOF)
-    spread = dot(rows_of(kept), collapse).reshape(len(picked), 4, DOF, LANES)
-    slot = iota((DOF, LANES), 1) // CDOF % 4
-    blocks = []
-    for c in range(len(picked)):
-        full = spread[c, 0]
+def spread_blocks(out_ref, pieces):
+    slot = iota((8, LANES), 1) // CDOF
+    for b in range(8):
+        value = pltpu.roll(pieces[0], -b * CDOF % LANES, 1)
         for i in range(1, 4):
-            full = jnp.where(slot == i, spread[c, i], full)
-        blocks.append(full)
-    return blocks
+            value = jnp.where(slot == i, pltpu.roll(pieces[i], (i - b) * CDOF % LANES, 1), value)
+        out_ref[pl.ds(b, 8, stride=8), :] = value
 
 
 def factor_of(full):
     left = iota((DOF, LANES), 1) < DOF
     high = full.astype(BF16).astype(F32)
-    both = jnp.where(left, high, full - high).astype(BF16)
+    both = jnp.where(left, high, pltpu.roll(full - high, DOF, 1)).astype(BF16)
     first = jnp.where(left, high, 0.0).astype(BF16)
     return rows_of([both, both, first, first])
 
 
 def folded(full):
-    return jnp.where(iota((DOF // 2, LANES), 1) < DOF, full[: DOF // 2], full[DOF // 2 :])
+    half = DOF // 2
+    return jnp.where(iota((half, LANES), 1) < DOF, full[:half], pltpu.roll(full[half:], DOF, 1))
 
 
 def unfolded(part):
@@ -116,7 +101,7 @@
 
 
 def local_kernel(shape, group_size, agg_ref, owner_ref, prolong_ref, fine_ref, tick_ref,
-                 outer_ref, inner_ref, label_ref, layer_ref, layer_send, rows_scr):
+                 outer_ref, inner_ref, label_ref, layer_ref, layer_send, rows_scr, blocks_scr):
     bx, by, bz = shape
     columns = bx * by
     rows_each = AGGS // group_size
@@ -139,15 +124,13 @@
             stacked.append(part)
         turned += split(rows_of(stacked).T)
     lefts = dot(rows_of(turned), permute).astype(BF16)
-    picked = dot(column_picker(), lanes_of([h for xy in range(columns) for h in split(prolong_ref[xy])]))
-    picked = [picked[:, xy * WIDE : (xy + 1) * WIDE] for xy in range(columns)]
-    low, high = (
-        rows_of([prolong_ref[xy, pl.ds(z, 8, stride=bz), :] for xy in range(columns)]) for z in (0, bz - 1)
-    )
-    layers = [jnp.where(gz == 0, high, low)] if group_size == 2 else [low, high]
-    picked += [dot(layer_picker(), lanes_of(split(layer))) for layer in layers]
-    blocks = spread_blocks(picked)
-    factors = [factor_of(full) for full in blocks[:columns]]
+    for xy in range(columns):
+        spread_blocks(blocks_scr.at[xy], [prolong_ref[xy, pl.ds(z, 8, stride=bz), :] for z in range(bz)])
+    low, high = ([prolong_ref[xy, pl.ds(z, 8, stride=bz), :] for xy in range(columns)] for z in (0, bz - 1))
+    layers = [[jnp.where(gz == 0, h, l) for l, h in zip(low, high)]] if group_size == 2 else [low, high]
+    for i, layer in enumerate(layers):
+        spread_blocks(blocks_scr.at[columns + i], layer)
+    factors = [factor_of(blocks_scr[xy]) for xy in range(columns)]
 
     wide_lane = iota((4, CDOF, WIDE), 2) % LANES
     for xy in range(columns):
@@ -179,7 +162,7 @@
         layer_ref[i] = layer
         both = layer[:, :LANES].astype(F32) + layer[:, LANES:].astype(F32)
         layer_send[i * DOF : i * DOF + DOF // 2] = folded(both + pltpu.roll(both, DOF, 1))
-        layer_send[i * DOF + DOF // 2 : (i + 1) * DOF] = folded(blocks[columns + i])
+        layer_send[i * DOF + DOF // 2 : (i + 1) * DOF] = folded(blocks_scr[columns + i])
 
     aggs = (agg_ref[...] + 1).reshape(nx * ny, nz).astype(F32).astype(BF16)
     width = 5 * LANES
@@ -269,16 +252,18 @@
     inner_ref[...] = dot(lanes_of([c for c in chosen for _ in range(2)]), rows_of(flat))
 
 
-def outer_kernel(group_size, outer_ref, inner_ref, label_ref, layer_send, odd_y, even_y, odd_x, even_x, *sends):
+def outer_kernel(group_size, outer_ref, inner_ref, label_ref, layer_send, odd_y, even_y, odd_x, even_x, *refs):
     gz = lax.axis_index("gz")
-    values = []
+    sends, blocks_scr = refs[:-1], refs[-1]
+    place = 0
     for axis, even, odd, low, high in (("gx", even_x, odd_x, (2, 3), (0, 1)), ("gy", even_y, odd_y, (1, 3), (0, 2))):
         second = lax.rem(lax.axis_index(axis), 2) == 1
-        values += [jnp.where(second, even[xy], odd[xy]) for xy in low]
-        values += [jnp.where(second, odd[xy], even[xy]) for xy in high]
-    picked = dot(column_picker(), lanes_of([h for value in values for h in split(value)]))
-    blocks = spread_blocks([picked[:, i * WIDE : (i + 1) * WIDE] for i in range(len(values))])
-    pieces = [diagonal(blocks_of(outer_ref[i], factor_of(full)), 0) for i, full in enumerate(blocks)]
+        for one, two, columns in ((even, odd, low), (odd, even, high)):
+            for xy in columns:
+                rows = [pl.ds(z, 8, stride=4) for z in range(4)]
+                spread_blocks(blocks_scr.at[place], [jnp.where(second, one[xy, z, :], two[xy, z, :]) for z in rows])
+                place += 1
+    pieces = [diagonal(blocks_of(outer_ref[i], factor_of(blocks_scr[i])), 0) for i in range(8)]
     half = iota((CDOF, LANES), 1) < DOF
     packs = [jnp.where(half, pieces[i], pieces[i + 1]) for i in range(0, len(pieces), 2)]
     tail = rows_of(packs + [label_ref[...], layer_send[...]])
@@ -363,7 +348,7 @@
                 value = jnp.where(brick == theirs, rows_of([part] * group_size), value)
             out_ref[:, at] = value
     send_out(0)
-    flat = flatten([packs[k] for k in range(4) for packs, _, _, _ in tails] + layer_packs)
+    flat = flatten([packs[k] for k in range(4) for packs, _, _, _ in tails]) + flatten(layer_packs)
     size = AGGS * AGGS
     for k in range(4):
         chosen = [choose(labels[k : k + 1], gz * size, size) for _, labels, _, _ in tails]
@@ -433,7 +418,10 @@
         ],
         in_specs=[VMEM] * 5,
         out_specs=[VMEM] * 5,
-        scratch_shapes=[pltpu.VMEM((columns * FACES, DOF, WIDE), BF16)],
+        scratch_shapes=[
+            pltpu.VMEM((columns * FACES, DOF, WIDE), BF16),
+            pltpu.VMEM((columns + layers, DOF, LANES), F32),
+        ],
         compiler_params=params,
         cost_estimate=pl.CostEstimate(flops=int(2e9), bytes_accessed=int(4e6), transcendentals=0),
     )(
@@ -446,6 +434,7 @@
         out_shape=[shape((size, LANES), F32)] * (group_size - 1),
         in_specs=[VMEM] * 8,
         out_specs=[VMEM] * (group_size - 1),
+        scratch_shapes=[pltpu.VMEM((8, DOF, LANES), F32)],
         compiler_params=params,
     )(outer, inner, labels, layer_send, *halos)
     received = [

time: 15 us -> 14.7 us (0.980)
  Pallas kernels: 5.64 us -> 4.87 us
  waiting for transfers between devices: 3.05 us -> 3.5 us
    pallas_call x1, Pallas kernels: 2.68 us -> 2.22 us  [shards(): pl.pallas_call(functools.partial(local_kernel, (bx, by, bz), group_size),...]
    ppermute x4, waiting for transfers between devices: 0.43 us -> 0.88 us  [shards(): lax.ppermute(base, ('gx', 'gy'), matching(sizes, along, first))]
    pallas_call x1, Pallas kernels: 1.05 us -> 0.66 us  [shards(): pl.pallas_call(functools.partial(outer_kernel, group_size), out_shape=[sh...]
  transfers between devices with their start and end apart: 5 -> 5, of which waited for: 2 -> 2; matrix products, arithmetic and copies ran while one was open for 0% -> 0% of each run, Pallas kernels for 21% -> 19%
where the time goes in v6:
time: 14.7 us; the launch traced here: 14.5 us
  starting transfers between devices  6.09 us (41%)
  Pallas kernels  4.87 us (33%)
  waiting for transfers between devices  3.5 us (24%)
    ppermute x4, starting transfers between devices, shards(): lax.ppermute(base, ('gx', 'gy'), matching(sizes, along, first))  4.5 us
    ppermute x1, waiting for transfers between devices, shards(): lax.ppermute(send, 'gz', rotation(group_size, shift))  2.62 us
    pallas_call x1, Pallas kernels, shards(): pl.pallas_call(functools.partial(local_kernel, (bx, by, bz), group_size),...  2.22 us
    ppermute x1, starting transfers between devices, shards(): lax.ppermute(send, 'gz', rotation(group_size, shift))  1.59 us
    pallas_call x1, Pallas kernels, shards(): pl.pallas_call(functools.partial(final_kernel, group_size), out_shape=ful...  1.47 us
    ppermute x4, waiting for transfers between devices, shards(): lax.ppermute(base, ('gx', 'gy'), matching(sizes, along, first))  0.88 us
    pallas_call x1, Pallas kernels, shards(): pl.pallas_call(functools.partial(outer_kernel, group_size), out_shape=[sh...  0.66 us
    pallas_call x1, Pallas kernels, shards(): pl.pallas_call(functools.partial(own_kernel, group_size), out_shape=[full...  0.51 us
  transfers between devices with their start and end apart: 5, of which 2 were waited for; matrix products, arithmetic and copies ran while one was open for 0% of the time, Pallas kernels for 19%

profile of v6, /device:TPU:0, one launch (start us, length us, event | category | flops | bytes accessed | tf_op | source)
XLA Modules:
  0.0 14.5 jit_solution(9359714713520331029)
XLA Ops:
  0.0 0.0 copy-start
  0.0 0.0 copy-start.1
  0.0 0.0 copy-start.2
  0.0 0.0 copy-start.3
  0.0 0.5 %collective-permute-start.3 = (f32[4,32,128]{2,1,0:T(8,128)}, f32[4,32,128]{2,1,0:T(8,128)S(1)}, u32[]{:S(2)}, u32[]{:S(2)}) collective-permute-start(f32[4,32,128]{2,1,0:T(8,128)} %bitcast.14), channel_id=1, source_target_pairs={{0,8},{2,10},{4,12},{6,14},{8,0},{10,2},{12,4},{14,6},{16,24},{18,... | collective-permute-start | bytes 196616 | tf_op jit(solution)/shard_map/ppermute | solution.py:404
  0.5 2.6 %collective-permute-start.2 = (f32[4,32,128]{2,1,0:T(8,128)}, f32[4,32,128]{2,1,0:T(8,128)S(1)}, u32[]{:S(2)}, u32[]{:S(2)}) collective-permute-start(f32[4,32,128]{2,1,0:T(8,128)} %bitcast.15), channel_id=1, source_target_pairs={{0,2},{2,0},{4,6},{6,4},{8,16},{10,18},{12,20},{14,22},{16,8},{18,... | collective-permute-start | bytes 196616 | tf_op jit(solution)/shard_map/ppermute | solution.py:404
  3.2 0.1 collective-permute-start.1
  3.3 1.2 %collective-permute-start = (f32[4,32,128]{2,1,0:T(8,128)}, f32[4,32,128]{2,1,0:T(8,128)S(1)}, u32[]{:S(2)}, u32[]{:S(2)}) collective-permute-start(f32[4,32,128]{2,1,0:T(8,128)} %bitcast.17), channel_id=1, source_target_pairs={{0,8},{2,4},{4,2},{6,14},{8,0},{10,12},{12,10},{14,6},{16,24},{18,... | collective-permute-start | bytes 196616 | tf_op jit(solution)/shard_map/ppermute | solution.py:404
  4.5 0.0 copy-done
  4.5 0.0 copy-done.1
  4.5 0.0 copy-done.2
  4.5 0.0 copy-done.3
  4.5 2.2 %shard_map.47 = (bf16[8,64,256]{2,1,0:T(8,128)(2,1)S(1)}, f32[64,256]{1,0:T(8,128)S(1)}, f32[8,128]{1,0:T(8,128)S(1)}, bf16[1,64,256]{2,1,0:T(8,128)(2,1)S(1)}, f32[64,128]{1,0:T(8,128)S(1)}) custom-call(s32[8,8,8]{2,1,0:T(8,128)S(1)} %copy-done.2, s32[1,1,8]{2,1,0:T(1,128)S(1)} %copy-done.3, f32[4,32,128]{2,1,0:T(8,128)S(1)} %bitcast.18, ...), custom_call_target="tpu_custom_call" | custom-call | flops 2000000000 | bytes 4000000 | tf_op jit(solution)/shard_map/pallas_call | solution.py:410
  6.8 0.0 collective-permute-done.3.even_x
  6.8 0.0 collective-permute-done.2.odd_x
  6.8 0.9 %collective-permute-done.1.even_y = f32[4,32,128]{2,1,0:T(8,128)S(1)} collective-permute-done((f32[4,32,128]{2,1,0:T(8,128)}, f32[4,32,128]{2,1,0:T(8,128)S(1)}, u32[]{:S(2)}, u32[]{:S(2)}) %collective-permute-start.1) | collective-permute-done | bytes 65568 | tf_op jit(solution)/shard_map/ppermute | solution.py:404
  7.7 0.0 collective-permute-done.odd_y
  7.7 0.7 %shard_map.48.send_ref = f32[200,128]{1,0:T(8,128)S(1)} custom-call(bf16[8,64,256]{2,1,0:T(8,128)(2,1)S(1)} %get-tuple-element.13.outer_ref, f32[64,256]{1,0:T(8,128)S(1)} %get-tuple-element.12.inner_ref, f32[8,128]{1,0:T(8,128)S(1)} %get-tuple-element.14.label_ref, f32[64,128]{1,0:T(8,128)S(1)} %get-tuple-element.15.layer_send, ...), custom_call_target="tpu_custom_call" | custom-call | tf_op jit(solution)/shard_map/pallas_call | solution.py:432
  8.3 1.6 %collective-permute-start.4 = (f32[200,128]{1,0:T(8,128)S(1)}, f32[200,128]{1,0:T(8,128)S(1)}, u32[]{:S(2)}, u32[]{:S(2)}) collective-permute-start(f32[200,128]{1,0:T(8,128)S(1)} %shard_map.48.send_ref), channel_id=1, source_target_pairs={{0,1},{1,0},{2,3},{3,2},{4,5},{5,4},{6,7},{7,6},{8,9},{9,8},{10,11... | collective-permute-start | bytes 307208 | tf_op jit(solution)/shard_map/ppermute | solution.py:441
  9.9 0.5 %shard_map.49 = (f32[8,14336]{1,0:T(8,128)S(1)}, bf16[1,256,128]{2,1,0:T(8,128)(2,1)S(1)}) custom-call(f32[64,256]{1,0:T(8,128)S(1)} %get-tuple-element.12.inner_ref, f32[200,128]{1,0:T(8,128)S(1)} %shard_map.48.send_ref), custom_call_target="tpu_custom_call" | custom-call | flops 1000000000 | bytes 2000000 | tf_op jit(solution)/shard_map/pallas_call | solution.py:444
  10.4 2.6 %collective-permute-done.4.refs_0_ = f32[200,128]{1,0:T(8,128)S(1)} collective-permute-done((f32[200,128]{1,0:T(8,128)S(1)}, f32[200,128]{1,0:T(8,128)S(1)}, u32[]{:S(2)}, u32[]{:S(2)}) %collective-permute-start.4) | collective-permute-done | bytes 102432 | tf_op jit(solution)/shard_map/ppermute | solution.py:441
  13.1 1.5 %shard_map.50 = f32[8,14336]{1,0:T(8,128)} custom-call(f32[8,14336]{1,0:T(8,128)S(1)} %get-tuple-element.16.own_ref, bf16[1,256,128]{2,1,0:T(8,128)(2,1)S(1)} %get-tuple-element.17.factor_ref, bf16[1,64,256]{2,1,0:T(8,128)(2,1)S(1)} %get-tuple-element.18.layer_ref, f32[8,128]{1,0:T(8,128)S(1)} %get-tuple-element.14.label_ref, ...), custom_call_target="tpu_custom_call" | custom-call | tf_op jit(solution)/shard_map/pallas_call | solution.py:452
  (1 shorter events, 0.0 us)
Async XLA Ops:
  0.0 4.5 %copy-start = (f32[2,2,4,7,4096]{4,2,3,1,0:T(4,128)S(1)}, f32[2,2,4,7,4096]{4,2,3,1,0:T(4,128)}, u32[]{:S(2)}) copy-start(f32[2,2,4,7,4096]{4,2,3,1,0:T(4,128)} %param.4) | copy-start | bytes 5505028
  0.0 4.5 %copy-start.1 = (f32[2,2,4,1024]{3,2,1,0:T(4,128)S(1)}, f32[2,2,4,1024]{3,2,1,0:T(4,128)}, u32[]{:S(2)}) copy-start(f32[2,2,4,1024]{3,2,1,0:T(4,128)} %param.5) | copy-start | bytes 196612
  0.0 4.5 %copy-start.2 = (s32[8,8,8]{2,1,0:T(8,128)S(1)}, s32[8,8,8]{2,1,0:T(8,128)}, u32[]{:S(2)}) copy-start(s32[8,8,8]{2,1,0:T(8,128)} %agg_ref.1) | copy-start | bytes 6148
  0.0 4.5 %copy-start.3 = (s32[1,1,8]{2,1,0:T(1,128)S(1)}, s32[1,1,8]{2,1,0:T(1,128)}, u32[]{:S(2)}) copy-start(s32[1,1,8]{2,1,0:T(1,128)} %owner_ref.1) | copy-start | bytes 100
  0.0 6.8 %collective-permute-start.3 = (f32[4,32,128]{2,1,0:T(8,128)}, f32[4,32,128]{2,1,0:T(8,128)S(1)}, u32[]{:S(2)}, u32[]{:S(2)}) collective-permute-start(f32[4,32,128]{2,1,0:T(8,128)} %bitcast.14), channel_id=1, source_target_pairs={{0,8},{2,10},{4,12},{6,14},{8,0},{10,2},{12,4},{14,6},{16,24},{18,... | collective-permute-start | bytes 196616 | tf_op jit(solution)/shard_map/ppermute | solution.py:404
  0.5 6.2 %collective-permute-start.2 = (f32[4,32,128]{2,1,0:T(8,128)}, f32[4,32,128]{2,1,0:T(8,128)S(1)}, u32[]{:S(2)}, u32[]{:S(2)}) collective-permute-start(f32[4,32,128]{2,1,0:T(8,128)} %bitcast.15), channel_id=1, source_target_pairs={{0,2},{2,0},{4,6},{6,4},{8,16},{10,18},{12,20},{14,22},{16,8},{18,... | collective-permute-start | bytes 196616 | tf_op jit(solution)/shard_map/ppermute | solution.py:404
  3.2 4.5 %collective-permute-start.1 = (f32[4,32,128]{2,1,0:T(8,128)}, f32[4,32,128]{2,1,0:T(8,128)S(1)}, u32[]{:S(2)}, u32[]{:S(2)}) collective-permute-start(f32[4,32,128]{2,1,0:T(8,128)} %bitcast.16), channel_id=1, source_target_pairs={{0,2},{2,0},{4,6},{6,4},{8,10},{10,8},{12,14},{14,12},{16,18},{18,... | collective-permute-start | bytes 196616 | tf_op jit(solution)/shard_map/ppermute | solution.py:404
  3.3 4.4 %collective-permute-start = (f32[4,32,128]{2,1,0:T(8,128)}, f32[4,32,128]{2,1,0:T(8,128)S(1)}, u32[]{:S(2)}, u32[]{:S(2)}) collective-permute-start(f32[4,32,128]{2,1,0:T(8,128)} %bitcast.17), channel_id=1, source_target_pairs={{0,8},{2,4},{4,2},{6,14},{8,0},{10,12},{12,10},{14,6},{16,24},{18,... | collective-permute-start | bytes 196616 | tf_op jit(solution)/shard_map/ppermute | solution.py:404
  8.3 4.7 %collective-permute-start.4 = (f32[200,128]{1,0:T(8,128)S(1)}, f32[200,128]{1,0:T(8,128)S(1)}, u32[]{:S(2)}, u32[]{:S(2)}) collective-permute-start(f32[200,128]{1,0:T(8,128)S(1)} %shard_map.48.send_ref), channel_id=1, source_target_pairs={{0,1},{1,0},{2,3},{3,2},{4,5},{5,4},{6,7},{7,6},{8,9},{9,8},{10,11... | collective-permute-start | bytes 307208 | tf_op jit(solution)/shard_map/ppermute | solution.py:441

commit v7 on v6

--- a/solution.py
+++ b/solution.py
@@ -101,10 +101,11 @@
 
 
 def local_kernel(shape, group_size, agg_ref, owner_ref, prolong_ref, fine_ref, tick_ref,
-                 outer_ref, inner_ref, label_ref, layer_ref, layer_send, rows_scr, blocks_scr):
+                 outer_ref, inner_ref, layer_ref, *refs):
     bx, by, bz = shape
     columns = bx * by
     rows_each = AGGS // group_size
+    sends, (rows_scr, blocks_scr) = refs[:-2], refs[-2:]
     gx, gy, gz = lax.axis_index("gx"), lax.axis_index("gy"), lax.axis_index("gz")
     nx, ny, nz = agg_ref.shape
 
@@ -158,11 +159,12 @@
     low = rows_of([rows_scr[xy * FACES + 5, :CDOF] for xy in range(columns)])
     high = rows_of([rows_scr[xy * FACES + 6, DOF - CDOF :] for xy in range(columns)])
     layers = [jnp.where(gz == 0, high, low)] if group_size == 2 else [low, high]
+    layer_parts = []
     for i, layer in enumerate(layers):
         layer_ref[i] = layer
         both = layer[:, :LANES].astype(F32) + layer[:, LANES:].astype(F32)
-        layer_send[i * DOF : i * DOF + DOF // 2] = folded(both + pltpu.roll(both, DOF, 1))
-        layer_send[i * DOF + DOF // 2 : (i + 1) * DOF] = folded(blocks_scr[columns + i])
+        for part in (both + pltpu.roll(both, DOF, 1), blocks_scr[columns + i]):
+            layer_parts.append(folded(part))
 
     aggs = (agg_ref[...] + 1).reshape(nx * ny, nz).astype(F32).astype(BF16)
     width = 5 * LANES
@@ -229,7 +231,7 @@
     label = by_column(outer_base + owner * (AGGS * AGGS), 3) + (other - 1) * AGGS
     label += (1 - gz) * AGGS * AGGS if group_size == 2 else jnp.where(first_half, 0, AGGS * AGGS)
     outer_labels.append(jnp.where(other > 0, label, -1))
-    label_ref[...] = rows_of(outer_labels + [jnp.full((3, LANES), -1, jnp.int32)]).astype(F32)
+    outer_labels = rows_of(outer_labels + [jnp.full((3, LANES), -1, jnp.int32)]).astype(F32)
 
     pieces = [[] for _ in range(5)]
     for x in range(bx):
@@ -250,11 +252,16 @@
     flat = flatten(packs)
     chosen = [choose(label, 0, AGGS * AGGS) for label in labels]
     inner_ref[...] = dot(lanes_of([c for c in chosen for _ in range(2)]), rows_of(flat))
-
-
-def outer_kernel(group_size, outer_ref, inner_ref, label_ref, layer_send, odd_y, even_y, odd_x, even_x, *refs):
-    gz = lax.axis_index("gz")
-    sends, blocks_scr = refs[:-1], refs[-1]
+    count = AGGS * AGGS // group_size
+    for shift, send in enumerate(sends, 1):
+        target = lax.rem(gz + shift, group_size)
+        block = inner_ref[pl.ds(pl.multiple_of(target * count, count), count)]
+        send[:count] = block[:, :LANES]
+        send[count : 2 * count] = block[:, LANES:]
+        send[2 * count :] = rows_of([outer_labels] + layer_parts)
+
+
+def outer_kernel(outer_ref, odd_y, even_y, odd_x, even_x, packs_ref, blocks_scr):
     place = 0
     for axis, even, odd, low, high in (("gx", even_x, odd_x, (2, 3), (0, 1)), ("gy", even_y, odd_y, (1, 3), (0, 2))):
         second = lax.rem(lax.axis_index(axis), 2) == 1
@@ -265,65 +272,30 @@
                 place += 1
     pieces = [diagonal(blocks_of(outer_ref[i], factor_of(blocks_scr[i])), 0) for i in range(8)]
     half = iota((CDOF, LANES), 1) < DOF
-    packs = [jnp.where(half, pieces[i], pieces[i + 1]) for i in range(0, len(pieces), 2)]
-    tail = rows_of(packs + [label_ref[...], layer_send[...]])
-    count = AGGS * AGGS // group_size
-    for shift, send in enumerate(sends, 1):
-        target = lax.rem(gz + shift, group_size)
-        block = inner_ref[pl.ds(pl.multiple_of(target * count, count), count)]
-        send[:count] = block[:, :LANES]
-        send[count : 2 * count] = block[:, LANES:]
-        send[2 * count :] = tail
+    packs_ref[...] = rows_of([jnp.where(half, pieces[i], pieces[i + 1]) for i in range(0, 8, 2)])
 
 
 def parts_of(tail):
-    packs = [tail[k * CDOF : (k + 1) * CDOF] for k in range(4)]
-    labels = tail[DOF : DOF + 8].astype(jnp.int32)
-    halves = [tail[at : at + DOF // 2] for at in range(DOF + 8, tail.shape[0], DOF // 2)]
-    return packs, labels, halves[::2], halves[1::2]
-
-
-def own_kernel(group_size, inner_ref, send_ref, out_ref, factor_ref):
+    halves = [tail[at : at + DOF // 2] for at in range(8, tail.shape[0], DOF // 2)]
+    return tail[:8].astype(jnp.int32), halves[::2], halves[1::2]
+
+
+def own_kernel(group_size, inner_ref, layer_ref, send_ref, packs_ref, *refs):
+    received, out_ref = refs[:-1], refs[-1]
     gz = lax.axis_index("gz")
     rows_each = AGGS // group_size
     count = AGGS * AGGS // group_size
-    mine = iota((AGGS, WIDE), 0) // rows_each == gz
-    block = inner_ref[pl.ds(pl.multiple_of(gz * count, count), count)]
-    for c in range(AGGS):
-        part = rows_of([block[c * rows_each : (c + 1) * rows_each]] * group_size)
-        out_ref[:, c * WIDE : (c + 1) * WIDE] = jnp.where(mine, part, 0.0)
-    packs, labels, _, blocks = parts_of(send_ref[2 * count :])
-    for i, part in enumerate(blocks):
-        factor_ref[i] = factor_of(unfolded(part))
-    for k, flat in enumerate(flatten(packs)):
-        chosen = choose(labels[k : k + 1], gz * AGGS * AGGS, AGGS * AGGS)
-        value = dot(lanes_of([chosen] * 2), flat)
-        for c in range(AGGS):
-            at = ((k + 1) * AGGS + c) * WIDE
-            out_ref[:, at : at + WIDE] = value[c * AGGS : (c + 1) * AGGS]
-    out_ref[:, 5 * AGGS * WIDE :] = jnp.zeros((AGGS, 2 * AGGS * WIDE), F32)
-
-
-def final_kernel(group_size, own_ref, factor_ref, layer_ref, label_ref, *refs):
-    received, out_hbm, out_ref, sems = refs[:-3], refs[-3], refs[-2], refs[-1]
-    gz = lax.axis_index("gz")
-    rows_each = AGGS // group_size
-    count = AGGS * AGGS // group_size
-    copies = []
-
-    def send_out(face):
-        part = pl.ds(face * AGGS * WIDE, AGGS * WIDE)
-        copies.append(pltpu.make_async_copy(out_ref.at[:, part], out_hbm.at[:, part], sems.at[face]))
-        copies[-1].start()
-
+    size = AGGS * AGGS
+    own_labels, _, own_blocks = parts_of(send_ref[2 * count :])
     tails = [parts_of(ref[2 * count :]) for ref in received]
+
     left = iota((DOF, LANES), 1) < DOF
     rows = [[layer_ref[i] for i in range(layer_ref.shape[0])]]
-    factors = [[factor_ref[i] for i in range(layer_ref.shape[0])]]
-    for _, _, layers, blocks in tails:
+    factors = [[factor_of(unfolded(part)) for part in own_blocks]]
+    for _, layers, blocks in tails:
         rows.append([lanes_of(split(jnp.where(left, unfolded(layer), 0.0))) for layer in layers])
         factors.append([factor_of(unfolded(part)) for part in blocks])
-    layer_labels = [label_ref[4:5].astype(jnp.int32)] + [labels[4:5] for _, labels, _, _ in tails]
+    layer_labels = [own_labels[4:5]] + [labels[4:5] for labels, _, _ in tails]
     half = iota((CDOF, LANES), 1) < DOF
     if group_size == 2:
         pieces = [diagonal(blocks_of(rows[i][0], factors[1 - i][0]), 0) for i in range(2)]
@@ -337,34 +309,56 @@
             low[above] = diagonal(blocks_of(rows[above][0], factors[i][1]), 0)
         layer_packs = [jnp.where(half, low[i], high[i]) for i in range(group_size)]
 
+    flat = flatten([packs_ref[k * CDOF : (k + 1) * CDOF] for k in range(4)] + layer_packs)
+    for k in range(4):
+        chosen = choose(own_labels[k : k + 1], gz * size, size)
+        value = dot(lanes_of([chosen] * 2), flat[k])
+        for c in range(AGGS):
+            at = ((k + 1) * AGGS + c) * WIDE
+            out_ref[:, at : at + WIDE] = value[c * AGGS : (c + 1) * AGGS]
+    chosen = [choose(label, gz * 2 * size, 2 * size) for label in layer_labels]
+    value = dot(lanes_of([c for c in chosen for _ in range(2)]), rows_of(flat[4:]))
+    for c in range(2 * AGGS):
+        at = (5 * AGGS + c) * WIDE
+        out_ref[:, at : at + WIDE] = value[c * AGGS : (c + 1) * AGGS]
+
+    block = inner_ref[pl.ds(pl.multiple_of(gz * count, count), count)]
     brick = iota((AGGS, LANES), 0) // rows_each
     for c in range(AGGS):
+        at = slice(c * rows_each, (c + 1) * rows_each)
         for h in range(2):
-            at = slice((2 * c + h) * LANES, (2 * c + h + 1) * LANES)
-            value = own_ref[:, at]
+            value = rows_of([block[at, h * LANES : (h + 1) * LANES]] * group_size)
             for shift, ref in enumerate(received, 1):
                 part = ref[h * count + c * rows_each : h * count + (c + 1) * rows_each]
                 theirs = lax.rem(gz - shift + group_size, group_size)
                 value = jnp.where(brick == theirs, rows_of([part] * group_size), value)
-            out_ref[:, at] = value
-    send_out(0)
-    flat = flatten([packs[k] for k in range(4) for packs, _, _, _ in tails]) + flatten(layer_packs)
+            out_ref[:, (2 * c + h) * LANES : (2 * c + h + 1) * LANES] = value
+
+
+def final_kernel(group_size, own_ref, *refs):
+    packs, firsts, (out_hbm, out_ref, sems) = refs[: group_size - 1], refs[group_size - 1 : -3], refs[-3:]
+    gz = lax.axis_index("gz")
+    count = AGGS * AGGS // group_size
     size = AGGS * AGGS
+    copies = []
+
+    def send_out(source, first, last):
+        part = pl.ds(first * AGGS * WIDE, (last - first) * AGGS * WIDE)
+        copies.append(pltpu.make_async_copy(source.at[:, part], out_hbm.at[:, part], sems.at[first]))
+        copies[-1].start()
+
+    send_out(own_ref, 0, 1)
+    send_out(own_ref, 5, 7)
+    flat = flatten([pack[k * CDOF : (k + 1) * CDOF] for k in range(4) for pack in packs])
+    labels = [ref[2 * count : 2 * count + 8].astype(jnp.int32) for ref in firsts]
     for k in range(4):
-        chosen = [choose(labels[k : k + 1], gz * size, size) for _, labels, _, _ in tails]
-        parts = flat[k * len(tails) : (k + 1) * len(tails)]
+        chosen = [choose(label[k : k + 1], gz * size, size) for label in labels]
+        parts = flat[k * len(packs) : (k + 1) * len(packs)]
         value = dot(lanes_of([c for c in chosen for _ in range(2)]), rows_of(parts))
         for c in range(AGGS):
             cut = slice(((k + 1) * AGGS + c) * WIDE, ((k + 1) * AGGS + c + 1) * WIDE)
             out_ref[:, cut] = own_ref[:, cut] + value[c * AGGS : (c + 1) * AGGS]
-        send_out(k + 1)
-    chosen = [choose(label, gz * 2 * size, 2 * size) for label in layer_labels]
-    value = dot(lanes_of([c for c in chosen for _ in range(2)]), rows_of(flat[4 * len(tails) :]))
-    for c in range(2 * AGGS):
-        cut = slice((5 * AGGS + c) * WIDE, (5 * AGGS + c + 1) * WIDE)
-        out_ref[:, cut] = value[c * AGGS : (c + 1) * AGGS]
-    send_out(5)
-    send_out(6)
+        send_out(out_ref, k + 1, k + 2)
     for copy in copies:
         copy.wait()
 
@@ -407,17 +401,17 @@
     layers = 1 if group_size == 2 else 2
     params = pltpu.CompilerParams(vmem_limit_bytes=32 * 1024 * 1024)
     shape = jax.ShapeDtypeStruct
-    outer, inner, labels, layer_rows, layer_send = pl.pallas_call(
+    size = 2 * AGGS * AGGS // group_size + 8 + layers * DOF
+    outer, inner, layer_rows, *firsts = pl.pallas_call(
         functools.partial(local_kernel, (bx, by, bz), group_size),
         out_shape=[
             shape((8, DOF, WIDE), BF16),
             shape((AGGS * AGGS, WIDE), F32),
-            shape((8, LANES), F32),
             shape((layers, DOF, WIDE), BF16),
-            shape((layers * DOF, LANES), F32),
-        ],
+        ]
+        + [shape((size, LANES), F32)] * (group_size - 1),
         in_specs=[VMEM] * 5,
-        out_specs=[VMEM] * 5,
+        out_specs=[VMEM] * (2 + group_size),
         scratch_shapes=[
             pltpu.VMEM((columns * FACES, DOF, WIDE), BF16),
             pltpu.VMEM((columns + layers, DOF, LANES), F32),
@@ -428,35 +422,35 @@
         *(pltpu.with_memory_space_constraint(a, pltpu.VMEM) for a in (agg_map, owner_map, base, fine)),
         tick,
     )
-    size = 2 * AGGS * AGGS // group_size + 4 * CDOF + 8 + layers * DOF
-    sends = pl.pallas_call(
-        functools.partial(outer_kernel, group_size),
-        out_shape=[shape((size, LANES), F32)] * (group_size - 1),
-        in_specs=[VMEM] * 8,
-        out_specs=[VMEM] * (group_size - 1),
+    shifts = range(1, group_size)
+    others = [lax.ppermute(first, "gz", rotation(group_size, shift)) for shift, first in zip(shifts, firsts)]
+    packs = pl.pallas_call(
+        outer_kernel,
+        out_shape=shape((4 * CDOF, LANES), F32),
+        in_specs=[VMEM] * 5,
+        out_specs=VMEM,
         scratch_shapes=[pltpu.VMEM((8, DOF, LANES), F32)],
         compiler_params=params,
-    )(outer, inner, labels, layer_send, *halos)
-    received = [
-        lax.ppermute(send, "gz", rotation(group_size, shift)) for shift, send in enumerate(sends, 1)
-    ]
+        cost_estimate=pl.CostEstimate(flops=int(5e10), bytes_accessed=int(5e7), transcendentals=0),
+    )(outer, *halos)
+    received = [lax.ppermute(packs, "gz", rotation(group_size, shift)) for shift in shifts]
     full = shape((AGGS, FACES * AGGS * CDOF * CDOF), F32)
-    own, factor = pl.pallas_call(
+    own = pl.pallas_call(
         functools.partial(own_kernel, group_size),
-        out_shape=[full, shape((layers, WIDE, LANES), BF16)],
-        in_specs=[VMEM, VMEM],
-        out_specs=[VMEM, VMEM],
+        out_shape=full,
+        in_specs=[VMEM] * (3 + group_size),
+        out_specs=VMEM,
         compiler_params=params,
         cost_estimate=pl.CostEstimate(flops=int(1e9), bytes_accessed=int(2e6), transcendentals=0),
-    )(inner, sends[0])
+    )(inner, layer_rows, firsts[0], packs, *others)
     out = pl.pallas_call(
         functools.partial(final_kernel, group_size),
         out_shape=full,
-        in_specs=[VMEM] * (3 + group_size),
+        in_specs=[VMEM] * (2 * group_size - 1),
         out_specs=HBM,
         scratch_shapes=[pltpu.VMEM(full.shape, F32), pltpu.SemaphoreType.DMA((FACES,))],
         compiler_params=params,
-    )(own, factor, layer_rows, labels, *received)
+    )(own, *received, *others)
     return out[None, None]
 
 

time: 14.7 us -> 14.4 us (0.980)
  waiting for transfers between devices: 3.5 us -> 2.33 us
  starting transfers between devices: 6.09 us -> 6.93 us
    ppermute x4, waiting for transfers between devices: 0.88 us -> 0.01 us  [shards(): lax.ppermute(base, ('gx', 'gy'), matching(sizes, along, first))]
    ppermute x1 -> x2, starting transfers between devices: 1.59 us -> 2.43 us  [the longest x1 1.58 us: shards(): lax.ppermute(first, 'gz', rotation(group_size, shift))]
    pallas_call x2, Pallas kernels: 1.17 us -> 1.47 us  [the longest x1 0.8 us: shards(): pl.pallas_call(functools.partial(own_kernel, group_size), out_shape=full,...]
    ppermute x1 -> x2, waiting for transfers between devices: 2.62 us -> 2.32 us  [the longest x1 1.25 us: shards(): lax.ppermute(first, 'gz', rotation(group_size, shift))]
    pallas_call x1, Pallas kernels: 1.47 us -> 1.2 us  [shards(): pl.pallas_call(functools.partial(final_kernel, group_size), out_shape=ful...]
  transfers between devices with their start and end apart: 5 -> 6, of which waited for: 2 -> 2; matrix products, arithmetic and copies ran while one was open for 0% -> 0% of each run, Pallas kernels for 19% -> 26%
where the time goes in v7:
time: 14.4 us; the launch traced here: 14.2 us
  starting transfers between devices  6.93 us (48%)
  Pallas kernels  4.92 us (34%)
  waiting for transfers between devices  2.33 us (16%)
    ppermute x4, starting transfers between devices, shards(): lax.ppermute(base, ('gx', 'gy'), matching(sizes, along, first))  4.5 us
    pallas_call x1, Pallas kernels, shards(): pl.pallas_call(functools.partial(local_kernel, (bx, by, bz), group_size),...  2.25 us
    ppermute x1, starting transfers between devices, shards(): lax.ppermute(first, 'gz', rotation(group_size, shift))  1.58 us
    ppermute x1, waiting for transfers between devices, shards(): lax.ppermute(first, 'gz', rotation(group_size, shift))  1.25 us
    pallas_call x1, Pallas kernels, shards(): pl.pallas_call(functools.partial(final_kernel, group_size), out_shape=ful...  1.2 us
    ppermute x1, waiting for transfers between devices, shards(): lax.ppermute(packs, 'gz', rotation(group_size, shift))  1.07 us
    ppermute x1, starting transfers between devices, shards(): lax.ppermute(packs, 'gz', rotation(group_size, shift))  0.85 us
    pallas_call x1, Pallas kernels, shards(): pl.pallas_call(functools.partial(own_kernel, group_size), out_shape=full,...  0.8 us
  transfers between devices with their start and end apart: 6, of which 2 were waited for; matrix products, arithmetic and copies ran while one was open for 0% of the time, Pallas kernels for 26%

profile of v7, /device:TPU:0, one launch (start us, length us, event | category | flops | bytes accessed | tf_op | source)
XLA Modules:
  0.0 14.2 jit_solution(15669247746265814950)
XLA Ops:
  0.0 0.0 copy-start
  0.0 0.0 copy-start.1
  0.0 0.0 copy-start.2
  0.0 0.0 copy-start.3
  0.0 0.5 %collective-permute-start.3 = (f32[4,32,128]{2,1,0:T(8,128)}, f32[4,32,128]{2,1,0:T(8,128)S(1)}, u32[]{:S(2)}, u32[]{:S(2)}) collective-permute-start(f32[4,32,128]{2,1,0:T(8,128)} %bitcast.14), channel_id=1, source_target_pairs={{0,8},{2,10},{4,12},{6,14},{8,0},{10,2},{12,4},{14,6},{16,24},{18,... | collective-permute-start | bytes 196616 | tf_op jit(solution)/shard_map/ppermute | solution.py:398
  0.5 2.6 %collective-permute-start.2 = (f32[4,32,128]{2,1,0:T(8,128)}, f32[4,32,128]{2,1,0:T(8,128)S(1)}, u32[]{:S(2)}, u32[]{:S(2)}) collective-permute-start(f32[4,32,128]{2,1,0:T(8,128)} %bitcast.15), channel_id=1, source_target_pairs={{0,2},{2,0},{4,6},{6,4},{8,16},{10,18},{12,20},{14,22},{16,8},{18,... | collective-permute-start | bytes 196616 | tf_op jit(solution)/shard_map/ppermute | solution.py:398
  3.2 0.1 collective-permute-start.1
  3.3 1.2 %collective-permute-start = (f32[4,32,128]{2,1,0:T(8,128)}, f32[4,32,128]{2,1,0:T(8,128)S(1)}, u32[]{:S(2)}, u32[]{:S(2)}) collective-permute-start(f32[4,32,128]{2,1,0:T(8,128)} %bitcast.17), channel_id=1, source_target_pairs={{0,8},{2,4},{4,2},{6,14},{8,0},{10,12},{12,10},{14,6},{16,24},{18,... | collective-permute-start | bytes 196616 | tf_op jit(solution)/shard_map/ppermute | solution.py:398
  4.5 0.0 copy-done
  4.5 0.0 copy-done.1
  4.5 0.0 copy-done.2
  4.5 0.0 copy-done.3
  4.5 2.2 %shard_map.47 = (bf16[8,64,256]{2,1,0:T(8,128)(2,1)S(1)}, f32[64,256]{1,0:T(8,128)S(1)}, bf16[1,64,256]{2,1,0:T(8,128)(2,1)S(1)}, f32[136,128]{1,0:T(8,128)S(1)}) custom-call(s32[8,8,8]{2,1,0:T(8,128)S(1)} %copy-done.2, s32[1,1,8]{2,1,0:T(1,128)S(1)} %copy-done.3, f32[4,32,128]{2,1,0:T(8,128)S(1)} %bitcast.18, f32[28,128,128]{2,1,0:T(8,128)S(1)} %bitcast.13, ...), custom_call_target="tpu_custom_call" | custom-call | flops 2000000000 | bytes 4000000 | tf_op jit(solution)/shard_map/pallas_call | solution.py:405
  6.8 1.6 %collective-permute-start.4 = (f32[136,128]{1,0:T(8,128)S(1)}, f32[136,128]{1,0:T(8,128)S(1)}, u32[]{:S(2)}, u32[]{:S(2)}) collective-permute-start(f32[136,128]{1,0:T(8,128)S(1)} %get-tuple-element.11.send_ref), channel_id=1, source_target_pairs={{0,1},{1,0},{2,3},{3,2},{4,5},{5,4},{6,7},{7,6},{8,9},{9,8},{10,11... | collective-permute-start | bytes 208904 | tf_op jit(solution)/shard_map/ppermute | solution.py:426
  8.4 0.0 collective-permute-done.3.even_x
  8.4 0.0 collective-permute-done.2.odd_x
  8.4 0.0 collective-permute-done.1.even_y
  8.4 0.0 collective-permute-done.odd_y
  8.4 0.7 %shard_map.48.packs_ref = f32[64,128]{1,0:T(8,128)S(1)} custom-call(bf16[8,64,256]{2,1,0:T(8,128)(2,1)S(1)} %get-tuple-element.12.outer_ref, f32[4,32,128]{2,1,0:T(8,128)S(1)} %collective-permute-done.odd_y, f32[4,32,128]{2,1,0:T(8,128)S(1)} %collective-permute-done.1.even_y, f32[4,32,128]{2,1,0:T(8,128)S(1)} %collective-permute-done.2.odd_x, ...), custom_call_target="tpu_custom_call" | custom-call | flops 49999998976 | bytes 50000000 | tf_op jit(solution)/shard_map/pallas_call | solution.py:427
  9.1 0.8 %collective-permute-start.5 = (f32[64,128]{1,0:T(8,128)S(1)}, f32[64,128]{1,0:T(8,128)S(1)}, u32[]{:S(2)}, u32[]{:S(2)}) collective-permute-start(f32[64,128]{1,0:T(8,128)S(1)} %shard_map.48.packs_ref), channel_id=1, source_target_pairs={{0,1},{1,0},{2,3},{3,2},{4,5},{5,4},{6,7},{7,6},{8,9},{9,8},{10,11... | collective-permute-start | bytes 98312 | tf_op jit(solution)/shard_map/ppermute | solution.py:436
  9.9 1.3 %collective-permute-done.4.refs_0_.refs_1_ = f32[136,128]{1,0:T(8,128)S(1)} collective-permute-done((f32[136,128]{1,0:T(8,128)S(1)}, f32[136,128]{1,0:T(8,128)S(1)}, u32[]{:S(2)}, u32[]{:S(2)}) %collective-permute-start.4) | collective-permute-done | bytes 69664 | tf_op jit(solution)/shard_map/ppermute | solution.py:426
  11.2 0.8 %shard_map.49.own_ref = f32[8,14336]{1,0:T(8,128)S(1)} custom-call(f32[64,256]{1,0:T(8,128)S(1)} %get-tuple-element.9.inner_ref, bf16[1,64,256]{2,1,0:T(8,128)(2,1)S(1)} %get-tuple-element.10.layer_ref, f32[136,128]{1,0:T(8,128)S(1)} %get-tuple-element.11.send_ref, f32[64,128]{1,0:T(8,128)S(1)} %shard_map.48.packs_ref, ...), custom_call_target="tpu_custom_call" | custom-call | flops 1000000000 | bytes 2000000 | tf_op jit(solution)/shard_map/pallas_call | solution.py:438
  12.0 1.1 %collective-permute-done.5.refs_0_ = f32[64,128]{1,0:T(8,128)S(1)} collective-permute-done((f32[64,128]{1,0:T(8,128)S(1)}, f32[64,128]{1,0:T(8,128)S(1)}, u32[]{:S(2)}, u32[]{:S(2)}) %collective-permute-start.5) | collective-permute-done | bytes 32800 | tf_op jit(solution)/shard_map/ppermute | solution.py:436
  13.0 1.2 %shard_map.50 = f32[8,14336]{1,0:T(8,128)} custom-call(f32[8,14336]{1,0:T(8,128)S(1)} %shard_map.49.own_ref, f32[64,128]{1,0:T(8,128)S(1)} %collective-permute-done.5.refs_0_, f32[136,128]{1,0:T(8,128)S(1)} %collective-permute-done.4.refs_0_.refs_1_), custom_call_target="tpu_custom_call" | custom-call | tf_op jit(solution)/shard_map/pallas_call | solution.py:446
  (1 shorter events, 0.0 us)
Async XLA Ops:
  0.0 4.5 %copy-start = (f32[2,2,4,7,4096]{4,2,3,1,0:T(4,128)S(1)}, f32[2,2,4,7,4096]{4,2,3,1,0:T(4,128)}, u32[]{:S(2)}) copy-start(f32[2,2,4,7,4096]{4,2,3,1,0:T(4,128)} %param.4) | copy-start | bytes 5505028
  0.0 4.5 %copy-start.1 = (f32[2,2,4,1024]{3,2,1,0:T(4,128)S(1)}, f32[2,2,4,1024]{3,2,1,0:T(4,128)}, u32[]{:S(2)}) copy-start(f32[2,2,4,1024]{3,2,1,0:T(4,128)} %param.5) | copy-start | bytes 196612
  0.0 4.5 %copy-start.2 = (s32[8,8,8]{2,1,0:T(8,128)S(1)}, s32[8,8,8]{2,1,0:T(8,128)}, u32[]{:S(2)}) copy-start(s32[8,8,8]{2,1,0:T(8,128)} %agg_ref.1) | copy-start | bytes 6148
  0.0 4.5 %copy-start.3 = (s32[1,1,8]{2,1,0:T(1,128)S(1)}, s32[1,1,8]{2,1,0:T(1,128)}, u32[]{:S(2)}) copy-start(s32[1,1,8]{2,1,0:T(1,128)} %owner_ref.1) | copy-start | bytes 100
  0.0 8.4 %collective-permute-start.3 = (f32[4,32,128]{2,1,0:T(8,128)}, f32[4,32,128]{2,1,0:T(8,128)S(1)}, u32[]{:S(2)}, u32[]{:S(2)}) collective-permute-start(f32[4,32,128]{2,1,0:T(8,128)} %bitcast.14), channel_id=1, source_target_pairs={{0,8},{2,10},{4,12},{6,14},{8,0},{10,2},{12,4},{14,6},{16,24},{18,... | collective-permute-start | bytes 196616 | tf_op jit(solution)/shard_map/ppermute | solution.py:398
  0.5 7.8 %collective-permute-start.2 = (f32[4,32,128]{2,1,0:T(8,128)}, f32[4,32,128]{2,1,0:T(8,128)S(1)}, u32[]{:S(2)}, u32[]{:S(2)}) collective-permute-start(f32[4,32,128]{2,1,0:T(8,128)} %bitcast.15), channel_id=1, source_target_pairs={{0,2},{2,0},{4,6},{6,4},{8,16},{10,18},{12,20},{14,22},{16,8},{18,... | collective-permute-start | bytes 196616 | tf_op jit(solution)/shard_map/ppermute | solution.py:398
  3.2 5.2 %collective-permute-start.1 = (f32[4,32,128]{2,1,0:T(8,128)}, f32[4,32,128]{2,1,0:T(8,128)S(1)}, u32[]{:S(2)}, u32[]{:S(2)}) collective-permute-start(f32[4,32,128]{2,1,0:T(8,128)} %bitcast.16), channel_id=1, source_target_pairs={{0,2},{2,0},{4,6},{6,4},{8,10},{10,8},{12,14},{14,12},{16,18},{18,... | collective-permute-start | bytes 196616 | tf_op jit(solution)/shard_map/ppermute | solution.py:398
  3.3 5.1 %collective-permute-start = (f32[4,32,128]{2,1,0:T(8,128)}, f32[4,32,128]{2,1,0:T(8,128)S(1)}, u32[]{:S(2)}, u32[]{:S(2)}) collective-permute-start(f32[4,32,128]{2,1,0:T(8,128)} %bitcast.17), channel_id=1, source_target_pairs={{0,8},{2,4},{4,2},{6,14},{8,0},{10,12},{12,10},{14,6},{16,24},{18,... | collective-permute-start | bytes 196616 | tf_op jit(solution)/shard_map/ppermute | solution.py:398
  6.8 4.4 %collective-permute-start.4 = (f32[136,128]{1,0:T(8,128)S(1)}, f32[136,128]{1,0:T(8,128)S(1)}, u32[]{:S(2)}, u32[]{:S(2)}) collective-permute-start(f32[136,128]{1,0:T(8,128)S(1)} %get-tuple-element.11.send_ref), channel_id=1, source_target_pairs={{0,1},{1,0},{2,3},{3,2},{4,5},{5,4},{6,7},{7,6},{8,9},{9,8},{10,11... | collective-permute-start | bytes 208904 | tf_op jit(solution)/shard_map/ppermute | solution.py:426
  9.1 4.0 %collective-permute-start.5 = (f32[64,128]{1,0:T(8,128)S(1)}, f32[64,128]{1,0:T(8,128)S(1)}, u32[]{:S(2)}, u32[]{:S(2)}) collective-permute-start(f32[64,128]{1,0:T(8,128)S(1)} %shard_map.48.packs_ref), channel_id=1, source_target_pairs={{0,1},{1,0},{2,3},{3,2},{4,5},{5,4},{6,7},{7,6},{8,9},{9,8},{10,11... | collective-permute-start | bytes 98312 | tf_op jit(solution)/shard_map/ppermute | solution.py:436

commit v8 on v7

--- a/solution.py
+++ b/solution.py
@@ -84,12 +84,15 @@
 
 
 def flatten(packs):
-    spread = ones_where(iota((LANES, WIDE), 0) % CDOF == iota((LANES, WIDE), 1) % CDOF)
-    element = ones_where(iota((LANES, LANES), 0) // CDOF == iota((LANES, LANES), 1) // CDOF)
-    row = ones_where(iota((WIDE, WIDE), 0) % CDOF == iota((WIDE, WIDE), 1) // CDOF)
-    wide = [rows_of([part] * 8) * element for pack in packs for part in split(pack)]
-    flat = dot(rows_of(wide), spread).astype(BF16)
-    return [flat[i * WIDE : (i + 1) * WIDE] * row for i in range(len(packs))]
+    spread = ones_where(iota((WIDE, WIDE), 0) % CDOF == iota((WIDE, WIDE), 1) % CDOF)
+    element = ones_where(iota((LANES, WIDE), 0) // CDOF == iota((LANES, WIDE), 1) // CDOF % 8)
+    row = iota((LANES, WIDE), 0) % CDOF == iota((LANES, WIDE), 1) // CDOF
+    wide = [rows_of([lanes_of(split(pack))] * 8) * element for pack in packs]
+    flat = dot(rows_of(wide), spread)
+    out = []
+    for i in range(len(packs)):
+        out.append(rows_of(split(jnp.where(row, flat[i * LANES : (i + 1) * LANES], 0.0))))
+    return out
 
 
 def choose(labels, base, count):
@@ -105,26 +108,19 @@
     bx, by, bz = shape
     columns = bx * by
     rows_each = AGGS // group_size
-    sends, (rows_scr, blocks_scr) = refs[:-2], refs[-2:]
+    sends, (rows_scr, blocks_scr, left_scr) = refs[:-3], refs[-3:]
     gx, gy, gz = lax.axis_index("gx"), lax.axis_index("gy"), lax.axis_index("gz")
     nx, ny, nz = agg_ref.shape
 
-    lane = iota((32, LANES), 1)
-    sub = iota((32, LANES), 0) % 4
-    p0, p1 = iota((LANES, LANES), 0), iota((LANES, LANES), 1)
-    permute = ones_where((p0 % 4 == p1 % 4) & (p0 // 32 == p1 // 4 % 4) & (p0 // 4 % 8 == p1 // 16))
-    turned = []
+    band = iota((8, LANES), 1) // 32
+    lefts = []
     for xy in range(columns):
-        raw = prolong_ref[xy]
-        rolled = [raw] + [pltpu.roll(raw, 32 * m, 1) for m in range(1, 4)]
-        stacked = []
-        for tau in range(4):
-            part = jnp.zeros_like(raw)
-            for z in range(4):
-                part = jnp.where((sub == z) & (lane // 32 == z), rolled[(z - tau) % 4], part)
-            stacked.append(part)
-        turned += split(rows_of(stacked).T)
-    lefts = dot(rows_of(turned), permute).astype(BF16)
+        for z in range(bz):
+            piece = prolong_ref[xy, pl.ds(z, 8, stride=bz), :]
+            for tau in range(4):
+                turned = pltpu.roll(piece, 32 * ((z - tau) % 4), 1) if z != tau else piece
+                left_scr[xy, pl.ds(tau * 4 + z, 8, stride=16), :] = jnp.where(band == z, turned, 0.0)
+        lefts.append(split(left_scr[xy].T))
     for xy in range(columns):
         spread_blocks(blocks_scr.at[xy], [prolong_ref[xy, pl.ds(z, 8, stride=bz), :] for z in range(bz)])
     low, high = ([prolong_ref[xy, pl.ds(z, 8, stride=bz), :] for xy in range(columns)] for z in (0, bz - 1))
@@ -135,8 +131,7 @@
 
     wide_lane = iota((4, CDOF, WIDE), 2) % LANES
     for xy in range(columns):
-        high = lefts[xy * WIDE : xy * WIDE + LANES]
-        low = lefts[xy * WIDE + LANES : (xy + 1) * WIDE]
+        high, low = lefts[xy]
         left = rows_of([lanes_of([high, high]), lanes_of([low, jnp.zeros_like(low)])])
         for first in range(0, FACES, 2):
             count = min(2, FACES - first)
@@ -415,6 +410,7 @@
         scratch_shapes=[
             pltpu.VMEM((columns * FACES, DOF, WIDE), BF16),
             pltpu.VMEM((columns + layers, DOF, LANES), F32),
+            pltpu.VMEM((columns, LANES, LANES), F32),
         ],
         compiler_params=params,
         cost_estimate=pl.CostEstimate(flops=int(2e9), bytes_accessed=int(4e6), transcendentals=0),

time: 14.4 us -> 14 us (0.972)
  Pallas kernels: 4.92 us -> 4.45 us
  starting transfers between devices: 6.93 us -> 7.25 us
  waiting for transfers between devices: 2.33 us -> 2.11 us
    ppermute x1, starting transfers between devices: 0.85 us -> 1.16 us  [shards(): lax.ppermute(packs, 'gz', rotation(group_size, shift))]
    pallas_call x1, Pallas kernels: 2.25 us -> 1.93 us  [shards(): pl.pallas_call(functools.partial(local_kernel, (bx, by, bz), group_size),...]
    ppermute x1, waiting for transfers between devices: 1.25 us -> 0.94 us  [shards(): lax.ppermute(first, 'gz', rotation(group_size, shift))]
  transfers between devices with their start and end apart: 6 -> 6, of which waited for: 2 -> 2; matrix products, arithmetic and copies ran while one was open for 0% -> 0% of each run, Pallas kernels for 26% -> 24%
where the time goes in v8:
time: 14 us; the launch traced here: 13.9 us
  starting transfers between devices  7.25 us (52%)
  Pallas kernels  4.45 us (32%)
  waiting for transfers between devices  2.11 us (15%)
    ppermute x4, starting transfers between devices, shards(): lax.ppermute(base, ('gx', 'gy'), matching(sizes, along, first))  4.5 us
    pallas_call x1, Pallas kernels, shards(): pl.pallas_call(functools.partial(local_kernel, (bx, by, bz), group_size),...  1.93 us
    ppermute x1, starting transfers between devices, shards(): lax.ppermute(first, 'gz', rotation(group_size, shift))  1.59 us
    ppermute x1, starting transfers between devices, shards(): lax.ppermute(packs, 'gz', rotation(group_size, shift))  1.16 us
    ppermute x1, waiting for transfers between devices, shards(): lax.ppermute(packs, 'gz', rotation(group_size, shift))  1.16 us
    pallas_call x1, Pallas kernels, shards(): pl.pallas_call(functools.partial(final_kernel, group_size), out_shape=ful...  1.14 us
    ppermute x1, waiting for transfers between devices, shards(): lax.ppermute(first, 'gz', rotation(group_size, shift))  0.94 us
    pallas_call x1, Pallas kernels, shards(): pl.pallas_call(functools.partial(own_kernel, group_size), out_shape=full,...  0.71 us
  transfers between devices with their start and end apart: 6, of which 2 were waited for; matrix products, arithmetic and copies ran while one was open for 0% of the time, Pallas kernels for 24%

profile of v8, /device:TPU:0, one launch (start us, length us, event | category | flops | bytes accessed | tf_op | source)
XLA Modules:
  0.0 13.9 jit_solution(14954281244824519428)
XLA Ops:
  0.0 0.0 copy-start
  0.0 0.0 copy-start.1
  0.0 0.0 copy-start.2
  0.0 0.0 copy-start.3
  0.0 0.5 %collective-permute-start.3 = (f32[4,32,128]{2,1,0:T(8,128)}, f32[4,32,128]{2,1,0:T(8,128)S(1)}, u32[]{:S(2)}, u32[]{:S(2)}) collective-permute-start(f32[4,32,128]{2,1,0:T(8,128)} %bitcast.14), channel_id=1, source_target_pairs={{0,8},{2,10},{4,12},{6,14},{8,0},{10,2},{12,4},{14,6},{16,24},{18,... | collective-permute-start | bytes 196616 | tf_op jit(solution)/shard_map/ppermute | solution.py:393
  0.5 2.6 %collective-permute-start.2 = (f32[4,32,128]{2,1,0:T(8,128)}, f32[4,32,128]{2,1,0:T(8,128)S(1)}, u32[]{:S(2)}, u32[]{:S(2)}) collective-permute-start(f32[4,32,128]{2,1,0:T(8,128)} %bitcast.15), channel_id=1, source_target_pairs={{0,2},{2,0},{4,6},{6,4},{8,16},{10,18},{12,20},{14,22},{16,8},{18,... | collective-permute-start | bytes 196616 | tf_op jit(solution)/shard_map/ppermute | solution.py:393
  3.2 0.1 collective-permute-start.1
  3.3 1.2 %collective-permute-start = (f32[4,32,128]{2,1,0:T(8,128)}, f32[4,32,128]{2,1,0:T(8,128)S(1)}, u32[]{:S(2)}, u32[]{:S(2)}) collective-permute-start(f32[4,32,128]{2,1,0:T(8,128)} %bitcast.17), channel_id=1, source_target_pairs={{0,8},{2,4},{4,2},{6,14},{8,0},{10,12},{12,10},{14,6},{16,24},{18,... | collective-permute-start | bytes 196616 | tf_op jit(solution)/shard_map/ppermute | solution.py:393
  4.5 0.0 copy-done
  4.5 0.0 copy-done.1
  4.5 0.0 copy-done.2
  4.5 0.0 copy-done.3
  4.5 1.9 %shard_map.47 = (bf16[8,64,256]{2,1,0:T(8,128)(2,1)S(1)}, f32[64,256]{1,0:T(8,128)S(1)}, bf16[1,64,256]{2,1,0:T(8,128)(2,1)S(1)}, f32[136,128]{1,0:T(8,128)S(1)}) custom-call(s32[8,8,8]{2,1,0:T(8,128)S(1)} %copy-done.2, s32[1,1,8]{2,1,0:T(1,128)S(1)} %copy-done.3, f32[4,32,128]{2,1,0:T(8,128)S(1)} %bitcast.18, f32[28,128,128]{2,1,0:T(8,128)S(1)} %bitcast.13, ...), custom_call_target="tpu_custom_call" | custom-call | flops 2000000000 | bytes 4000000 | tf_op jit(solution)/shard_map/pallas_call | solution.py:400
  6.5 1.6 %collective-permute-start.4 = (f32[136,128]{1,0:T(8,128)S(1)}, f32[136,128]{1,0:T(8,128)S(1)}, u32[]{:S(2)}, u32[]{:S(2)}) collective-permute-start(f32[136,128]{1,0:T(8,128)S(1)} %get-tuple-element.11.send_ref), channel_id=1, source_target_pairs={{0,1},{1,0},{2,3},{3,2},{4,5},{5,4},{6,7},{7,6},{8,9},{9,8},{10,11... | collective-permute-start | bytes 208904 | tf_op jit(solution)/shard_map/ppermute | solution.py:422
  8.1 0.0 collective-permute-done.3.even_x
  8.1 0.0 collective-permute-done.2.odd_x
  8.1 0.0 collective-permute-done.1.even_y
  8.1 0.0 collective-permute-done.odd_y
  8.1 0.7 %shard_map.48.packs_ref = f32[64,128]{1,0:T(8,128)S(1)} custom-call(bf16[8,64,256]{2,1,0:T(8,128)(2,1)S(1)} %get-tuple-element.12.outer_ref, f32[4,32,128]{2,1,0:T(8,128)S(1)} %collective-permute-done.odd_y, f32[4,32,128]{2,1,0:T(8,128)S(1)} %collective-permute-done.1.even_y, f32[4,32,128]{2,1,0:T(8,128)S(1)} %collective-permute-done.2.odd_x, ...), custom_call_target="tpu_custom_call" | custom-call | flops 49999998976 | bytes 50000000 | tf_op jit(solution)/shard_map/pallas_call | solution.py:423
  8.7 1.2 %collective-permute-start.5 = (f32[64,128]{1,0:T(8,128)S(1)}, f32[64,128]{1,0:T(8,128)S(1)}, u32[]{:S(2)}, u32[]{:S(2)}) collective-permute-start(f32[64,128]{1,0:T(8,128)S(1)} %shard_map.48.packs_ref), channel_id=1, source_target_pairs={{0,1},{1,0},{2,3},{3,2},{4,5},{5,4},{6,7},{7,6},{8,9},{9,8},{10,11... | collective-permute-start | bytes 98312 | tf_op jit(solution)/shard_map/ppermute | solution.py:432
  9.9 0.9 %collective-permute-done.4.refs_0_.refs_1_ = f32[136,128]{1,0:T(8,128)S(1)} collective-permute-done((f32[136,128]{1,0:T(8,128)S(1)}, f32[136,128]{1,0:T(8,128)S(1)}, u32[]{:S(2)}, u32[]{:S(2)}) %collective-permute-start.4) | collective-permute-done | bytes 69664 | tf_op jit(solution)/shard_map/ppermute | solution.py:422
  10.9 0.7 %shard_map.49.own_ref = f32[8,14336]{1,0:T(8,128)S(1)} custom-call(f32[64,256]{1,0:T(8,128)S(1)} %get-tuple-element.9.inner_ref, bf16[1,64,256]{2,1,0:T(8,128)(2,1)S(1)} %get-tuple-element.10.layer_ref, f32[136,128]{1,0:T(8,128)S(1)} %get-tuple-element.11.send_ref, f32[64,128]{1,0:T(8,128)S(1)} %shard_map.48.packs_ref, ...), custom_call_target="tpu_custom_call" | custom-call | flops 1000000000 | bytes 2000000 | tf_op jit(solution)/shard_map/pallas_call | solution.py:434
  11.6 1.2 %collective-permute-done.5.refs_0_ = f32[64,128]{1,0:T(8,128)S(1)} collective-permute-done((f32[64,128]{1,0:T(8,128)S(1)}, f32[64,128]{1,0:T(8,128)S(1)}, u32[]{:S(2)}, u32[]{:S(2)}) %collective-permute-start.5) | collective-permute-done | bytes 32800 | tf_op jit(solution)/shard_map/ppermute | solution.py:432
  12.7 1.1 %shard_map.50 = f32[8,14336]{1,0:T(8,128)} custom-call(f32[8,14336]{1,0:T(8,128)S(1)} %shard_map.49.own_ref, f32[64,128]{1,0:T(8,128)S(1)} %collective-permute-done.5.refs_0_, f32[136,128]{1,0:T(8,128)S(1)} %collective-permute-done.4.refs_0_.refs_1_), custom_call_target="tpu_custom_call" | custom-call | tf_op jit(solution)/shard_map/pallas_call | solution.py:442
  (1 shorter events, 0.0 us)
Async XLA Ops:
  0.0 4.5 %copy-start = (f32[2,2,4,7,4096]{4,2,3,1,0:T(4,128)S(1)}, f32[2,2,4,7,4096]{4,2,3,1,0:T(4,128)}, u32[]{:S(2)}) copy-start(f32[2,2,4,7,4096]{4,2,3,1,0:T(4,128)} %param.4) | copy-start | bytes 5505028
  0.0 4.5 %copy-start.1 = (f32[2,2,4,1024]{3,2,1,0:T(4,128)S(1)}, f32[2,2,4,1024]{3,2,1,0:T(4,128)}, u32[]{:S(2)}) copy-start(f32[2,2,4,1024]{3,2,1,0:T(4,128)} %param.5) | copy-start | bytes 196612
  0.0 4.5 %copy-start.2 = (s32[8,8,8]{2,1,0:T(8,128)S(1)}, s32[8,8,8]{2,1,0:T(8,128)}, u32[]{:S(2)}) copy-start(s32[8,8,8]{2,1,0:T(8,128)} %agg_ref.1) | copy-start | bytes 6148
  0.0 4.5 %copy-start.3 = (s32[1,1,8]{2,1,0:T(1,128)S(1)}, s32[1,1,8]{2,1,0:T(1,128)}, u32[]{:S(2)}) copy-start(s32[1,1,8]{2,1,0:T(1,128)} %owner_ref.1) | copy-start | bytes 100
  0.0 8.1 %collective-permute-start.3 = (f32[4,32,128]{2,1,0:T(8,128)}, f32[4,32,128]{2,1,0:T(8,128)S(1)}, u32[]{:S(2)}, u32[]{:S(2)}) collective-permute-start(f32[4,32,128]{2,1,0:T(8,128)} %bitcast.14), channel_id=1, source_target_pairs={{0,8},{2,10},{4,12},{6,14},{8,0},{10,2},{12,4},{14,6},{16,24},{18,... | collective-permute-start | bytes 196616 | tf_op jit(solution)/shard_map/ppermute | solution.py:393
  0.5 7.5 %collective-permute-start.2 = (f32[4,32,128]{2,1,0:T(8,128)}, f32[4,32,128]{2,1,0:T(8,128)S(1)}, u32[]{:S(2)}, u32[]{:S(2)}) collective-permute-start(f32[4,32,128]{2,1,0:T(8,128)} %bitcast.15), channel_id=1, source_target_pairs={{0,2},{2,0},{4,6},{6,4},{8,16},{10,18},{12,20},{14,22},{16,8},{18,... | collective-permute-start | bytes 196616 | tf_op jit(solution)/shard_map/ppermute | solution.py:393
  3.2 4.9 %collective-permute-start.1 = (f32[4,32,128]{2,1,0:T(8,128)}, f32[4,32,128]{2,1,0:T(8,128)S(1)}, u32[]{:S(2)}, u32[]{:S(2)}) collective-permute-start(f32[4,32,128]{2,1,0:T(8,128)} %bitcast.16), channel_id=1, source_target_pairs={{0,2},{2,0},{4,6},{6,4},{8,10},{10,8},{12,14},{14,12},{16,18},{18,... | collective-permute-start | bytes 196616 | tf_op jit(solution)/shard_map/ppermute | solution.py:393
  3.3 4.8 %collective-permute-start = (f32[4,32,128]{2,1,0:T(8,128)}, f32[4,32,128]{2,1,0:T(8,128)S(1)}, u32[]{:S(2)}, u32[]{:S(2)}) collective-permute-start(f32[4,32,128]{2,1,0:T(8,128)} %bitcast.17), channel_id=1, source_target_pairs={{0,8},{2,4},{4,2},{6,14},{8,0},{10,12},{12,10},{14,6},{16,24},{18,... | collective-permute-start | bytes 196616 | tf_op jit(solution)/shard_map/ppermute | solution.py:393
  6.5 4.4 %collective-permute-start.4 = (f32[136,128]{1,0:T(8,128)S(1)}, f32[136,128]{1,0:T(8,128)S(1)}, u32[]{:S(2)}, u32[]{:S(2)}) collective-permute-start(f32[136,128]{1,0:T(8,128)S(1)} %get-tuple-element.11.send_ref), channel_id=1, source_target_pairs={{0,1},{1,0},{2,3},{3,2},{4,5},{5,4},{6,7},{7,6},{8,9},{9,8},{10,11... | collective-permute-start | bytes 208904 | tf_op jit(solution)/shard_map/ppermute | solution.py:422
  8.7 4.0 %collective-permute-start.5 = (f32[64,128]{1,0:T(8,128)S(1)}, f32[64,128]{1,0:T(8,128)S(1)}, u32[]{:S(2)}, u32[]{:S(2)}) collective-permute-start(f32[64,128]{1,0:T(8,128)S(1)} %shard_map.48.packs_ref), channel_id=1, source_target_pairs={{0,1},{1,0},{2,3},{3,2},{4,5},{5,4},{6,7},{7,6},{8,9},{9,8},{10,11... | collective-permute-start | bytes 98312 | tf_op jit(solution)/shard_map/ppermute | solution.py:432

commit v9 on v8

--- a/solution.py
+++ b/solution.py
@@ -344,7 +344,7 @@
 
     send_out(own_ref, 0, 1)
     send_out(own_ref, 5, 7)
-    flat = flatten([pack[k * CDOF : (k + 1) * CDOF] for k in range(4) for pack in packs])
+    flat = [f for k in range(4) for f in flatten([pack[k * CDOF : (k + 1) * CDOF] for pack in packs])]
     labels = [ref[2 * count : 2 * count + 8].astype(jnp.int32) for ref in firsts]
     for k in range(4):
         chosen = [choose(label[k : k + 1], gz * size, size) for label in labels]

time: 14 us -> 14 us (level)
  no operation moved by 1% of the time
where the time goes in v9:
time: 14 us; the launch traced here: 13.9 us
  starting transfers between devices  7.25 us (52%)
  Pallas kernels  4.44 us (32%)
  waiting for transfers between devices  2.11 us (15%)
    ppermute x4, starting transfers between devices, shards(): lax.ppermute(base, ('gx', 'gy'), matching(sizes, along, first))  4.5 us
    pallas_call x1, Pallas kernels, shards(): pl.pallas_call(functools.partial(local_kernel, (bx, by, bz), group_size),...  1.93 us
    ppermute x1, starting transfers between devices, shards(): lax.ppermute(first, 'gz', rotation(group_size, shift))  1.59 us
    ppermute x1, starting transfers between devices, shards(): lax.ppermute(packs, 'gz', rotation(group_size, shift))  1.16 us
    ppermute x1, waiting for transfers between devices, shards(): lax.ppermute(packs, 'gz', rotation(group_size, shift))  1.16 us
    pallas_call x1, Pallas kernels, shards(): pl.pallas_call(functools.partial(final_kernel, group_size), out_shape=ful...  1.13 us
    ppermute x1, waiting for transfers between devices, shards(): lax.ppermute(first, 'gz', rotation(group_size, shift))  0.94 us
    pallas_call x1, Pallas kernels, shards(): pl.pallas_call(functools.partial(own_kernel, group_size), out_shape=full,...  0.71 us
  transfers between devices with their start and end apart: 6, of which 2 were waited for; matrix products, arithmetic and copies ran while one was open for 0% of the time, Pallas kernels for 24%

profile of v9, /device:TPU:0, one launch (start us, length us, event | category | flops | bytes accessed | tf_op | source)
XLA Modules:
  0.0 13.9 jit_solution(13748584246837453439)
XLA Ops:
  0.0 0.0 copy-start
  0.0 0.0 copy-start.1
  0.0 0.0 copy-start.2
  0.0 0.0 copy-start.3
  0.0 0.5 %collective-permute-start.3 = (f32[4,32,128]{2,1,0:T(8,128)}, f32[4,32,128]{2,1,0:T(8,128)S(1)}, u32[]{:S(2)}, u32[]{:S(2)}) collective-permute-start(f32[4,32,128]{2,1,0:T(8,128)} %bitcast.14), channel_id=1, source_target_pairs={{0,8},{2,10},{4,12},{6,14},{8,0},{10,2},{12,4},{14,6},{16,24},{18,... | collective-permute-start | bytes 196616 | tf_op jit(solution)/shard_map/ppermute | solution.py:393
  0.5 2.6 %collective-permute-start.2 = (f32[4,32,128]{2,1,0:T(8,128)}, f32[4,32,128]{2,1,0:T(8,128)S(1)}, u32[]{:S(2)}, u32[]{:S(2)}) collective-permute-start(f32[4,32,128]{2,1,0:T(8,128)} %bitcast.15), channel_id=1, source_target_pairs={{0,2},{2,0},{4,6},{6,4},{8,16},{10,18},{12,20},{14,22},{16,8},{18,... | collective-permute-start | bytes 196616 | tf_op jit(solution)/shard_map/ppermute | solution.py:393
  3.2 0.1 collective-permute-start.1
  3.3 1.2 %collective-permute-start = (f32[4,32,128]{2,1,0:T(8,128)}, f32[4,32,128]{2,1,0:T(8,128)S(1)}, u32[]{:S(2)}, u32[]{:S(2)}) collective-permute-start(f32[4,32,128]{2,1,0:T(8,128)} %bitcast.17), channel_id=1, source_target_pairs={{0,8},{2,4},{4,2},{6,14},{8,0},{10,12},{12,10},{14,6},{16,24},{18,... | collective-permute-start | bytes 196616 | tf_op jit(solution)/shard_map/ppermute | solution.py:393
  4.5 0.0 copy-done
  4.5 0.0 copy-done.1
  4.5 0.0 copy-done.2
  4.5 0.0 copy-done.3
  4.5 1.9 %shard_map.47 = (bf16[8,64,256]{2,1,0:T(8,128)(2,1)S(1)}, f32[64,256]{1,0:T(8,128)S(1)}, bf16[1,64,256]{2,1,0:T(8,128)(2,1)S(1)}, f32[136,128]{1,0:T(8,128)S(1)}) custom-call(s32[8,8,8]{2,1,0:T(8,128)S(1)} %copy-done.2, s32[1,1,8]{2,1,0:T(1,128)S(1)} %copy-done.3, f32[4,32,128]{2,1,0:T(8,128)S(1)} %bitcast.18, f32[28,128,128]{2,1,0:T(8,128)S(1)} %bitcast.13, ...), custom_call_target="tpu_custom_call" | custom-call | flops 2000000000 | bytes 4000000 | tf_op jit(solution)/shard_map/pallas_call | solution.py:400
  6.5 1.6 %collective-permute-start.4 = (f32[136,128]{1,0:T(8,128)S(1)}, f32[136,128]{1,0:T(8,128)S(1)}, u32[]{:S(2)}, u32[]{:S(2)}) collective-permute-start(f32[136,128]{1,0:T(8,128)S(1)} %get-tuple-element.11.send_ref), channel_id=1, source_target_pairs={{0,1},{1,0},{2,3},{3,2},{4,5},{5,4},{6,7},{7,6},{8,9},{9,8},{10,11... | collective-permute-start | bytes 208904 | tf_op jit(solution)/shard_map/ppermute | solution.py:422
  8.1 0.0 collective-permute-done.3.even_x
  8.1 0.0 collective-permute-done.2.odd_x
  8.1 0.0 collective-permute-done.1.even_y
  8.1 0.0 collective-permute-done.odd_y
  8.1 0.7 %shard_map.48.packs_ref = f32[64,128]{1,0:T(8,128)S(1)} custom-call(bf16[8,64,256]{2,1,0:T(8,128)(2,1)S(1)} %get-tuple-element.12.outer_ref, f32[4,32,128]{2,1,0:T(8,128)S(1)} %collective-permute-done.odd_y, f32[4,32,128]{2,1,0:T(8,128)S(1)} %collective-permute-done.1.even_y, f32[4,32,128]{2,1,0:T(8,128)S(1)} %collective-permute-done.2.odd_x, ...), custom_call_target="tpu_custom_call" | custom-call | flops 49999998976 | bytes 50000000 | tf_op jit(solution)/shard_map/pallas_call | solution.py:423
  8.7 1.2 %collective-permute-start.5 = (f32[64,128]{1,0:T(8,128)S(1)}, f32[64,128]{1,0:T(8,128)S(1)}, u32[]{:S(2)}, u32[]{:S(2)}) collective-permute-start(f32[64,128]{1,0:T(8,128)S(1)} %shard_map.48.packs_ref), channel_id=1, source_target_pairs={{0,1},{1,0},{2,3},{3,2},{4,5},{5,4},{6,7},{7,6},{8,9},{9,8},{10,11... | collective-permute-start | bytes 98312 | tf_op jit(solution)/shard_map/ppermute | solution.py:432
  9.9 0.9 %collective-permute-done.4.refs_0_.refs_1_ = f32[136,128]{1,0:T(8,128)S(1)} collective-permute-done((f32[136,128]{1,0:T(8,128)S(1)}, f32[136,128]{1,0:T(8,128)S(1)}, u32[]{:S(2)}, u32[]{:S(2)}) %collective-permute-start.4) | collective-permute-done | bytes 69664 | tf_op jit(solution)/shard_map/ppermute | solution.py:422
  10.9 0.7 %shard_map.49.own_ref = f32[8,14336]{1,0:T(8,128)S(1)} custom-call(f32[64,256]{1,0:T(8,128)S(1)} %get-tuple-element.9.inner_ref, bf16[1,64,256]{2,1,0:T(8,128)(2,1)S(1)} %get-tuple-element.10.layer_ref, f32[136,128]{1,0:T(8,128)S(1)} %get-tuple-element.11.send_ref, f32[64,128]{1,0:T(8,128)S(1)} %shard_map.48.packs_ref, ...), custom_call_target="tpu_custom_call" | custom-call | flops 1000000000 | bytes 2000000 | tf_op jit(solution)/shard_map/pallas_call | solution.py:434
  11.6 1.2 %collective-permute-done.5.refs_0_ = f32[64,128]{1,0:T(8,128)S(1)} collective-permute-done((f32[64,128]{1,0:T(8,128)S(1)}, f32[64,128]{1,0:T(8,128)S(1)}, u32[]{:S(2)}, u32[]{:S(2)}) %collective-permute-start.5) | collective-permute-done | bytes 32800 | tf_op jit(solution)/shard_map/ppermute | solution.py:432
  12.7 1.1 %shard_map.50 = f32[8,14336]{1,0:T(8,128)} custom-call(f32[8,14336]{1,0:T(8,128)S(1)} %shard_map.49.own_ref, f32[64,128]{1,0:T(8,128)S(1)} %collective-permute-done.5.refs_0_, f32[136,128]{1,0:T(8,128)S(1)} %collective-permute-done.4.refs_0_.refs_1_), custom_call_target="tpu_custom_call" | custom-call | tf_op jit(solution)/shard_map/pallas_call | solution.py:442
  (1 shorter events, 0.0 us)
Async XLA Ops:
  0.0 4.5 %copy-start = (f32[2,2,4,7,4096]{4,2,3,1,0:T(4,128)S(1)}, f32[2,2,4,7,4096]{4,2,3,1,0:T(4,128)}, u32[]{:S(2)}) copy-start(f32[2,2,4,7,4096]{4,2,3,1,0:T(4,128)} %param.4) | copy-start | bytes 5505028
  0.0 4.5 %copy-start.1 = (f32[2,2,4,1024]{3,2,1,0:T(4,128)S(1)}, f32[2,2,4,1024]{3,2,1,0:T(4,128)}, u32[]{:S(2)}) copy-start(f32[2,2,4,1024]{3,2,1,0:T(4,128)} %param.5) | copy-start | bytes 196612
  0.0 4.5 %copy-start.2 = (s32[8,8,8]{2,1,0:T(8,128)S(1)}, s32[8,8,8]{2,1,0:T(8,128)}, u32[]{:S(2)}) copy-start(s32[8,8,8]{2,1,0:T(8,128)} %agg_ref.1) | copy-start | bytes 6148
  0.0 4.5 %copy-start.3 = (s32[1,1,8]{2,1,0:T(1,128)S(1)}, s32[1,1,8]{2,1,0:T(1,128)}, u32[]{:S(2)}) copy-start(s32[1,1,8]{2,1,0:T(1,128)} %owner_ref.1) | copy-start | bytes 100
  0.0 8.1 %collective-permute-start.3 = (f32[4,32,128]{2,1,0:T(8,128)}, f32[4,32,128]{2,1,0:T(8,128)S(1)}, u32[]{:S(2)}, u32[]{:S(2)}) collective-permute-start(f32[4,32,128]{2,1,0:T(8,128)} %bitcast.14), channel_id=1, source_target_pairs={{0,8},{2,10},{4,12},{6,14},{8,0},{10,2},{12,4},{14,6},{16,24},{18,... | collective-permute-start | bytes 196616 | tf_op jit(solution)/shard_map/ppermute | solution.py:393
  0.5 7.5 %collective-permute-start.2 = (f32[4,32,128]{2,1,0:T(8,128)}, f32[4,32,128]{2,1,0:T(8,128)S(1)}, u32[]{:S(2)}, u32[]{:S(2)}) collective-permute-start(f32[4,32,128]{2,1,0:T(8,128)} %bitcast.15), channel_id=1, source_target_pairs={{0,2},{2,0},{4,6},{6,4},{8,16},{10,18},{12,20},{14,22},{16,8},{18,... | collective-permute-start | bytes 196616 | tf_op jit(solution)/shard_map/ppermute | solution.py:393
  3.2 4.9 %collective-permute-start.1 = (f32[4,32,128]{2,1,0:T(8,128)}, f32[4,32,128]{2,1,0:T(8,128)S(1)}, u32[]{:S(2)}, u32[]{:S(2)}) collective-permute-start(f32[4,32,128]{2,1,0:T(8,128)} %bitcast.16), channel_id=1, source_target_pairs={{0,2},{2,0},{4,6},{6,4},{8,10},{10,8},{12,14},{14,12},{16,18},{18,... | collective-permute-start | bytes 196616 | tf_op jit(solution)/shard_map/ppermute | solution.py:393
  3.3 4.8 %collective-permute-start = (f32[4,32,128]{2,1,0:T(8,128)}, f32[4,32,128]{2,1,0:T(8,128)S(1)}, u32[]{:S(2)}, u32[]{:S(2)}) collective-permute-start(f32[4,32,128]{2,1,0:T(8,128)} %bitcast.17), channel_id=1, source_target_pairs={{0,8},{2,4},{4,2},{6,14},{8,0},{10,12},{12,10},{14,6},{16,24},{18,... | collective-permute-start | bytes 196616 | tf_op jit(solution)/shard_map/ppermute | solution.py:393
  6.5 4.4 %collective-permute-start.4 = (f32[136,128]{1,0:T(8,128)S(1)}, f32[136,128]{1,0:T(8,128)S(1)}, u32[]{:S(2)}, u32[]{:S(2)}) collective-permute-start(f32[136,128]{1,0:T(8,128)S(1)} %get-tuple-element.11.send_ref), channel_id=1, source_target_pairs={{0,1},{1,0},{2,3},{3,2},{4,5},{5,4},{6,7},{7,6},{8,9},{9,8},{10,11... | collective-permute-start | bytes 208904 | tf_op jit(solution)/shard_map/ppermute | solution.py:422
  8.7 4.0 %collective-permute-start.5 = (f32[64,128]{1,0:T(8,128)S(1)}, f32[64,128]{1,0:T(8,128)S(1)}, u32[]{:S(2)}, u32[]{:S(2)}) collective-permute-start(f32[64,128]{1,0:T(8,128)S(1)} %shard_map.48.packs_ref), channel_id=1, source_target_pairs={{0,1},{1,0},{2,3},{3,2},{4,5},{5,4},{6,7},{7,6},{8,9},{9,8},{10,11... | collective-permute-start | bytes 98312 | tf_op jit(solution)/shard_map/ppermute | solution.py:432
